TPU v7x, 32 devices: a whole 2x2x4 slice. The times are simulated.
32 devices in a mesh: dp: 8 (over z, x), chan: 4 (over y, core).
Axes of the slice: x: 2, y: 2, z: 4, core: 2. Of those that a mesh axis runs over, the one named last changes fastest.
Arguments:
- tokens: bfloat16 [224, 196, 768], P('dp', None, 'chan'), may hold values from -6 to 6
- ln1_gain: float32 [768], P('chan'), may hold values from 0.5 to 1.5
- ln1_bias: float32 [768], P('chan'), may hold values from -1.5 to 1.5
- mix_in: bfloat16 [196, 384], replicated, may hold values from -0.4375 to 0.4375
- mix_in_bias: float32 [384], replicated, may hold values from -2.5 to 2.5
- mix_out: bfloat16 [384, 196], replicated, may hold values from -0.3125 to 0.3125
- mix_out_bias: float32 [196], replicated, may hold values from -1.5 to 1.5
- ln2_gain: float32 [768], replicated, may hold values from 0.5 to 1.5
- ln2_bias: float32 [768], replicated, may hold values from -1.5 to 1.5
- chan_in: bfloat16 [768, 3072], replicated, may hold values from -0.21875 to 0.21875
- chan_in_bias: float32 [3072], replicated, may hold values from -2.5 to 2.5
- chan_out: bfloat16 [3072, 768], replicated, may hold values from -0.109375 to 0.109375
- chan_out_bias: float32 [768], replicated, may hold values from -1.5 to 1.5
- skip_masks: int32 [224, 2], P('dp'), may hold values 0 or 1
- cotangent: bfloat16 [224, 196, 768], P('dp', 'chan'), may hold values from -6 to 6
Outputs:
- output: bfloat16 [224, 196, 768], P('dp', 'chan')
- input_grad: float32 [224, 196, 768], P('dp', None, 'chan')
- grad_ln1_gain: float32 [768], replicated
- grad_ln1_bias: float32 [768], replicated
- grad_mix_in: float32 [196, 384], replicated
- grad_mix_in_bias: float32 [384], replicated
- grad_mix_out: float32 [384, 196], replicated
- grad_mix_out_bias: float32 [196], replicated
- grad_ln2_gain: float32 [768], replicated
- grad_ln2_bias: float32 [768], replicated
- grad_chan_in: float32 [768, 3072], P(None, ('dp', 'chan'))
- grad_chan_in_bias: float32 [3072], replicated
- grad_chan_out: float32 [3072, 768], P(('dp', 'chan'))
- grad_chan_out_bias: float32 [768], replicated
All inputs are finite; a program needn't handle non-finite values. No bound on the sum of `skip_masks` on one device may be relied on, other than what follows from the above.
Results may differ from a plain program's by a relative error of at most 0.007.
Values may be sent and summed in bfloat16 or wider, within the bound.
No kernel may reach another device: no remote copies, remote signals or barrier semaphores. Data moves between devices by JAX's collectives and lax.ppermute only.
A program may use at most 192 MiB of HBM per device.

v0:
```python
import jax
import jax.numpy as jnp
from jax import lax
from jax.sharding import PartitionSpec as P

epsilon = 1e-06


def gelu_exact(values):
    return jax.nn.gelu(values, approximate=False)


def gelu_back(pre_value, incoming):
    unused, pullback = jax.vjp(gelu_exact, pre_value)
    return pullback(incoming)[0]


def shards(
    tokens,
    ln1_gain,
    ln1_bias,
    mix_in,
    mix_in_bias,
    mix_out,
    mix_out_bias,
    ln2_gain,
    ln2_bias,
    chan_in,
    chan_in_bias,
    chan_out,
    chan_out_bias,
    skip_masks,
    cotangent,
):
    images, patches, local_width = tokens.shape
    full_width = local_width * lax.axis_size("chan")
    tokens_wide = tokens.astype(jnp.float32)
    row_sum, row_squares = lax.psum(
        (jnp.sum(tokens_wide, -1), jnp.sum(tokens_wide * tokens_wide, -1)), "chan"
    )
    center = row_sum / full_width
    spread = row_squares / full_width - center * center
    scale_one = lax.rsqrt(spread + epsilon)[..., None]
    normed = (tokens_wide - center[..., None]) * scale_one
    mixed_in = (normed * ln1_gain + ln1_bias).astype(jnp.bfloat16)
    token_pre = (
        jnp.einsum("bsd,sk->bdk", mixed_in, mix_in, preferred_element_type=jnp.float32)
        + mix_in_bias
    )
    token_act = gelu_exact(token_pre).astype(jnp.bfloat16)
    token_out = (
        jnp.einsum("bdk,ks->bsd", token_act, mix_out, preferred_element_type=jnp.float32)
        + mix_out_bias[None, :, None]
    )
    keep_token = skip_masks[:, 0].astype(jnp.float32)[:, None, None]
    keep_chan = skip_masks[:, 1].astype(jnp.float32)[:, None, None]
    residual = tokens_wide + keep_token * token_out
    patch_rows = lax.all_to_all(
        residual.astype(jnp.bfloat16), "chan", split_axis=1, concat_axis=2, tiled=True
    )
    stream_wide = patch_rows.astype(jnp.float32)
    center_two = jnp.mean(stream_wide, -1, keepdims=True)
    offsets = stream_wide - center_two
    scale_two = lax.rsqrt(jnp.mean(offsets * offsets, -1, keepdims=True) + epsilon)
    normed_two = offsets * scale_two
    chan_inp = (normed_two * ln2_gain + ln2_bias).astype(jnp.bfloat16)
    flat_in = chan_inp.reshape(-1, full_width)
    chan_pre = jnp.dot(flat_in, chan_in, preferred_element_type=jnp.float32) + chan_in_bias
    chan_act = gelu_exact(chan_pre).astype(jnp.bfloat16)
    chan_res = jnp.dot(chan_act, chan_out, preferred_element_type=jnp.float32) + chan_out_bias
    output = (stream_wide + keep_chan * chan_res.reshape(stream_wide.shape)).astype(jnp.bfloat16)
    upstream = cotangent.astype(jnp.float32)
    out_grad = (keep_chan * upstream).astype(jnp.bfloat16).reshape(-1, full_width)
    grad_w4 = jnp.einsum("rf,rd->fd", chan_act, out_grad, preferred_element_type=jnp.float32)
    grad_b4 = jnp.sum(out_grad.astype(jnp.float32), 0)
    act_grad = jnp.einsum("rd,fd->rf", out_grad, chan_out, preferred_element_type=jnp.float32)
    pre_grad = gelu_back(chan_pre, act_grad).astype(jnp.bfloat16)
    grad_b3 = jnp.sum(pre_grad.astype(jnp.float32), 0)
    grad_w3 = jnp.einsum("rd,rf->df", flat_in, pre_grad, preferred_element_type=jnp.float32)
    in_grad = jnp.einsum(
        "rf,df->rd", pre_grad, chan_in, preferred_element_type=jnp.float32
    ).reshape(stream_wide.shape)
    grad_g2 = jnp.sum(in_grad * normed_two, (0, 1))
    grad_c2 = jnp.sum(in_grad, (0, 1))
    scaled_two = in_grad * ln2_gain
    stream_back = scale_two * (
        scaled_two
        - jnp.mean(scaled_two, -1, keepdims=True)
        - normed_two * jnp.mean(scaled_two * normed_two, -1, keepdims=True)
    )
    stream_grad = (upstream + stream_back).astype(jnp.bfloat16)
    chan_grad = lax.all_to_all(stream_grad, "chan", split_axis=2, concat_axis=1, tiled=True)
    chan_grad_wide = chan_grad.astype(jnp.float32)
    tok_grad = (keep_token * chan_grad_wide).astype(jnp.bfloat16)
    grad_b2 = jnp.sum(tok_grad.astype(jnp.float32), (0, 2))
    grad_w2 = jnp.einsum("bdk,bsd->ks", token_act, tok_grad, preferred_element_type=jnp.float32)
    act1_grad = jnp.einsum("bsd,ks->bdk", tok_grad, mix_out, preferred_element_type=jnp.float32)
    pre1_grad = gelu_back(token_pre, act1_grad).astype(jnp.bfloat16)
    grad_b1 = jnp.sum(pre1_grad.astype(jnp.float32), (0, 1))
    grad_w1 = jnp.einsum("bsd,bdk->sk", mixed_in, pre1_grad, preferred_element_type=jnp.float32)
    norm_grad = jnp.einsum("bdk,sk->bsd", pre1_grad, mix_in, preferred_element_type=jnp.float32)
    local_g1 = jnp.sum(norm_grad * normed, (0, 1))
    local_c1 = jnp.sum(norm_grad, (0, 1))
    scaled_one = norm_grad * ln1_gain
    part_one, part_two = (
        lax.psum(jnp.sum(scaled_one, -1).astype(jnp.bfloat16), "chan").astype(jnp.float32),
        lax.psum(jnp.sum(scaled_one * normed, -1).astype(jnp.bfloat16), "chan").astype(jnp.float32),
    )
    input_grad = chan_grad_wide + scale_one * (
        scaled_one - part_one[..., None] / full_width - normed * (part_two[..., None] / full_width)
    )
    offset_start = lax.axis_index("chan") * local_width
    full_g1 = lax.dynamic_update_slice(
        jnp.zeros((full_width,), jnp.float32), local_g1, (offset_start,)
    )
    full_c1 = lax.dynamic_update_slice(
        jnp.zeros((full_width,), jnp.float32), local_c1, (offset_start,)
    )
    sum_g1, sum_c1, sum_w1, sum_b1, sum_w2, sum_b2, sum_g2, sum_c2, sum_b3, sum_b4 = lax.psum(
        (full_g1, full_c1, grad_w1, grad_b1, grad_w2, grad_b2, grad_g2, grad_c2, grad_b3, grad_b4),
        ("dp", "chan"),
    )
    share_w3, share_w4 = (
        lax.psum_scatter(grad_w3, ("dp", "chan"), scatter_dimension=1, tiled=True),
        lax.psum_scatter(grad_w4, ("dp", "chan"), scatter_dimension=0, tiled=True),
    )
    return (
        output,
        input_grad,
        sum_g1,
        sum_c1,
        sum_w1,
        sum_b1,
        sum_w2,
        sum_b2,
        sum_g2,
        sum_c2,
        share_w3,
        sum_b3,
        share_w4,
        sum_b4,
    )


def solution(mesh):
    return jax.shard_map(
        shards,
        mesh=mesh,
        in_specs=(
            P("dp", None, "chan"),
            P("chan"),
            P("chan"),
            P(),
            P(),
            P(),
            P(),
            P(),
            P(),
            P(),
            P(),
            P(),
            P(),
            P("dp", None),
            P("dp", "chan", None),
        ),
        out_specs=(
            P("dp", "chan", None),
            P("dp", None, "chan"),
            P(),
            P(),
            P(),
            P(),
            P(),
            P(),
            P(),
            P(),
            P(None, ("dp", "chan")),
            P(),
            P(("dp", "chan"), None),
            P(),
        ),
        check_vma=False,
    )
```

profile of v0, /device:TPU:17, one launch (start us, length us, event | category | flops | bytes accessed | tf_op | source)
XLA Modules:
  0.0 790.2 jit_solution(16158760556708120150)
XLA Ops:
  7.2 0.8 convert_bitcast_fusion
  8.0 2.8 convert_reduce_fusion.1
  10.8 11.0 %all-reduce.2 = (f32[28,196]{1,0:T(8,128)S(1)}, f32[28,196]{1,0:T(8,128)S(1)}) all-reduce(f32[28,196]{1,0:T(8,128)S(1)} %get-tuple-element.24, f32[28,196]{1,0:T(8,128)S(1)} %get-tuple-element.23), channel_id=1, replica_groups=mesh['dp'=8,'chan'=4] {'chan'}, use_global_device_ids=true, to_apply=%region_3.0 | all-reduce | flops 10976 | bytes 87808 | tf_op jit(solution)/shard_map/psum | solution.py:38
  21.8 5.6 convert_reduce_fusion.3
  27.5 19.6 %multiply_convert_fusion.1 = (bf16[28,192,384]{2,1,0:T(8,128)(2,1)S(1)}, f32[28,192,384]{2,1,0:T(8,128)}) fusion(f32[28,192,384]{2,1,0:T(8,128)S(1)} %get-tuple-element.51, f32[384]{0:T(512)S(1)} %copy-done.22, u32[192,384]{1,0:T(8,128)S(1)} %get-tuple-element.19, u32[192,384]{1,0:T(8,128)S(1)} %get-tuple-element.18), kind=kLoop, calls=%fused_computation.31 | loop fusion | flops 142442496 | bytes 21235200 | tf_op jit(solution)/shard_map/convert_element_type | solution.py:50
  47.1 1.9 copy-done.2
  49.1 1.6 fusion.25
  50.7 5.7 copy.56
  56.4 5.4 all-to-all-start
  61.8 0.2 all-reduce.6.cloned.1.call-start
  62.0 4.5 convert_reduce_fusion.6
  66.5 4.0 reshape.138
  70.5 28.1 %all-to-all-done = bf16[28,196,192]{2,0,1:T(8,128)(2,1)S(1)} async-done(((bf16[28,196,192]{2,0,1:T(8,128)(2,1)}), bf16[28,196,192]{2,0,1:T(8,128)(2,1)S(1)}, u32[]{:S(2)}, u32[]{:S(2)}) %all-to-all-start) | async-done | bytes 2107424 | tf_op jit(solution)/shard_map/all_to_all | solution.py:58
  98.6 5.3 copy.57
  103.9 5.2 copy.58
  109.1 6.9 reshape.145
  116.0 7.5 copy.59
  123.5 7.7 reshape.140
  131.1 7.2 reshape.141
  138.3 3.3 bitcast_reduce_fusion
  141.6 3.7 multiply_reduce_fusion
  145.4 0.1 div.33
  145.5 0.6 copy-done.10
  146.1 0.1 rsqrt.17
  146.2 48.6 %multiply_convert_fusion = (bf16[1372,3072]{1,0:T(8,128)(2,1)}, f32[1372,3072]{1,0:T(8,128)}, f32[1372,3072]{1,0:T(8,128)}) fusion(f32[3072]{0:T(1024)S(1)} %copy-done.27, bf16[768,3072]{1,0:T(8,128)(2,1)} %param.24, f32[1372,768]{1,0:T(8,128)} %reshape.141, f32[768]{0:T(1024)S(1)} %copy-done.29, f32[768]{0:T(1024)S(1)} %copy-done.21, f32[1372]{0:T(1024)S(1)} %rsqrt.17, ...), kind=kOutput, calls=%fused_computation.4 | convolution fusion | flops 6757352448 | bytes 51110624 | tf_op jit(solution)/shard_map/dot_general | solution.py:68
  194.8 21.5 %convert_reduce_fusion = (f32[3072]{0:T(1024)S(1)}, bf16[1372,3072]{1,0:T(8,128)(2,1)}) fusion(f32[1372,3072]{1,0:T(8,128)} %get-tuple-element.42, bf16[1372,768]{1,0:T(8,128)(2,1)S(1)} %copy-done.7, bf16[3072,768]{1,0:T(8,128)(2,1)} %param.26, f32[1372,3072]{1,0:T(8,128)} %get-tuple-element.52, f32[3072]{0:T(1024)S(1)} %copy-done.27), kind=kOutput, calls=%fused_computation.2 | convolution fusion | flops 6545556480 | bytes 48998400 | tf_op jit(solution)/shard_map/rd,fd->rf/dot_general | solution.py:76
  216.3 15.8 %multiply_reduce_fusion.1 = (f32[768]{0:T(1024)S(1)}, f32[1372]{0:T(1024)S(1)}, f32[1372]{0:T(1024)S(1)}, f32[768]{0:T(1024)S(1)}, f32[1372,768]{1,0:T(8,128)}) fusion(f32[1372,768]{1,0:T(8,128)} %reshape.141, f32[1372]{0:T(1024)S(1)} %rsqrt.17, f32[1372]{0:T(1024)S(1)} %div.33, f32[768]{0:T(1024)S(1)} %copy-done.21, ...), kind=kOutput, calls=%fused_computation.70 | convolution fusion | flops 6483386368 | bytes 21608896 | tf_op jit(solution)/shard_map/rf,df->rd/dot_general | solution.py:80
  232.1 5.2 reshape.139
  237.3 0.1 div.38
  237.4 0.1 div.36
  237.5 12.1 %convolution_add_fusion = f32[1372,768]{1,0:T(8,128)} fusion(bf16[1372,3072]{1,0:T(8,128)(2,1)} %get-tuple-element.41, bf16[3072,768]{1,0:T(8,128)(2,1)} %param.26, f32[768]{0:T(1024)S(1)} %copy-done.28), kind=kOutput, calls=%fused_computation.75 | convolution fusion | flops 6474961920 | bytes 17366016 | tf_op jit(solution)/shard_map/dot_general | solution.py:70
  249.7 5.4 reshape.137
  255.1 7.8 fusion.28
  262.8 11.4 %copy.61 = bf16[28,49,768]{1,0,2:T(8,128)(2,1)} copy(bf16[28,49,768]{2,1,0:T(8,128)(2,1)} %get-tuple-element.45) | data formatting | bytes 4214784 | tf_op jit(solution)/shard_map/convert_element_type | solution.py:91
  274.3 10.7 %reshape.152 = bf16[4,2,131712]{2,1,0:T(2,128)(2,1)S(1)} reshape(bf16[768,28,49]{2,1,0:T(8,128)(2,1)} %bitcast.62) | data formatting | bytes 4214784
  285.0 29.7 %all_to_all.8 = bf16[4,2,131712]{2,1,0:T(2,128)(2,1)} all-to-all(bf16[4,2,131712]{2,1,0:T(2,128)(2,1)S(1)} %reshape.152), channel_id=1, replica_groups=mesh['dp'=8,'chan'=4] {'chan'}, dimensions={0} | all-to-all | bytes 4214784 | tf_op jit(solution)/shard_map/all_to_all | solution.py:92
  314.7 11.9 %reshape.153 = bf16[768,28,49]{2,1,0:T(8,128)(2,1)} reshape(bf16[4,2,131712]{2,1,0:T(2,128)(2,1)} %all_to_all.8) | data formatting | bytes 4214784
  326.6 10.1 %copy.62 = f32[28,49,4,192]{3,1,2,0:T(8,128)} copy(bf16[28,49,4,192]{1,0,3,2:T(8,128)(2,1)} %bitcast.59) | data formatting | bytes 6322176 | tf_op jit(solution)/shard_map/convert_element_type | solution.py:93
  336.8 7.0 reshape.142
  343.8 6.4 copy.64
  350.2 6.9 convolution_bitcast_fusion
  357.2 8.2 %convert_reduce_fusion.4 = (f32[384]{0:T(512)S(1)}, bf16[28,192,384]{2,1,0:T(8,128)(2,1)S(1)}) fusion(f32[28,192,384]{2,1,0:T(8,128)} %get-tuple-element.44, bf16[384,196]{0,1:T(8,128)(2,1)S(1)} %copy-done.26, f32[28,196,192]{1,2,0:T(8,128)S(1)} %copy-done.1, f32[28]{0:T(128)S(1)} %copy-done.18, f32[28,192,384]{2,1,0:T(8,128)} %copy-done.6, ...), kind=kOutput, calls=%fused_computation.29 | convolution fusion | flops 846440064 | bytes 25012336 | tf_op jit(solution)/shard_map/bsd,ks->bdk/dot_general | solution.py:97
  365.4 2.0 copy-done.32
  367.5 2.7 convolution_bitcast_fusion.1
  370.2 0.0 reduce-scatter.3.cloned.1.call-start
  370.2 14.2 %fusion.37 = f32[768,3072]{0,1:T(8,128)} fusion(bf16[1372,3072]{1,0:T(8,128)(2,1)} %get-tuple-element.58, f32[1372,768]{1,0:T(8,128)} %reshape.141, f32[768]{0:T(1024)S(1)} %copy-done.29, f32[768]{0:T(1024)S(1)} %copy-done.21, f32[1372]{0:T(1024)S(1)} %rsqrt.17, f32[1372]{0:T(1024)S(1)} %div.33), kind=kOutput, calls=%fused_computation.95 | convolution fusion | flops 6479176704 | bytes 22098656 | tf_op jit(solution)/shard_map/rd,rf->df/dot_general | solution.py:79
  384.4 0.0 reduce-scatter.5.cloned.1.call-start
  384.5 13.1 %fusion.42 = f32[3072,768]{1,0:T(8,128)} fusion(bf16[1372,3072]{1,0:T(8,128)(2,1)} %get-tuple-element.41, bf16[1372,768]{1,0:T(8,128)(2,1)} %reshape.138), kind=kOutput, calls=%fused_computation.97 | convolution fusion | flops 6473908224 | bytes 19974144 | tf_op jit(solution)/shard_map/rf,rd->fd/dot_general | solution.py:74
  397.6 10.5 %copy.65 = f32[28,49,4,192]{3,2,1,0:T(4,128)} copy(bf16[28,49,4,192]{1,0,3,2:T(8,128)(2,1)} %bitcast.60) | data formatting | bytes 6322176 | tf_op jit(solution)/shard_map/convert_element_type | solution.py:93
  408.1 4.1 convert_reduce_fusion.5
  412.2 0.1 copy.66
  412.3 0.1 reduce_sum.158
  412.4 7.0 fusion.23
  419.4 3.0 reduce_sum.155
  422.4 0.3 dynamic_update_slice.6
  422.6 0.2 dynamic_update_slice.7
  422.8 40.0 %all-reduce = (f32[768]{0:T(1024)}, f32[768]{0:T(1024)}, f32[384]{0:T(512)}, f32[196]{0:T(256)}, f32[768]{0:T(1024)}, /*index=5*/f32[768]{0:T(1024)}, f32[3072]{0:T(1024)}, f32[768]{0:T(1024)}) all-reduce(f32[768]{0:T(1024)S(1)} %dynamic_update_slice.6, ...), channel_id=1, replica_groups=mesh['dp'=8,'chan'=4] {'dp','chan'}, use_global_device_ids=true, to_apply=%region_13.0 | all-reduce | flops 7492 | bytes 59936 | tf_op jit(solution)/shard_map/psum | solution.py:119
  462.8 11.8 %all-reduce.3 = (bf16[28,196]{1,0:T(8,128)(2,1)S(1)}, bf16[28,196]{1,0:T(8,128)(2,1)S(1)}) all-reduce(bf16[28,196]{1,0:T(8,128)(2,1)S(1)} %get-tuple-element.17, bf16[28,196]{1,0:T(8,128)(2,1)S(1)} %get-tuple-element.20), channel_id=1, replica_groups=mesh['dp'=8,'chan'=4] {'chan'}, use_global_device_ids=true, to_apply=%region_11.0 | all-reduce | flops 10976 | bytes 43904 | tf_op jit(solution)/shard_map/psum | solution.py:107
  474.7 9.3 %fusion.22 = f32[28,196,192]{1,2,0:T(8,128)} fusion(f32[28,196,192]{1,2,0:T(8,128)} %copy.64, bf16[28,196,192]{1,2,0:T(8,128)(2,1)S(1)} %copy-done.4, f32[28,192,196]{2,1,0:T(8,128)} %get-tuple-element.54, f32[28,196]{1,0:T(8,128)S(1)} %convert_multiply_fusion.2, f32[28,196]{1,0:T(8,128)S(1)} %convert_multiply_fusion.3, f32[192]{0:T(256)S(1)} %copy-done.24, ...), kind=kLoop, calls=%fused_computation.59 | loop fusion | flops 9483264 | bytes 14840320 | tf_op jit(solution)/shard_map/add | solution.py:109
  484.0 13.1 %all-reduce.6.cloned.1.call-done = (f32[196,384]{1,0:T(8,128)}, f32[384,196]{0,1:T(8,128)}) async-done(((f32[196,384]{1,0:T(8,128)}, f32[384,196]{0,1:T(8,128)}), (f32[196,384]{1,0:T(8,128)}, f32[384,196]{0,1:T(8,128)})) %all-reduce.6.cloned.1.call-update) | async-done | bytes 602128 | tf_op jit(solution)/shard_map/psum | solution.py:119
  497.1 141.6 %reduce-scatter.3.cloned.1.call-done = f32[768,96]{0,1:T(8,128)} async-done(((f32[768,3072]{0,1:T(8,128)}), f32[768,96]{0,1:T(8,128)}) %reduce-scatter.3.cloned.1.call-update) | async-done | bytes 294928 | tf_op jit(solution)/shard_map/reduce_scatter | solution.py:124
  638.7 141.1 %reduce-scatter.5.cloned.1.call-done = f32[96,768]{1,0:T(8,128)} async-done(((f32[3072,768]{1,0:T(8,128)}), f32[96,768]{1,0:T(8,128)}) %reduce-scatter.5.cloned.1.call-update) | async-done | bytes 294928 | tf_op jit(solution)/shard_map/reduce_scatter | solution.py:125
  779.8 1.7 copy.72
  781.5 1.7 copy.73
  (74 shorter events, 0.3 us)
Async XLA Ops:
  7.2 14.6 %copy-start = (bf16[196,384]{1,0:T(8,128)(2,1)S(1)}, bf16[196,384]{1,0:T(8,128)(2,1)}, u32[]{:S(2)}) copy-start(bf16[196,384]{1,0:T(8,128)(2,1)} %param.18) | copy-start | bytes 451588
  8.0 39.2 %copy-start.17 = (f32[28]{0:T(128)}, f32[28]{0:T(128)S(1)}, u32[]{:S(2)}) copy-start(f32[28]{0:T(128)S(1)} %get-tuple-element.50) | copy-start | bytes 340
  8.0 54.1 %copy-start.19 = (f32[28]{0:T(128)}, f32[28]{0:T(128)S(1)}, u32[]{:S(2)}) copy-start(f32[28]{0:T(128)S(1)} %get-tuple-element.49) | copy-start | bytes 340
  21.8 5.7 copy-start.12
  21.8 5.7 copy-start.14
  21.8 5.7 copy-start.22
  27.5 19.6 %copy-start.6 = (f32[28,192,384]{2,1,0:T(8,128)}, f32[28,192,384]{2,1,0:T(8,128)S(1)}, u32[]{:S(2)}) copy-start(f32[28,192,384]{2,1,0:T(8,128)S(1)} %get-tuple-element.51) | copy-start | bytes 24772612
  27.5 21.6 %copy-start.3 = (bf16[28,196,192]{1,2,0:T(8,128)(2,1)S(1)}, bf16[28,196,192]{1,2,0:T(8,128)(2,1)}, u32[]{:S(2)}) copy-start(bf16[28,196,192]{1,2,0:T(8,128)(2,1)} %param.15) | copy-start | bytes 6322180
  27.5 21.5 %copy-start.25 = (bf16[384,196]{0,1:T(8,128)(2,1)S(1)}, bf16[384,196]{0,1:T(8,128)(2,1)}, u32[]{:S(2)}) copy-start(bf16[384,196]{0,1:T(8,128)(2,1)} %param.20) | copy-start | bytes 451588
  27.5 21.5 %copy-start.30 = (f32[196]{0:T(256)S(1)}, f32[196]{0:T(256)}, u32[]{:S(2)}) copy-start(f32[196]{0:T(256)} %param.21) | copy-start | bytes 2356
  47.1 1.9 copy-start.2
  56.4 42.2 %all-to-all-start = ((bf16[28,196,192]{2,0,1:T(8,128)(2,1)}), bf16[28,196,192]{2,0,1:T(8,128)(2,1)S(1)}, u32[]{:S(2)}, u32[]{:S(2)}) async-start(bf16[28,196,192]{2,0,1:T(8,128)(2,1)} %copy.56), calls=%async_computation | async-start | bytes 6422528 | tf_op jit(solution)/shard_map/all_to_all | solution.py:58
  61.8 435.2 %all-reduce.6.cloned.1.call-start = ((), (), s32[]{:S(2)}) async-start(), calls=%async_computation.6 | async-start | bytes 1228800 | tf_op jit(solution)/shard_map/psum | solution.py:119
  138.3 7.9 copy-start.21
  138.3 7.9 copy-start.27
  138.3 7.9 copy-start.29
  141.6 3.9 copy-start.8
  145.5 0.6 copy-start.10
  146.2 48.6 %copy-start.7 = (bf16[1372,768]{1,0:T(8,128)(2,1)S(1)}, bf16[1372,768]{1,0:T(8,128)(2,1)}, u32[]{:S(2)}) copy-start(bf16[1372,768]{1,0:T(8,128)(2,1)} %reshape.138) | copy-start | bytes 6322180
  232.1 5.4 copy-start.28
  249.6 5.4 copy-start.5
  249.7 5.4 copy-start.9
  249.7 5.4 copy-start.11
  249.7 5.4 copy-start.20
  343.8 6.4 copy-start.18
  343.8 13.4 %copy-start.23 = (f32[384]{0:T(512)S(1)}, f32[384]{0:T(512)}, u32[]{:S(2)}) copy-start(f32[384]{0:T(512)} %param.19) | copy-start | bytes 4612
  343.8 13.4 %copy-start.26 = (bf16[384,196]{0,1:T(8,128)(2,1)S(1)}, bf16[384,196]{0,1:T(8,128)(2,1)}, u32[]{:S(2)}) copy-start(bf16[384,196]{0,1:T(8,128)(2,1)} %param.20) | copy-start | bytes 451588
  350.2 6.9 copy-start.1
  357.1 10.3 %copy-start.4 = (bf16[28,196,192]{1,2,0:T(8,128)(2,1)S(1)}, bf16[28,196,192]{1,2,0:T(8,128)(2,1)}, u32[]{:S(2)}) copy-start(bf16[28,196,192]{1,2,0:T(8,128)(2,1)} %param.15) | copy-start | bytes 6322180
  357.1 10.3 %copy-start.13 = (f32[28,196]{1,0:T(8,128)S(1)}, f32[28,196]{1,0:T(8,128)}, u32[]{:S(2)}) copy-start(f32[28,196]{1,0:T(8,128)} %copy-done.12) | copy-start | bytes 65860
  357.1 10.3 %copy-start.15 = (f32[28,196]{1,0:T(8,128)S(1)}, f32[28,196]{1,0:T(8,128)}, u32[]{:S(2)}) copy-start(f32[28,196]{1,0:T(8,128)} %copy-done.14) | copy-start | bytes 65860
  357.2 10.3 %copy-start.24 = (f32[192]{0:T(256)S(1)}, f32[192]{0:T(256)}, u32[]{:S(2)}) copy-start(f32[192]{0:T(256)} %param.16) | copy-start | bytes 2308
  357.2 10.3 %copy-start.31 = (f32[192]{0:T(256)S(1)}, f32[192]{0:T(256)}, u32[]{:S(2)}) copy-start(f32[192]{0:T(256)} %param.17) | copy-start | bytes 2308
  365.4 2.0 copy-start.32
  370.2 268.5 %reduce-scatter.3.cloned.1.call-start = ((), (), s32[]{:S(2)}) async-start(), calls=%async_computation.4 | async-start | bytes 9732096 | tf_op jit(solution)/shard_map/reduce_scatter | solution.py:124
  384.4 395.4 %reduce-scatter.5.cloned.1.call-start = ((), (), s32[]{:S(2)}) async-start(), calls=%async_computation.5 | async-start | bytes 9732096 | tf_op jit(solution)/shard_map/reduce_scatter | solution.py:125
  412.4 10.5 %copy-start.16 = (f32[768]{0:T(1024)S(1)}, f32[768]{0:T(1024)}, u32[]{:S(2)}) copy-start(f32[768]{0:T(1024)} %get-tuple-element.39) | copy-start | bytes 9220
Sparse Core Ops, SparseCore 0:
  370.3 126.7 all-reduce.5
  504.5 134.1 reduce-scatter.2
  645.2 134.5 reduce-scatter.4
where the time goes:
time: 802 us; the launch traced here: 790 us
  waiting for transfers between devices  324 us (40%)
  matrix products  157 us (20%)
  local copies, waits for them, and re-layouts  137 us (17%)
  blocking collectives  92.5 us (12%)
  other arithmetic  58.8 us (7%)
  between operations  14.7 us (2%)
    reduce_scatter x1, waiting for transfers between devices, shards(): lax.psum_scatter(grad_w3, ('dp', 'chan'), scatter_dimension=1, tiled=True)  142 us
    reduce_scatter x1, waiting for transfers between devices, shards(): lax.psum_scatter(grad_w4, ('dp', 'chan'), scatter_dimension=0, tiled=True)  141 us
    dot_general x1, matrix products, shards(): jnp.dot(flat_in, chan_in, preferred_element_type=jnp.float32) + chan_in_bias  48.6 us
    psum x1, blocking collectives, shards(): lax.psum((full_g1, full_c1, grad_w1, grad_b1, grad_w2, grad_b2, grad_g2,...  40 us
    convert_element_type x5, local copies, waits for them, and re-layouts, shards(): stream_wide = patch_rows.astype(jnp.float32)  34.4 us
    convert_element_type x4, local copies, waits for them, and re-layouts, shards(): chan_grad_wide = chan_grad.astype(jnp.float32)  34 us
    unnamed x70, local copies, waits for them, and re-layouts  30.8 us
    all_to_all x1, blocking collectives, shards(): lax.all_to_all(stream_grad, 'chan', split_axis=2, concat_axis=1, tiled=True)  29.7 us
  transfers between devices with their start and end apart: 4, of which 4 were waited for; matrix products, arithmetic and copies ran while one was open for 9% of the time, Pallas kernels for 0%

commit v1 on v0

v1 whole, which is shorter than its diff:
```python
import functools

import jax
import jax.numpy as jnp
from jax import lax
from jax.experimental import pallas as pl
from jax.experimental.pallas import tpu as pltpu
from jax.sharding import PartitionSpec as P

F32, BF16 = jnp.float32, jnp.bfloat16
EPS = 1e-6
RSQRT2 = 0.7071067811865476
RSQRT2PI = 0.3989422804014327
MIB = 2**20
ANY = pl.BlockSpec(memory_space=pl.ANY)
SMEM = pl.BlockSpec(memory_space=pltpu.SMEM)


def nn(a, b):
    return jnp.dot(a, b, preferred_element_type=F32)


def nt(a, b):
    return lax.dot_general(a, b, (((1,), (1,)), ((), ())), preferred_element_type=F32)


def tn(a, b):
    return lax.dot_general(a, b, (((0,), (0,)), ((), ())), preferred_element_type=F32)


def gelu_pair(x):
    half = 0.5 + 0.5 * lax.erf(x * RSQRT2)
    return x * half, half + x * (RSQRT2PI * jnp.exp(-0.5 * (x * x)))


def shape(dims, dtype=F32):
    return jax.ShapeDtypeStruct(dims, dtype)


def whole(dims):
    zeros = (0,) * len(dims)
    return pl.BlockSpec(dims, lambda i: zeros)


def at(dims, first):
    rest = (0,) * (len(dims) - 1)
    return pl.BlockSpec(dims, lambda i: (first,) + rest)


def column(row, size):
    r = lax.broadcasted_iota(jnp.int32, (size, size), 0)
    c = lax.broadcasted_iota(jnp.int32, (size, size), 1)
    return jnp.sum(jnp.where(r == c, jnp.broadcast_to(row, (size, size)), 0.0), 1, keepdims=True)


def stats_kernel(tok, out):
    images, width, _ = tok.shape

    def one(b, carry):
        x = tok[b].astype(F32)
        m = jnp.sum(x, 0, keepdims=True) * (1.0 / width)
        o = x - m
        out[0, pl.ds(b, 1), :] = m
        out[1, pl.ds(b, 1), :] = jnp.sum(o * o, 0, keepdims=True)
        return carry

    lax.fori_loop(0, images, one, 0, unroll=2)


def stats_call(tok):
    images, width, patches = tok.shape
    return pl.pallas_call(
        stats_kernel,
        grid=(1,),
        in_specs=[whole(tok.shape)],
        out_specs=whole((2, images, patches)),
        out_shape=shape((2, images, patches)),
        compiler_params=pltpu.CompilerParams(vmem_limit_bytes=24 * MIB),
        name="stats",
    )(tok)


def join_stats(stats, mr, width):
    m = 0.25 * ((stats[0][0] + stats[1][0]) + (stats[2][0] + stats[3][0]))
    q = jnp.zeros_like(m)
    for s in stats:
        o = s[0] - m
        q = q + (s[1] + width * (o * o))
    mr[0] = m
    mr[1] = lax.rsqrt(q * (1.0 / (4 * width)) + EPS)


def spread_rows(dst, src, P_, PP):
    for j in range(4):
        dst[pl.ds(j * PP, P_), :] = src[pl.ds(j * P_, P_), :].astype(F32)


def picker(rows, columns, P_, PP):
    r = lax.broadcasted_iota(jnp.int32, (rows, columns), 0)
    c = lax.broadcasted_iota(jnp.int32, (rows, columns), 1)
    pick = jnp.zeros((rows, columns), F32)
    for j in range(4):
        inside = jnp.logical_and(r >= j * PP, r < j * PP + P_)
        pick = jnp.where(jnp.logical_and(inside, c == r - j * (PP - P_)), 1.0, pick)
    return pick.astype(BF16)


def token_kernel(me, keep, t0, t1, t2, t3, tok, w_in, b_in, w_outT, b_out, g1, c1,
                 act, gp, s0, s1, s2, s3,
                 mr, left, wide, biasb, gcol, mix, rhs, buf, sem, *, first, P_, PP):
    nb, width, S = tok.shape
    K = w_in.shape[1]
    join_stats((t0, t1, t2, t3), mr, width)
    gcol[0] = jnp.broadcast_to(column(g1[...], width), (width, S))
    gcol[1] = jnp.broadcast_to(column(c1[...], width), (width, S))
    wide[...] = jnp.zeros_like(wide)
    spread_rows(wide, w_outT, P_, PP)
    left[:, 0:K] = wide[...].astype(BF16)
    left[:, K:] = picker(4 * PP, left.shape[1] - K, P_, PP)
    biasb[...] = jnp.zeros_like(biasb)
    bcol = jnp.broadcast_to(column(b_out[...], S), (S, biasb.shape[1]))
    for j in range(4):
        biasb[pl.ds(j * PP, P_), :] = bcol[j * P_:(j + 1) * P_, :]
    rhs[...] = jnp.zeros_like(rhs)

    def pair(p, carry):
        for i in range(2):
            b = 2 * p + i
            raw = tok[b]
            x = raw.astype(F32)
            m = mr[0, pl.ds(first + b, 1), :]
            r = mr[1, pl.ds(first + b, 1), :]
            mix[pl.ds(i * width, width), :] = (((x - m) * r) * gcol[0] + gcol[1]).astype(BF16)
            rhs[pl.ds(i * width, width), K:K + S] = raw
        pre = nn(mix[...], w_in[...]) + b_in[...]
        g, d = gelu_pair(pre)
        k0, k1 = keep[first + 2 * p], keep[first + 2 * p + 1]
        rows = lax.broadcasted_iota(jnp.int32, (2 * width, 1), 0)
        a = (g * jnp.where(rows < width, k0, k1)).astype(BF16)
        rhs[:, 0:K] = a
        here = pl.ds(pl.multiple_of(p * 2 * width, 2 * width), 2 * width)
        act[here, :] = a
        gp[here, :] = d.astype(BF16)
        lanes = lax.broadcasted_iota(jnp.int32, (1, 2 * width), 1)
        out = nt(left[...], rhs[...]) + biasb[...] * jnp.where(lanes < width, k0, k1)
        for j in range(4):
            buf[j, p] = out[j * PP:(j + 1) * PP, :].astype(BF16)
        return carry

    lax.fori_loop(0, nb // 2, pair, 0)
    sends = (s0, s1, s2, s3)
    copies = [pltpu.make_async_copy(buf.at[me[0] ^ k], sends[k], sem.at[k]) for k in range(4)]
    for c in copies:
        c.start()
    for c in copies:
        c.wait()


def token_call(me, keep, stats, tok, w_in, b_in, w_outT, b_out, g1, c1, half, P_, PP):
    images, width, S = tok.shape
    nb = images // 2
    K = w_in.shape[1]
    piece = shape((nb // 2, PP, 2 * width), BF16)
    return pl.pallas_call(
        functools.partial(token_kernel, first=half * nb, P_=P_, PP=PP),
        grid=(1,),
        in_specs=[SMEM, SMEM] + [whole(stats[0].shape)] * 4 + [at((nb, width, S), half), whole(w_in.shape), whole(b_in.shape),
                  whole(w_outT.shape), whole(b_out.shape), whole(g1.shape), whole(c1.shape)],
        out_specs=[whole((nb * width, K)), whole((nb * width, K)), ANY, ANY, ANY, ANY],
        out_shape=[shape((nb * width, K), BF16), shape((nb * width, K), BF16), piece, piece, piece, piece],
        scratch_shapes=[pltpu.VMEM((2, images, S), F32), pltpu.VMEM((4 * PP, K + 256), BF16), pltpu.VMEM((4 * PP, K), F32),
                        pltpu.VMEM((4 * PP, 2 * width), F32), pltpu.VMEM((2, width, S), F32), pltpu.VMEM((2 * width, S), BF16),
                        pltpu.VMEM((2 * width, K + 256), BF16), pltpu.VMEM((4, nb // 2, PP, 2 * width), BF16),
                        pltpu.SemaphoreType.DMA((4,))],
        compiler_params=pltpu.CompilerParams(vmem_limit_bytes=32 * MIB),
        name="token_forward",
    )(me, keep, *stats, tok, w_in, b_in, w_outT, b_out, g1, c1)


def chan_kernel(me, keep, p0, p1, p2, p3, cot, w1, w2, b1, b2, g2, c2, *rest, nb, P_, R, RB, first, joined):
    rest = rest[1:] if joined else rest
    (act, pg, b3, x, og, out, s0, s1, s2, s3, gg, gc, b4,
     st, ct, nrm, r2s, acc_o, acc_i, bufi, bufo, sem) = rest
    step = pl.program_id(0)
    last = pl.num_programs(0) - 1
    W = x.shape[1]
    q = W // 4
    rows = nb * P_
    pieces = (p0, p1, p2, p3)
    sends = (s0, s1, s2, s3)

    @pl.when(step == 0)
    def _():
        copies = [pltpu.make_async_copy(pieces[k], bufi.at[me[0] ^ k], sem.at[k]) for k in range(4)]
        for c in copies:
            c.start()
        tail = jnp.zeros((R - rows, W), F32)
        ct[pl.ds(rows, R - rows), :] = tail
        st[pl.ds(rows, R - rows), :] = tail
        for b in range(nb):
            v = cot[b].astype(F32)
            ct[pl.ds(b * P_, P_), :] = v
            st[pl.ds(b * P_, P_), :] = v * keep[first + b]

        def put(i, s):
            r = pl.ds(pl.multiple_of(i * RB, RB), RB)
            v = st[r, :]
            og[r, :] = v.astype(BF16)
            return s + jnp.sum(v, 0, keepdims=True)

        b4[...] = lax.fori_loop(0, R // RB, put, jnp.zeros((1, W), F32))
        for c in copies:
            c.wait()
        for b in range(nb):
            lo = (b % 2) * q
            v = jnp.concatenate([bufi[j, b // 2][0:P_, lo:lo + q].astype(F32) for j in range(4)], axis=1)
            st[pl.ds(b * P_, P_), :] = v

        def norm(i, _):
            r = pl.ds(pl.multiple_of(i * RB, RB), RB)
            v = st[r, :]
            m = jnp.mean(v, 1, keepdims=True)
            o = v - m
            rr = lax.rsqrt(jnp.mean(o * o, 1, keepdims=True) + EPS)
            n = o * rr
            nrm[r, :] = n
            r2s[r, :] = jnp.broadcast_to(rr, (RB, 128))
            x[r, :] = (n * g2[...] + c2[...]).astype(BF16)
            return 0

        lax.fori_loop(0, R // RB, norm, 0)
        acc_o[...] = jnp.zeros_like(acc_o)
        acc_i[...] = jnp.zeros_like(acc_i)

    pre = nn(x[...], w1[...]) + b1[...]
    g, gp = gelu_pair(pre)
    a = g.astype(BF16)
    act[...] = a
    d = (nt(og[...], w2[...]) * gp).astype(BF16)
    pg[...] = d
    b3[...] = jnp.sum(d.astype(F32), 0, keepdims=True)
    acc_o[...] += nn(a, w2[...])
    acc_i[...] += nt(d, w1[...])

    @pl.when(step == last)
    def _():
        def back(i, s):
            r = pl.ds(pl.multiple_of(i * RB, RB), RB)
            e = acc_i[r, :]
            n = nrm[r, :]
            sg, sc = s
            sg = sg + jnp.sum((e * n).reshape(RB // 8, 8, W), 0)
            sc = sc + jnp.sum(e.reshape(RB // 8, 8, W), 0)
            e = e * g2[...]
            m1 = jnp.mean(e, 1, keepdims=True)
            m2 = jnp.mean(e * n, 1, keepdims=True)
            acc_i[r, :] = ct[r, :] + r2s[r, 0:1] * (e - m1 - n * m2)
            return sg, sc

        z = jnp.zeros((8, W), F32)
        sg, sc = lax.fori_loop(0, R // RB, back, (z, z))
        gg[...] = jnp.sum(sg, 0, keepdims=True)
        gc[...] = jnp.sum(sc, 0, keepdims=True)
        for b in range(nb):
            r = pl.ds(b * P_, P_)
            out[b] = (st[r, :] + keep[first + b] * (acc_o[r, :] + b2[...])).astype(BF16)
        for p in range(nb // 2):
            va = acc_i[pl.ds(2 * p * P_, P_), :]
            vb = acc_i[pl.ds((2 * p + 1) * P_, P_), :]
            for j in range(4):
                bufo[j, p, 0:P_, :] = jnp.concatenate([va[:, j * q:(j + 1) * q], vb[:, j * q:(j + 1) * q]], axis=1).astype(BF16)
                bufo[j, p, P_:, :] = jnp.zeros((bufo.shape[2] - P_, 2 * q), BF16)
        copies = [pltpu.make_async_copy(bufo.at[me[0] ^ k], sends[k], sem.at[k]) for k in range(4)]
        for c in copies:
            c.start()
        for c in copies:
            c.wait()


def chan_call(me, keep, pieces, cot, half, w1, w2, b1, b2, g2, c2, out_before, fb=512):
    images, P_, W = cot.shape
    nb = images // 2
    rows = nb * P_
    R = -(-rows // 16) * 16
    F = w1.shape[1]
    wide = pl.BlockSpec((R, fb), lambda i: (0, i))
    line = pl.BlockSpec((1, fb), lambda i: (0, i))
    row = whole((1, W))
    piece = shape(pieces[0].shape, BF16)
    joined = out_before is not None
    args = (me, keep, *pieces, cot, w1, w2, b1, b2, g2, c2) + ((out_before,) if joined else ())
    return pl.pallas_call(
        functools.partial(chan_kernel, nb=nb, P_=P_, R=R, RB=16, first=half * nb, joined=joined),
        grid=(F // fb,),
        in_specs=[SMEM, SMEM, ANY, ANY, ANY, ANY, at((nb, P_, W), half),
                  pl.BlockSpec((W, fb), lambda i: (0, i)), pl.BlockSpec((fb, W), lambda i: (i, 0)),
                  line, row, row, row] + ([ANY] if joined else []),
        out_specs=[wide, wide, line, whole((R, W)), whole((R, W)), at((nb, P_, W), half), ANY, ANY, ANY, ANY, row, row, row],
        out_shape=[shape((R, F), BF16), shape((R, F), BF16), shape((1, F)), shape((R, W), BF16), shape((R, W), BF16),
                   shape(cot.shape, BF16), piece, piece, piece, piece, shape((1, W)), shape((1, W)), shape((1, W))],
        scratch_shapes=[pltpu.VMEM((R, W), F32)] * 3 + [pltpu.VMEM((R, 128), F32), pltpu.VMEM((R, W), F32), pltpu.VMEM((R, W), F32),
                        pltpu.VMEM((4,) + piece.shape, BF16), pltpu.VMEM((4,) + piece.shape, BF16), pltpu.SemaphoreType.DMA((4,))],
        input_output_aliases={13: 5} if joined else {},
        compiler_params=pltpu.CompilerParams(vmem_limit_bytes=56 * MIB),
        name="channel_mlp",
    )(*args)


def grad_kernel(a0, a1, b0, b1, out):
    out[...] = (tn(a0[...], b0[...]) + tn(a1[...], b1[...])).astype(BF16)


def grad_call(a, b, fb=768):
    R, F = a[0].shape
    W = b[0].shape[1]
    wide = pl.BlockSpec((R, fb), lambda i: (0, i))
    return pl.pallas_call(
        grad_kernel,
        grid=(F // fb,),
        in_specs=[wide, wide, whole((R, W)), whole((R, W))],
        out_specs=pl.BlockSpec((fb, W), lambda i: (i, 0)),
        out_shape=shape((F, W), BF16),
        compiler_params=pltpu.CompilerParams(vmem_limit_bytes=40 * MIB),
        name="channel_grad",
    )(*a, *b)


def as_row(col, size):
    r = lax.broadcasted_iota(jnp.int32, (size, size), 0)
    c = lax.broadcasted_iota(jnp.int32, (size, size), 1)
    return jnp.sum(jnp.where(r == c, jnp.broadcast_to(col, (size, size)), 0.0), 0, keepdims=True)


def back_kernel(me, keep, t0, t1, t2, t3, p0, p1, p2, p3, act, gp, tok, w_in, w_outT, g1, c1, *rest, first, P_, PP, joined):
    if joined:
        before, rest = rest[:6], rest[6:]
    u, ps, gw1, gw2, ob1, ob2, og, oc, mr, right, wide, gcol, mix, bufi, gb1, gb2, gg, gc, sem = rest
    nb, width, S = tok.shape
    K = w_in.shape[1]
    pieces = (p0, p1, p2, p3)
    copies = [pltpu.make_async_copy(pieces[k], bufi.at[me[0] ^ k], sem.at[k]) for k in range(4)]
    for c in copies:
        c.start()
    join_stats((t0, t1, t2, t3), mr, width)
    gcol[0] = jnp.broadcast_to(column(g1[...], width), (width, S))
    gcol[1] = jnp.broadcast_to(column(c1[...], width), (width, S))
    wide[...] = jnp.zeros_like(wide)
    spread_rows(wide, w_outT, P_, PP)
    right[:, 0:K] = wide[...].astype(BF16)
    right[:, K:] = picker(4 * PP, right.shape[1] - K, P_, PP)
    for o in (gb1, gb2, gg, gc):
        o[...] = jnp.zeros_like(o)
    if joined:
        gw1[...] = before[0][...]
        gw2[...] = before[1][...]
    else:
        gw1[...] = jnp.zeros_like(gw1)
        gw2[...] = jnp.zeros_like(gw2)
    for c in copies:
        c.wait()

    def pair(p, carry):
        sg = bufi[:, p].reshape(4 * PP, 2 * width)
        here = pl.ds(pl.multiple_of(p * 2 * width, 2 * width), 2 * width)
        k0, k1 = keep[first + 2 * p], keep[first + 2 * p + 1]
        lanes = lax.broadcasted_iota(jnp.int32, (1, 2 * width), 1)
        gb2[...] += sg.astype(F32) * jnp.where(lanes < width, k0, k1)
        both = tn(sg, right[...])
        rows = lax.broadcasted_iota(jnp.int32, (2 * width, 1), 0)
        pre1 = ((both[:, 0:K] * gp[here, :].astype(F32)) * jnp.where(rows < width, k0, k1)).astype(BF16)
        gb1[...] += jnp.sum(pre1.astype(F32).reshape(2 * width // 8, 8, K), 0)
        gw2[...] += nn(sg, act[here, :])
        ng = nt(pre1, w_in[...])
        for i in range(2):
            b = 2 * p + i
            part = slice(i * width, (i + 1) * width)
            m = mr[0, pl.ds(first + b, 1), :]
            r = mr[1, pl.ds(first + b, 1), :]
            n = (tok[b].astype(F32) - m) * r
            mix[pl.ds(i * width, width), :] = (n * gcol[0] + gcol[1]).astype(BF16)
            v = ng[part, :]
            gg[...] += v * n
            gc[...] += v
            e = v * gcol[0]
            ps[0, pl.ds(b, 1), :] = jnp.sum(e, 0, keepdims=True)
            ps[1, pl.ds(b, 1), :] = jnp.sum(e * n, 0, keepdims=True)
            u[b] = both[part, K:K + S] + r * e
        gw1[...] += tn(mix[...], pre1)
        return carry

    lax.fori_loop(0, nb // 2, pair, 0)
    sums = (jnp.sum(gb1[...], 0, keepdims=True),
            as_row(jnp.sum(gb2[...], 1, keepdims=True), 4 * PP),
            as_row(jnp.sum(gg[...], 1, keepdims=True), width),
            as_row(jnp.sum(gc[...], 1, keepdims=True), width))
    for i, o in enumerate((ob1, ob2, og, oc)):
        o[...] = sums[i] + before[2 + i][...] if joined else sums[i]


def back_call(me, keep, stats, pieces, act, gp, tok, w_in, w_outT, g1, c1, half, P_, PP, before):
    images, width, S = tok.shape
    nb = images // 2
    K = w_in.shape[1]
    joined = before is not None
    sums = [(S, K), (4 * PP, K), (1, K), (1, 4 * PP), (1, width), (1, width)]
    args = (me, keep, *stats, *pieces, act, gp, tok, w_in, w_outT, g1, c1) + (tuple(before) if joined else ())
    return pl.pallas_call(
        functools.partial(back_kernel, first=half * nb, P_=P_, PP=PP, joined=joined),
        grid=(1,),
        in_specs=[SMEM, SMEM] + [whole(stats[0].shape)] * 4 + [ANY] * 4 + [whole(act.shape), whole(gp.shape),
                  at((nb, width, S), half), whole(w_in.shape), whole(w_outT.shape), whole(g1.shape), whole(c1.shape)]
                 + ([whole(s) for s in sums] if joined else []),
        out_specs=[whole((nb, width, S)), whole((2, nb, S))] + [whole(s) for s in sums],
        out_shape=[shape((nb, width, S)), shape((2, nb, S))] + [shape(s) for s in sums],
        scratch_shapes=[pltpu.VMEM((2, images, S), F32), pltpu.VMEM((4 * PP, K + 256), BF16), pltpu.VMEM((4 * PP, K), F32),
                        pltpu.VMEM((2, width, S), F32), pltpu.VMEM((2 * width, S), BF16), pltpu.VMEM((4,) + pieces[0].shape, BF16),
                        pltpu.VMEM((8, K), F32), pltpu.VMEM((4 * PP, 2 * width), F32), pltpu.VMEM((width, S), F32),
                        pltpu.VMEM((width, S), F32), pltpu.SemaphoreType.DMA((4,))],
        compiler_params=pltpu.CompilerParams(vmem_limit_bytes=48 * MIB),
        name="token_backward",
    )(*args)


def finish_kernel(t0, t1, t2, t3, s0, s1, s2, s3, u, tok, *rest, first, joined):
    out, mr = rest[1:] if joined else rest
    nb, width, S = tok.shape
    join_stats((t0, t1, t2, t3), mr, width)
    scale = 1.0 / (4 * width)

    def one(b, carry):
        a = ((s0[0, pl.ds(b, 1), :] + s1[0, pl.ds(b, 1), :]) + (s2[0, pl.ds(b, 1), :] + s3[0, pl.ds(b, 1), :])) * scale
        c = ((s0[1, pl.ds(b, 1), :] + s1[1, pl.ds(b, 1), :]) + (s2[1, pl.ds(b, 1), :] + s3[1, pl.ds(b, 1), :])) * scale
        m = mr[0, pl.ds(first + b, 1), :]
        r = mr[1, pl.ds(first + b, 1), :]
        n = (tok[b].astype(F32) - m) * r
        out[b] = u[b] - r * (a + n * c)
        return carry

    lax.fori_loop(0, nb, one, 0, unroll=2)


def finish_call(stats, sums, u, tok, half, out_before):
    images, width, S = tok.shape
    nb = images // 2
    joined = out_before is not None
    return pl.pallas_call(
        functools.partial(finish_kernel, first=half * nb, joined=joined),
        grid=(1,),
        in_specs=[whole(stats[0].shape)] * 4 + [whole(sums[0].shape)] * 4 + [whole(u.shape), at((nb, width, S), half)]
                 + ([ANY] if joined else []),
        out_specs=at((nb, width, S), half),
        out_shape=shape((images, width, S)),
        scratch_shapes=[pltpu.VMEM((2, images, S), F32)],
        input_output_aliases={10: 0} if joined else {},
        compiler_params=pltpu.CompilerParams(vmem_limit_bytes=40 * MIB),
        name="norm_backward",
    )(*stats, *sums, u, tok, *((out_before,) if joined else ()))


def exchange(value):
    return [value] + [lax.ppermute(value, "chan", [(i, i ^ k) for i in range(4)]) for k in (1, 2, 3)]


def trade(pieces):
    return [pieces[0]] + [lax.ppermute(pieces[k], "chan", [(i, i ^ k) for i in range(4)]) for k in (1, 2, 3)]


def shards(tokens, ln1_gain, ln1_bias, mix_in, mix_in_bias, mix_out, mix_out_bias, ln2_gain, ln2_bias,
           chan_in, chan_in_bias, chan_out, chan_out_bias, skip_masks, cotangent):
    images, S, width = tokens.shape
    P_ = cotangent.shape[1]
    W = cotangent.shape[2]
    PP = -(-P_ // 8) * 8
    tok = jnp.swapaxes(tokens, 1, 2)
    w_outT = jnp.swapaxes(mix_out, 0, 1)
    row = lambda v: v.reshape(1, -1)
    chan = lax.axis_index("chan")
    me = chan.reshape(1).astype(jnp.int32)
    keep1 = skip_masks[:, 0].astype(F32)
    keep2 = skip_masks[:, 1].astype(F32)
    g1, c1 = row(ln1_gain), row(ln1_bias)

    stats = exchange(stats_call(tok))
    halves = (0, 1)
    fwd = [token_call(me, keep1, stats, tok, mix_in, row(mix_in_bias), w_outT, row(mix_out_bias), g1, c1, h, P_, PP) for h in halves]
    arrived = [trade(f[2:6]) for f in fwd]
    chans, out = [], None
    for h in halves:
        r = chan_call(me, keep2, arrived[h], cotangent, h, chan_in, chan_out, row(chan_in_bias), row(chan_out_bias),
                      row(ln2_gain), row(ln2_bias), out)
        out = r[5]
        chans.append(r)
    returned = [trade(r[6:10]) for r in chans]
    grad_w4 = grad_call([r[0] for r in chans], [r[4] for r in chans])
    grad_w3 = grad_call([r[1] for r in chans], [r[3] for r in chans])
    sums, back = None, []
    for h in halves:
        r = back_call(me, keep1, stats, returned[h], fwd[h][0], fwd[h][1], tok, mix_in, w_outT, g1, c1, h, P_, PP, sums)
        sums = r[2:]
        back.append(r)
    grad = None
    for h in halves:
        grad = finish_call(stats, exchange(back[h][1]), back[h][0], tok, h, grad)
    gw1, gw2, gb1, gb2, gg1, gc1 = sums
    place = lambda v: lax.dynamic_update_slice(jnp.zeros((W,), F32), v.reshape(-1), (chan * width,))
    unpad = lambda v: v.reshape(4, PP, -1)[:, :P_].reshape(S, -1)
    both = lambda i: (chans[0][i] + chans[1][i]).reshape(-1)
    small = lax.psum((place(gg1), place(gc1), gw1, gb1.reshape(-1), unpad(gw2), unpad(gb2.reshape(-1, 1)).reshape(-1),
                      both(10), both(11), both(2), both(12)), ("dp", "chan"))
    s_g1, s_c1, s_w1, s_b1, s_w2, s_b2, s_g2, s_c2, s_b3, s_b4 = small
    share_w4 = lax.psum_scatter(grad_w4, ("dp", "chan"), scatter_dimension=0, tiled=True).astype(F32)
    share_w3 = lax.psum_scatter(grad_w3, ("dp", "chan"), scatter_dimension=0, tiled=True).astype(F32)
    return (out, jnp.swapaxes(grad, 1, 2), s_g1, s_c1, s_w1, s_b1, jnp.swapaxes(s_w2, 0, 1), s_b2, s_g2, s_c2,
            jnp.swapaxes(share_w3, 0, 1), s_b3, share_w4, s_b4)


def solution(mesh):
    rep = P()
    return jax.shard_map(
        shards, mesh=mesh,
        in_specs=(P("dp", None, "chan"), P("chan"), P("chan")) + (rep,) * 10 + (P("dp", None), P("dp", "chan", None)),
        out_specs=(P("dp", "chan", None), P("dp", None, "chan"), rep, rep, rep, rep, rep, rep, rep, rep,
                   P(None, ("dp", "chan")), rep, P(("dp", "chan"), None), rep),
        check_vma=False,
    )
```

time: 802 us -> 499 us (0.62); the launches traced: 790 us -> 496 us
  matrix products: 157 us -> 0 us
  Pallas kernels: 0 us -> 135 us
  local copies, waits for them, and re-layouts: 137 us -> 35.8 us
  waiting for transfers between devices: 324 us -> 250 us
  other arithmetic: 58.8 us -> 4.54 us
  blocking collectives: 92.5 us -> 40.6 us
  starting transfers between devices: 5.67 us -> 15.3 us
    dot_general x12 -> x0, matrix products: 157 us -> none  [the longest x1 48.6 us: shards(): jnp.dot(flat_in, chan_in, preferred_element_type=jnp.float32) + chan_in_bias]
    reduce_scatter x1, waiting for transfers between devices: 141 us -> 0.01 us  [shards(): lax.psum_scatter(grad_w4, ('dp', 'chan'), scatter_dimension=0, tiled=True)]
    pallas_call x0 -> x11, Pallas kernels: none -> 135 us  [the longest x2 73.9 us: chan_call(): pl.pallas_call(functools.partial(chan_kernel, nb=nb, P_=P_, R=R, RB=16, f...]
    psum x1, waiting for transfers between devices: 13.1 us -> 133 us  [shards(): lax.psum((place(gg1), place(gc1), gw1, gb1.reshape(-1), unpad(gw2), unpad...]
    convert_element_type x11 -> x0, local copies, waits for them, and re-layouts: 85.7 us -> none  [the longest x5 34.4 us: shards(): stream_wide = patch_rows.astype(jnp.float32)]
    reduce_scatter x1, waiting for transfers between devices: 142 us -> 102 us  [shards(): lax.psum_scatter(grad_w3, ('dp', 'chan'), scatter_dimension=0, tiled=True)]
    all_to_all x1 -> x0, blocking collectives: 29.7 us -> none  [shards(): lax.all_to_all(stream_grad, 'chan', split_axis=2, concat_axis=1, tiled=True)]
    all_to_all x1 -> x0, waiting for transfers between devices: 28.1 us -> none  [shards(): lax.all_to_all(residual.astype(jnp.bfloat16), 'chan', split_axis=1, conca...]
  transfers between devices with their start and end apart: 4 -> 24, of which waited for: 4 -> 7; matrix products, arithmetic and copies ran while one was open for 9% -> 2% of each run, Pallas kernels for 0% -> 16%
where the time goes in v1:
time: 499 us; the launch traced here: 496 us
  waiting for transfers between devices  250 us (50%)
  Pallas kernels  135 us (27%)
  blocking collectives  40.6 us (8%)
  local copies, waits for them, and re-layouts  35.8 us (7%)
  starting transfers between devices  15.3 us (3%)
  between operations  14.2 us (3%)
    psum x1, waiting for transfers between devices, shards(): lax.psum((place(gg1), place(gc1), gw1, gb1.reshape(-1), unpad(gw2), unpad...  133 us
    reduce_scatter x1, waiting for transfers between devices, shards(): lax.psum_scatter(grad_w3, ('dp', 'chan'), scatter_dimension=0, tiled=True)  102 us
    pallas_call x2, Pallas kernels, chan_call(): pl.pallas_call(functools.partial(chan_kernel, nb=nb, P_=P_, R=R, RB=16, f...  73.9 us
    psum x1, blocking collectives, shards(): lax.psum((place(gg1), place(gc1), gw1, gb1.reshape(-1), unpad(gw2), unpad...  40.6 us
    unnamed x114, local copies, waits for them, and re-layouts  31.3 us
    pallas_call x2, Pallas kernels, back_call(): pl.pallas_call(functools.partial(back_kernel, first=half * nb, P_=P_, PP=...  21.9 us
    pallas_call x2, Pallas kernels, grad_call(): pl.pallas_call(grad_kernel, grid=(F // fb,), in_specs=[wide, wide, whole(...  19.9 us
    pallas_call x2, Pallas kernels, token_call(): pl.pallas_call(functools.partial(token_kernel, first=half * nb, P_=P_, PP...  12.6 us
  transfers between devices with their start and end apart: 24, of which 7 were waited for; matrix products, arithmetic and copies ran while one was open for 2% of the time, Pallas kernels for 16%

profile of v1, /device:TPU:17, one launch (start us, length us, event | category | flops | bytes accessed | tf_op | source)
XLA Modules:
  0.0 495.6 jit_solution(6479044646747500368)
XLA Ops:
  7.2 1.8 copy-done
  9.0 1.7 stats.1.t0
  10.7 0.7 collective-permute-start
  11.5 1.3 collective-permute-start.1
  13.2 0.5 convert_bitcast_fusion.1
  13.7 1.4 collective-permute-done.1.t2
  15.2 1.6 collective-permute-done.2.t3
  16.8 0.9 copy-done.8
  17.7 0.9 copy-done.10
  18.6 6.3 %token_forward.3 = (bf16[2688,384]{1,0:T(8,128)(2,1)S(1)}, bf16[2688,384]{1,0:T(8,128)(2,1)S(1)}, bf16[7,56,384]{2,1,0:T(8,128)(2,1)S(1)}, bf16[7,56,384]{2,1,0:...) custom-call(s32[1]{0:T(128)} %bitcast.me, f32[28]{0:T(128)S(1)} %get-tuple-element.132.keep, ...), custom_call_target="tpu_custom_call" | custom-call | tf_op jit(solution)/shard_map/token_forward/pallas_call | solution.py:164
  25.0 1.3 copy-done.15
  26.3 1.3 copy-done.17
  27.6 0.7 copy-done.28
  28.7 1.1 collective-permute-start.7
  29.7 0.7 collective-permute-start.8
  30.5 6.3 %token_forward.2 = (bf16[2688,384]{1,0:T(8,128)(2,1)S(1)}, bf16[2688,384]{1,0:T(8,128)(2,1)S(1)}, bf16[7,56,384]{2,1,0:T(8,128)(2,1)S(1)}, bf16[7,56,384]{2,1,0:...) custom-call(s32[1]{0:T(128)} %bitcast.me, f32[28]{0:T(128)S(1)} %get-tuple-element.132.keep, ...), custom_call_target="tpu_custom_call" | custom-call | tf_op jit(solution)/shard_map/token_forward/pallas_call | solution.py:164
  36.8 1.3 copy-done.12
  38.1 1.3 copy-done.14
  39.4 0.7 copy-done.31
  40.2 1.1 collective-permute-start.4
  41.3 1.0 collective-permute-start.5
  42.3 0.6 reshape.96.b2
  42.8 0.6 reshape.97.g2
  43.4 0.6 reshape.98.c2
  44.0 0.5 collective-permute-done.8.p3
  45.3 36.5 %channel_mlp.2 = (bf16[688,3072]{1,0:T(8,128)(2,1)}, bf16[688,3072]{1,0:T(8,128)(2,1)}, f32[1,3072]{1,0:T(1,128)}, bf16[688,768]{1,0:T(8,128)(2,1)}, bf16[688,76...) custom-call(s32[1]{0:T(128)} %bitcast.me, ...), custom_call_target="tpu_custom_call" | custom-call | tf_op jit(solution)/shard_map/channel_mlp/pallas_call | solution.py:292
  81.9 0.7 copy-done.38
  82.7 37.4 %channel_mlp.3 = (bf16[688,3072]{1,0:T(8,128)(2,1)}, bf16[688,3072]{1,0:T(8,128)(2,1)}, f32[1,3072]{1,0:T(1,128)}, bf16[688,768]{1,0:T(8,128)(2,1)}, bf16[688,76...) custom-call(s32[1]{0:T(128)} %bitcast.me, ...), custom_call_target="tpu_custom_call", output_to_operand_aliasing={{5}: (13, {})} | custom-call | tf_op jit(solution)/shard_map/channel_mlp/pallas_call | solution.py:292
  120.2 2.2 copy-done.5
  122.4 1.2 copy-done.21
  123.6 10.0 %channel_grad.3 = bf16[3072,768]{1,0:T(8,128)(2,1)} custom-call(bf16[688,3072]{1,0:T(8,128)(2,1)S(1)} %bitcast.31, bf16[688,3072]{1,0:T(8,128)(2,1)S(1)} %copy-done.5, bf16[688,768]{1,0:T(8,128)(2,1)S(1)} %copy-done.19, bf16[688,768]{1,0:T(8,128)(2,1)S(1)} %copy-done.21), custom_call_target="tpu_custom_call" | custom-call | tf_op jit(solution)/shard_map/channel_grad/pallas_call | solution.py:317
  133.7 1.1 copy-done.18
  135.2 2.2 copy-done.3
  137.4 2.2 copy-done.4
  139.6 9.9 %channel_grad.2 = bf16[3072,768]{1,0:T(8,128)(2,1)} custom-call(bf16[688,3072]{1,0:T(8,128)(2,1)S(1)} %copy-done.3, bf16[688,3072]{1,0:T(8,128)(2,1)S(1)} %copy-done.4, bf16[688,768]{1,0:T(8,128)(2,1)S(1)} %copy-done.18, bf16[688,768]{1,0:T(8,128)(2,1)S(1)} %copy-done.20), custom_call_target="tpu_custom_call" | custom-call | tf_op jit(solution)/shard_map/channel_grad/pallas_call | solution.py:317
  149.6 1.3 collective-permute-start.13
  150.9 0.9 collective-permute-start.14
  151.8 1.2 collective-permute-start.10
  153.0 0.7 copy-done.29
  153.7 0.9 collective-permute-start.11
  154.6 3.7 collective-permute-done.13.p2
  158.3 7.9 %collective-permute-done.14.p3 = bf16[7,56,384]{2,1,0:T(8,128)(2,1)} collective-permute-done((bf16[7,56,384]{2,1,0:T(8,128)(2,1)}, bf16[7,56,384]{2,1,0:T(8,128)(2,1)}, u32[]{:S(2)}, u32[]{:S(2)}) %collective-permute-start.14) | collective-permute-done | bytes 301088 | tf_op jit(solution)/shard_map/ppermute | solution.py:465
  166.2 1.0 copy-done.30
  167.2 11.1 %token_backward.2 = (f32[14,192,196]{2,1,0:T(8,128)}, f32[2,14,196]{2,1,0:T(8,128)S(1)}, f32[196,384]{1,0:T(8,128)S(1)}, f32[224,384]{1,0:T(8,128)S(1)}, f32[1,3...) custom-call(s32[1]{0:T(128)} %bitcast.me, f32[28]{0:T(128)S(1)} %get-tuple-element.132.keep, ...), custom_call_target="tpu_custom_call" | custom-call | tf_op jit(solution)/shard_map/token_backward/pallas_call | solution.py:407
  178.4 0.7 copy-done.26
  179.2 1.0 copy-done.27
  180.2 10.8 %token_backward.3 = (f32[14,192,196]{2,1,0:T(8,128)}, f32[2,14,196]{2,1,0:T(8,128)S(1)}, f32[196,384]{1,0:T(8,128)S(1)}, f32[224,384]{1,0:T(8,128)S(1)}, f32[1,3...) custom-call(s32[1]{0:T(128)} %bitcast.me, f32[28]{0:T(128)S(1)} %get-tuple-element.132.keep, ...), custom_call_target="tpu_custom_call" | custom-call | tf_op jit(solution)/shard_map/token_backward/pallas_call | solution.py:407
  191.0 0.7 copy-done.22
  191.8 0.7 copy-done.23
  192.9 1.2 collective-permute-start.16
  194.6 1.2 collective-permute-start.19
  195.8 1.8 reshape.103
  197.6 0.7 collective-permute-start.20
  198.9 0.7 reduce.10
  200.1 40.6 %all-reduce = (f32[768]{0:T(1024)}, f32[768]{0:T(1024)}, f32[384]{0:T(512)}, f32[196]{0:T(256)}, f32[768]{0:T(1024)}, /*index=5*/f32[768]{0:T(1024)}, f32[3072]{0:T(1024)}, f32[768]{0:T(1024)}) all-reduce(f32[768]{0:T(1024)S(1)} %dynamic_update_slice.6, ...), channel_id=1, replica_groups=mesh['dp'=8,'chan'=4] {'dp','chan'}, use_global_device_ids=true, to_apply=%region_0.0 | all-reduce | flops 7492 | bytes 59936 | tf_op jit(solution)/shard_map/psum | solution.py:508
  240.8 1.8 copy-done.6
  242.6 2.3 norm_backward.2.rest_0_
  244.9 2.3 norm_backward.3
  247.2 1.6 convert_element_type.18
  248.8 102.5 %reduce-scatter.3.cloned.1.call-done = bf16[96,768]{1,0:T(8,128)(2,1)} async-done(((bf16[3072,768]{1,0:T(8,128)(2,1)}), bf16[96,768]{1,0:T(8,128)(2,1)}) %reduce-scatter.3.cloned.1.call-update) | async-done | bytes 147472 | tf_op jit(solution)/shard_map/reduce_scatter | solution.py:512
  351.3 1.6 convert_bitcast_fusion
  352.9 132.7 %all-reduce.4.cloned.1.call-done = (f32[196,384]{1,0:T(8,128)}, f32[384,196]{0,1:T(8,128)}) async-done(((f32[196,384]{1,0:T(8,128)}, f32[384,196]{0,1:T(8,128)}), (f32[196,384]{1,0:T(8,128)}, f32[384,196]{0,1:T(8,128)})) %all-reduce.4.cloned.1.call-update) | async-done | bytes 602128 | tf_op jit(solution)/shard_map/psum | solution.py:508
  485.7 1.7 copy.37
  487.4 1.7 copy.38
  (134 shorter events, 4.8 us)
Async XLA Ops:
  7.2 9.6 %copy-start.32 = (f32[192]{0:T(256)S(1)}, f32[192]{0:T(256)}, u32[]{:S(2)}) copy-start(f32[192]{0:T(256)} %param.16) | copy-start | bytes 2308
  7.2 240.0 %reduce-scatter.5.cloned.1.call-start = ((), (), s32[]{:S(2)}) async-start(), calls=%async_computation.3 | async-start | bytes 4866048 | tf_op jit(solution)/shard_map/reduce_scatter | solution.py:511
  7.2 1.8 copy-start
  9.0 4.2 copy-start.53
  9.0 4.7 copy-start.52
  9.0 7.8 %copy-start.1 = (bf16[28,196,192]{1,2,0:T(8,128)(2,1)S(1)}, bf16[28,196,192]{1,2,0:T(8,128)(2,1)}, u32[]{:S(2)}) copy-start(bf16[28,196,192]{1,2,0:T(8,128)(2,1)} %param.15) | copy-start | bytes 6322180
  9.0 7.8 %copy-start.33 = (f32[192]{0:T(256)S(1)}, f32[192]{0:T(256)}, u32[]{:S(2)}) copy-start(f32[192]{0:T(256)} %param.17) | copy-start | bytes 2308
  9.0 7.8 %copy-start.34 = (f32[196]{0:T(256)S(1)}, f32[196]{0:T(256)}, u32[]{:S(2)}) copy-start(f32[196]{0:T(256)} %param.21) | copy-start | bytes 2356
  10.7 3.0 collective-permute-start
  11.5 3.7 collective-permute-start.1
  12.7 4.0 collective-permute-start.2
  18.6 23.6 %copy-start.43 = (f32[768]{0:T(1024)S(1)}, f32[768]{0:T(1024)}, u32[]{:S(2)}) copy-start(f32[768]{0:T(1024)} %param.27) | copy-start | bytes 9220
  18.6 24.2 %copy-start.44 = (f32[768]{0:T(1024)S(1)}, f32[768]{0:T(1024)}, u32[]{:S(2)}) copy-start(f32[768]{0:T(1024)} %param.22) | copy-start | bytes 9220
  18.6 24.8 %copy-start.45 = (f32[768]{0:T(1024)S(1)}, f32[768]{0:T(1024)}, u32[]{:S(2)}) copy-start(f32[768]{0:T(1024)} %param.23) | copy-start | bytes 9220
  25.0 1.3 copy-start.15
  26.3 1.3 copy-start.17
  28.3 13.0 %collective-permute-start.6 = (bf16[7,56,384]{2,1,0:T(8,128)(2,1)S(1)}, bf16[7,56,384]{2,1,0:T(8,128)(2,1)S(1)}, u32[]{:S(2)}, u32[]{:S(2)}) collective-permute-start(bf16[7,56,384]{2,1,0:T(8,128)(2,1)S(1)} %get-tuple-element.73), channel_id=1, source_target_pairs={{0,1},{1,0},{2,3},{3,2},{4,5},{5,4},{6,7},{7,6},{8,9},{9,8},{10,11... | collective-permute-start | bytes 903176 | tf_op jit(solution)/shard_map/ppermute | solution.py:465
  28.7 15.4 %collective-permute-start.7 = (bf16[7,56,384]{2,1,0:T(8,128)(2,1)S(1)}, bf16[7,56,384]{2,1,0:T(8,128)(2,1)S(1)}, u32[]{:S(2)}, u32[]{:S(2)}) collective-permute-start(bf16[7,56,384]{2,1,0:T(8,128)(2,1)S(1)} %get-tuple-element.74), channel_id=1, source_target_pairs={{0,2},{1,3},{2,0},{3,1},{4,6},{5,7},{6,4},{7,5},{8,10},{9,11},{10,... | collective-permute-start | bytes 903176 | tf_op jit(solution)/shard_map/ppermute | solution.py:465
  29.7 14.8 %collective-permute-start.8 = (bf16[7,56,384]{2,1,0:T(8,128)(2,1)S(1)}, bf16[7,56,384]{2,1,0:T(8,128)(2,1)S(1)}, u32[]{:S(2)}, u32[]{:S(2)}) collective-permute-start(bf16[7,56,384]{2,1,0:T(8,128)(2,1)S(1)} %get-tuple-element.75), channel_id=1, source_target_pairs={{0,3},{1,2},{2,1},{3,0},{4,7},{5,6},{6,5},{7,4},{8,11},{9,10},{10,... | collective-permute-start | bytes 903176 | tf_op jit(solution)/shard_map/ppermute | solution.py:465
  36.8 1.3 copy-start.12
  38.1 1.3 copy-start.14
  40.1 41.7 %collective-permute-start.3 = (bf16[7,56,384]{2,1,0:T(8,128)(2,1)S(1)}, bf16[7,56,384]{2,1,0:T(8,128)(2,1)S(1)}, u32[]{:S(2)}, u32[]{:S(2)}) collective-permute-start(bf16[7,56,384]{2,1,0:T(8,128)(2,1)S(1)} %get-tuple-element.69), channel_id=1, source_target_pairs={{0,1},{1,0},{2,3},{3,2},{4,5},{5,4},{6,7},{7,6},{8,9},{9,8},{10,11... | collective-permute-start | bytes 903176 | tf_op jit(solution)/shard_map/ppermute | solution.py:465
  40.2 41.6 %collective-permute-start.4 = (bf16[7,56,384]{2,1,0:T(8,128)(2,1)S(1)}, bf16[7,56,384]{2,1,0:T(8,128)(2,1)S(1)}, u32[]{:S(2)}, u32[]{:S(2)}) collective-permute-start(bf16[7,56,384]{2,1,0:T(8,128)(2,1)S(1)} %get-tuple-element.70), channel_id=1, source_target_pairs={{0,2},{1,3},{2,0},{3,1},{4,6},{5,7},{6,4},{7,5},{8,10},{9,11},{10,... | collective-permute-start | bytes 903176 | tf_op jit(solution)/shard_map/ppermute | solution.py:465
  41.3 3.3 copy-start.35
  41.3 40.5 %collective-permute-start.5 = (bf16[7,56,384]{2,1,0:T(8,128)(2,1)S(1)}, bf16[7,56,384]{2,1,0:T(8,128)(2,1)S(1)}, u32[]{:S(2)}, u32[]{:S(2)}) collective-permute-start(bf16[7,56,384]{2,1,0:T(8,128)(2,1)S(1)} %get-tuple-element.71), channel_id=1, source_target_pairs={{0,3},{1,2},{2,1},{3,0},{4,7},{5,6},{6,5},{7,4},{8,11},{9,10},{10,... | collective-permute-start | bytes 903176 | tf_op jit(solution)/shard_map/ppermute | solution.py:465
  81.9 38.3 %slice-start = ((s8[4227072]{0:T(1024)(128)(4,1)}), s8[4194304]{0:T(1024)(128)(4,1)S(1)}, s32[]{:S(2)}) async-start(s8[4227072]{0:T(1024)(128)(4,1)} %bitcast.30), calls=%async_computation.5 | async-start | bytes 8388608
  82.7 37.5 %slice-start.1 = ((s8[4227072]{0:T(1024)(128)(4,1)}), s8[32768]{0:T(1024)(128)(4,1)S(1)}, s32[]{:S(2)}) async-start(s8[4227072]{0:T(1024)(128)(4,1)} %bitcast.30), calls=%async_computation.6 | async-start | bytes 65536
  82.7 37.5 %copy-start.19 = (bf16[688,768]{1,0:T(8,128)(2,1)S(1)}, bf16[688,768]{1,0:T(8,128)(2,1)}, u32[]{:S(2)}) copy-start(bf16[688,768]{1,0:T(8,128)(2,1)} %get-tuple-element.118.b0) | copy-start | bytes 3170308
  120.2 2.2 copy-start.5
  133.6 1.2 copy-start.18
  133.6 1.5 copy-start.20
  133.6 217.7 %reduce-scatter.3.cloned.1.call-start = ((), (), s32[]{:S(2)}) async-start(), calls=%async_computation.2 | async-start | bytes 4866048 | tf_op jit(solution)/shard_map/reduce_scatter | solution.py:512
  135.2 2.2 copy-start.3
  137.4 2.2 copy-start.4
  149.5 16.7 %copy-start.9 = (bf16[196,384]{1,0:T(8,128)(2,1)S(1)}, bf16[196,384]{1,0:T(8,128)(2,1)}, u32[]{:S(2)}) copy-start(bf16[196,384]{1,0:T(8,128)(2,1)} %w_in.7) | copy-start | bytes 451588
  149.5 16.7 %copy-start.11 = (bf16[384,196]{0,1:T(8,128)(2,1)S(1)}, bf16[384,196]{0,1:T(8,128)(2,1)}, u32[]{:S(2)}) copy-start(bf16[384,196]{0,1:T(8,128)(2,1)} %param.20) | copy-start | bytes 451588
  149.5 16.7 %copy-start.16 = (bf16[2688,384]{1,0:T(8,128)(2,1)S(1)}, bf16[2688,384]{1,0:T(8,128)(2,1)}, u32[]{:S(2)}) copy-start(bf16[2688,384]{1,0:T(8,128)(2,1)} %copy-done.15) | copy-start | bytes 6193156
  149.5 16.7 %copy-start.25 = (bf16[7,56,384]{2,1,0:T(8,128)(2,1)S(1)}, bf16[7,56,384]{2,1,0:T(8,128)(2,1)}, u32[]{:S(2)}) copy-start(bf16[7,56,384]{2,1,0:T(8,128)(2,1)} %get-tuple-element.84.p0) | copy-start | bytes 903172
  149.5 336.2 %all-reduce.4.cloned.1.call-start = ((), (), s32[]{:S(2)}) async-start(), calls=%async_computation.4 | async-start | bytes 1228800 | tf_op jit(solution)/shard_map/psum | solution.py:508
  149.5 3.4 collective-permute-start.12
  149.6 8.7 %collective-permute-start.13 = (bf16[7,56,384]{2,1,0:T(8,128)(2,1)}, bf16[7,56,384]{2,1,0:T(8,128)(2,1)}, u32[]{:S(2)}, u32[]{:S(2)}) collective-permute-start(bf16[7,56,384]{2,1,0:T(8,128)(2,1)} %get-tuple-element.86), channel_id=1, source_target_pairs={{0,2},{1,3},{2,0},{3,1},{4,6},{5,7},{6,4},{7,5},{8,10},{9,11},{10,... | collective-permute-start | bytes 903176 | tf_op jit(solution)/shard_map/ppermute | solution.py:465
  150.9 15.3 %collective-permute-start.14 = (bf16[7,56,384]{2,1,0:T(8,128)(2,1)}, bf16[7,56,384]{2,1,0:T(8,128)(2,1)}, u32[]{:S(2)}, u32[]{:S(2)}) collective-permute-start(bf16[7,56,384]{2,1,0:T(8,128)(2,1)} %get-tuple-element.87), channel_id=1, source_target_pairs={{0,3},{1,2},{2,1},{3,0},{4,7},{5,6},{6,5},{7,4},{8,11},{9,10},{10,... | collective-permute-start | bytes 903176 | tf_op jit(solution)/shard_map/ppermute | solution.py:465
  151.7 26.7 %collective-permute-start.9 = (bf16[7,56,384]{2,1,0:T(8,128)(2,1)}, bf16[7,56,384]{2,1,0:T(8,128)(2,1)S(1)}, u32[]{:S(2)}, u32[]{:S(2)}) collective-permute-start(bf16[7,56,384]{2,1,0:T(8,128)(2,1)} %get-tuple-element.79), channel_id=1, source_target_pairs={{0,1},{1,0},{2,3},{3,2},{4,5},{5,4},{6,7},{7,6},{8,9},{9,8},{10,11... | collective-permute-start | bytes 903176 | tf_op jit(solution)/shard_map/ppermute | solution.py:465
  151.8 27.4 %collective-permute-start.10 = (bf16[7,56,384]{2,1,0:T(8,128)(2,1)}, bf16[7,56,384]{2,1,0:T(8,128)(2,1)}, u32[]{:S(2)}, u32[]{:S(2)}) collective-permute-start(bf16[7,56,384]{2,1,0:T(8,128)(2,1)} %get-tuple-element.80), channel_id=1, source_target_pairs={{0,2},{1,3},{2,0},{3,1},{4,6},{5,7},{6,4},{7,5},{8,10},{9,11},{10,... | collective-permute-start | bytes 903176 | tf_op jit(solution)/shard_map/ppermute | solution.py:465
  153.7 25.5 %collective-permute-start.11 = (bf16[7,56,384]{2,1,0:T(8,128)(2,1)}, bf16[7,56,384]{2,1,0:T(8,128)(2,1)}, u32[]{:S(2)}, u32[]{:S(2)}) collective-permute-start(bf16[7,56,384]{2,1,0:T(8,128)(2,1)} %get-tuple-element.81), channel_id=1, source_target_pairs={{0,3},{1,2},{2,1},{3,0},{4,7},{5,6},{6,5},{7,4},{8,11},{9,10},{10,... | collective-permute-start | bytes 903176 | tf_op jit(solution)/shard_map/ppermute | solution.py:465
  167.2 11.2 %copy-start.46 = (f32[1,768]{1,0:T(1,128)S(1)}, f32[1,768]{1,0:T(1,128)}, u32[]{:S(2)}) copy-start(f32[1,768]{1,0:T(1,128)} %get-tuple-element.108) | copy-start | bytes 9220
  167.2 11.2 %copy-start.47 = (f32[1,768]{1,0:T(1,128)S(1)}, f32[1,768]{1,0:T(1,128)}, u32[]{:S(2)}) copy-start(f32[1,768]{1,0:T(1,128)} %get-tuple-element.120) | copy-start | bytes 9220
  167.2 11.2 %copy-start.48 = (f32[1,768]{1,0:T(1,128)S(1)}, f32[1,768]{1,0:T(1,128)}, u32[]{:S(2)}) copy-start(f32[1,768]{1,0:T(1,128)} %get-tuple-element.109) | copy-start | bytes 9220
  167.2 11.2 %copy-start.49 = (f32[1,768]{1,0:T(1,128)S(1)}, f32[1,768]{1,0:T(1,128)}, u32[]{:S(2)}) copy-start(f32[1,768]{1,0:T(1,128)} %get-tuple-element.121) | copy-start | bytes 9220
  167.2 12.0 %copy-start.13 = (bf16[2688,384]{1,0:T(8,128)(2,1)S(1)}, bf16[2688,384]{1,0:T(8,128)(2,1)}, u32[]{:S(2)}) copy-start(bf16[2688,384]{1,0:T(8,128)(2,1)} %copy-done.12) | copy-start | bytes 6193156
  167.2 12.0 %copy-start.24 = (bf16[7,56,384]{2,1,0:T(8,128)(2,1)S(1)}, bf16[7,56,384]{2,1,0:T(8,128)(2,1)}, u32[]{:S(2)}) copy-start(bf16[7,56,384]{2,1,0:T(8,128)(2,1)} %get-tuple-element.78.p0) | copy-start | bytes 903172
  178.3 19.3 %collective-permute-start.18 = (f32[2,14,196]{2,1,0:T(8,128)S(1)}, f32[2,14,196]{2,1,0:T(8,128)S(1)}, u32[]{:S(2)}, u32[]{:S(2)}) collective-permute-start(f32[2,14,196]{2,1,0:T(8,128)S(1)} %get-tuple-element.98.s0), channel_id=1, source_target_pairs={{0,1},{1,0},{2,3},{3,2},{4,5},{5,4},{6,7},{7,6},{8,9},{9,8},{10,11... | collective-permute-start | bytes 65864 | tf_op jit(solution)/shard_map/ppermute | solution.py:461
  180.1 18.1 %copy-start.50 = (f32[1,768]{1,0:T(1,128)S(1)}, f32[1,768]{1,0:T(1,128)}, u32[]{:S(2)}) copy-start(f32[1,768]{1,0:T(1,128)} %get-tuple-element.106) | copy-start | bytes 9220
  180.1 18.1 %copy-start.51 = (f32[1,768]{1,0:T(1,128)S(1)}, f32[1,768]{1,0:T(1,128)}, u32[]{:S(2)}) copy-start(f32[1,768]{1,0:T(1,128)} %get-tuple-element.107) | copy-start | bytes 9220
  180.1 18.2 %copy-start.41 = (f32[1,3072]{1,0:T(1,128)S(1)}, f32[1,3072]{1,0:T(1,128)}, u32[]{:S(2)}) copy-start(f32[1,3072]{1,0:T(1,128)} %get-tuple-element.114) | copy-start | bytes 36868
  180.2 18.2 %copy-start.42 = (f32[1,3072]{1,0:T(1,128)S(1)}, f32[1,3072]{1,0:T(1,128)}, u32[]{:S(2)}) copy-start(f32[1,3072]{1,0:T(1,128)} %get-tuple-element.115) | copy-start | bytes 36868
  180.2 60.6 %copy-start.2 = (bf16[28,196,192]{1,2,0:T(8,128)(2,1)S(1)}, bf16[28,196,192]{1,2,0:T(8,128)(2,1)}, u32[]{:S(2)}) copy-start(bf16[28,196,192]{1,2,0:T(8,128)(2,1)} %param.15) | copy-start | bytes 6322180
  192.5 52.4 %collective-permute-start.15 = (f32[2,14,196]{2,1,0:T(8,128)S(1)}, f32[2,14,196]{2,1,0:T(8,128)S(1)}, u32[]{:S(2)}, u32[]{:S(2)}) collective-permute-start(f32[2,14,196]{2,1,0:T(8,128)S(1)} %get-tuple-element.96.s0), channel_id=1, source_target_pairs={{0,1},{1,0},{2,3},{3,2},{4,5},{5,4},{6,7},{7,6},{8,9},{9,8},{10,11... | collective-permute-start | bytes 65864 | tf_op jit(solution)/shard_map/ppermute | solution.py:461
  192.9 51.9 %collective-permute-start.16 = (f32[2,14,196]{2,1,0:T(8,128)S(1)}, f32[2,14,196]{2,1,0:T(8,128)S(1)}, u32[]{:S(2)}, u32[]{:S(2)}) collective-permute-start(f32[2,14,196]{2,1,0:T(8,128)S(1)} %get-tuple-element.96.s0), channel_id=1, source_target_pairs={{0,2},{1,3},{2,0},{3,1},{4,6},{5,7},{6,4},{7,5},{8,10},{9,11},{10,... | collective-permute-start | bytes 65864 | tf_op jit(solution)/shard_map/ppermute | solution.py:461
  194.1 50.7 %collective-permute-start.17 = (f32[2,14,196]{2,1,0:T(8,128)S(1)}, f32[2,14,196]{2,1,0:T(8,128)S(1)}, u32[]{:S(2)}, u32[]{:S(2)}) collective-permute-start(f32[2,14,196]{2,1,0:T(8,128)S(1)} %get-tuple-element.96.s0), channel_id=1, source_target_pairs={{0,3},{1,2},{2,1},{3,0},{4,7},{5,6},{6,5},{7,4},{8,11},{9,10},{10,... | collective-permute-start | bytes 65864 | tf_op jit(solution)/shard_map/ppermute | solution.py:461
  194.6 46.2 %collective-permute-start.19 = (f32[2,14,196]{2,1,0:T(8,128)S(1)}, f32[2,14,196]{2,1,0:T(8,128)S(1)}, u32[]{:S(2)}, u32[]{:S(2)}) collective-permute-start(f32[2,14,196]{2,1,0:T(8,128)S(1)} %get-tuple-element.98.s0), channel_id=1, source_target_pairs={{0,2},{1,3},{2,0},{3,1},{4,6},{5,7},{6,4},{7,5},{8,10},{9,11},{10,... | collective-permute-start | bytes 65864 | tf_op jit(solution)/shard_map/ppermute | solution.py:461
  197.6 43.2 %collective-permute-start.20 = (f32[2,14,196]{2,1,0:T(8,128)S(1)}, f32[2,14,196]{2,1,0:T(8,128)S(1)}, u32[]{:S(2)}, u32[]{:S(2)}) collective-permute-start(f32[2,14,196]{2,1,0:T(8,128)S(1)} %get-tuple-element.98.s0), channel_id=1, source_target_pairs={{0,3},{1,2},{2,1},{3,0},{4,7},{5,6},{6,5},{7,4},{8,11},{9,10},{10,... | collective-permute-start | bytes 65864 | tf_op jit(solution)/shard_map/ppermute | solution.py:461
  240.8 1.8 copy-start.6
  242.6 2.3 copy-start.7
  (16 other events, 13.2 us)
Sparse Core Ops, SparseCore 0:
  133.8 104.9 reduce-scatter.4
  245.2 106.0 reduce-scatter.2
  357.2 128.4 all-reduce.3

commit v2 on v1

v2 whole, which is shorter than its diff:
```python
import functools

import jax
import jax.numpy as jnp
from jax import lax
from jax.experimental import pallas as pl
from jax.experimental.pallas import tpu as pltpu
from jax.sharding import PartitionSpec as P

F32, BF16 = jnp.float32, jnp.bfloat16
EPS = 1e-6
RSQRT2 = 0.7071067811865476
RSQRT2PI = 0.3989422804014327
LIMIT = 60 * 2**20
ANY = pl.BlockSpec(memory_space=pl.ANY)
SMEM = pl.BlockSpec(memory_space=pltpu.SMEM)


def nn(a, b):
    return jnp.dot(a, b, preferred_element_type=F32)


def nt(a, b):
    return lax.dot_general(a, b, (((1,), (1,)), ((), ())), preferred_element_type=F32)


def tn(a, b):
    return lax.dot_general(a, b, (((0,), (0,)), ((), ())), preferred_element_type=F32)


def gelu_pair(x):
    half = 0.5 + 0.5 * lax.erf(x * RSQRT2)
    return x * half, half + x * (RSQRT2PI * jnp.exp(-0.5 * (x * x)))


def shape(dims, dtype=F32):
    return jax.ShapeDtypeStruct(dims, dtype)


def cost(weight):
    return pl.CostEstimate(flops=10**11 * weight + 1, bytes_accessed=1, transcendentals=0)


def whole(dims):
    zeros = (0,) * len(dims)
    return pl.BlockSpec(dims, lambda i: zeros)


def at(dims, first):
    rest = (0,) * (len(dims) - 1)
    return pl.BlockSpec(dims, lambda i: (first,) + rest)


def column(row, size):
    r = lax.broadcasted_iota(jnp.int32, (size, size), 0)
    c = lax.broadcasted_iota(jnp.int32, (size, size), 1)
    return jnp.sum(jnp.where(r == c, jnp.broadcast_to(row, (size, size)), 0.0), 1, keepdims=True)


def stats_kernel(tok, out):
    images, width, _ = tok.shape
    first = pl.program_id(0) * images
    for b in range(images):
        x = tok[b].astype(F32)
        m = jnp.sum(x, 0, keepdims=True) * (1.0 / width)
        o = x - m
        out[0, pl.ds(first + b, 1), :] = m
        out[1, pl.ds(first + b, 1), :] = jnp.sum(o * o, 0, keepdims=True)


def stats_call(tok, steps=4):
    images, width, patches = tok.shape
    return pl.pallas_call(
        stats_kernel,
        grid=(steps,),
        in_specs=[pl.BlockSpec((images // steps, width, patches), lambda i: (i, 0, 0))],
        out_specs=whole((2, images, patches)),
        out_shape=shape((2, images, patches)),
        compiler_params=pltpu.CompilerParams(vmem_limit_bytes=LIMIT),
        cost_estimate=cost(0),
        name="stats",
    )(tok)


def join_stats(stats, mr, width):
    m = 0.25 * ((stats[0][0] + stats[1][0]) + (stats[2][0] + stats[3][0]))
    q = jnp.zeros_like(m)
    for s in stats:
        o = s[0] - m
        q = q + (s[1] + width * (o * o))
    mr[0] = m
    mr[1] = lax.rsqrt(q * (1.0 / (4 * width)) + EPS)


def spread_rows(dst, src, P_, PP):
    for j in range(4):
        dst[pl.ds(j * PP, P_), :] = src[pl.ds(j * P_, P_), :].astype(F32)


def picker(rows, columns, P_, PP):
    r = lax.broadcasted_iota(jnp.int32, (rows, columns), 0)
    c = lax.broadcasted_iota(jnp.int32, (rows, columns), 1)
    pick = jnp.zeros((rows, columns), F32)
    for j in range(4):
        inside = jnp.logical_and(r >= j * PP, r < j * PP + P_)
        pick = jnp.where(jnp.logical_and(inside, c == r - j * (PP - P_)), 1.0, pick)
    return pick.astype(BF16)


def token_kernel(me, keep, t0, t1, t2, t3, tok, w_in, b_in, w_outT, b_out, g1, c1,
                 act, gp, s0, s1, s2, s3, mr, left, wide, biasb, gcol, mix, rhs, buf, *, first, P_, PP):
    _, width, S = tok.shape
    K = w_in.shape[1]
    p = pl.program_id(0)

    @pl.when(p == 0)
    def _():
        join_stats((t0, t1, t2, t3), mr, width)
        gcol[0] = jnp.broadcast_to(column(g1[...], width), (width, S))
        gcol[1] = jnp.broadcast_to(column(c1[...], width), (width, S))
        wide[...] = jnp.zeros_like(wide)
        spread_rows(wide, w_outT, P_, PP)
        left[:, 0:K] = wide[...].astype(BF16)
        left[:, K:] = picker(4 * PP, left.shape[1] - K, P_, PP)
        biasb[...] = jnp.zeros_like(biasb)
        bcol = jnp.broadcast_to(column(b_out[...], S), (S, biasb.shape[1]))
        for j in range(4):
            biasb[pl.ds(j * PP, P_), :] = bcol[j * P_:(j + 1) * P_, :]
        rhs[...] = jnp.zeros_like(rhs)

    for i in range(2):
        b = first + 2 * p + i
        raw = tok[i]
        m = mr[0, pl.ds(b, 1), :]
        r = mr[1, pl.ds(b, 1), :]
        mix[pl.ds(i * width, width), :] = (((raw.astype(F32) - m) * r) * gcol[0] + gcol[1]).astype(BF16)
        rhs[pl.ds(i * width, width), K:K + S] = raw
    g, d = gelu_pair(nn(mix[...], w_in[...]) + b_in[...])
    k0, k1 = keep[first + 2 * p], keep[first + 2 * p + 1]
    rows = lax.broadcasted_iota(jnp.int32, (2 * width, 1), 0)
    a = (g * jnp.where(rows < width, k0, k1)).astype(BF16)
    rhs[:, 0:K] = a
    act[...] = a
    gp[...] = d.astype(BF16)
    lanes = lax.broadcasted_iota(jnp.int32, (1, 2 * width), 1)
    out = nt(left[...], rhs[...]) + biasb[...] * jnp.where(lanes < width, k0, k1)
    for j in range(4):
        buf[j] = out[j * PP:(j + 1) * PP, :].astype(BF16)
    for k, o in enumerate((s0, s1, s2, s3)):
        o[0] = buf[me[1] ^ k]


def token_call(ids, keep, stats, tok, w_in, b_in, w_outT, b_out, g1, c1, half, P_, PP):
    images, width, S = tok.shape
    nb = images // 2
    K = w_in.shape[1]
    piece = shape((nb // 2, PP, 2 * width), BF16)
    rows = pl.BlockSpec((2 * width, K), lambda i: (i, 0))
    send = pl.BlockSpec((1, PP, 2 * width), lambda i: (i, 0, 0))
    return pl.pallas_call(
        functools.partial(token_kernel, first=half * nb, P_=P_, PP=PP),
        grid=(nb // 2,),
        in_specs=[SMEM, SMEM] + [whole(stats[0].shape)] * 4
                 + [pl.BlockSpec((2, width, S), lambda i: (half * (nb // 2) + i, 0, 0)), whole(w_in.shape), whole(b_in.shape),
                    whole(w_outT.shape), whole(b_out.shape), whole(g1.shape), whole(c1.shape)],
        out_specs=[rows, rows, send, send, send, send],
        out_shape=[shape((nb * width, K), BF16), shape((nb * width, K), BF16), piece, piece, piece, piece],
        scratch_shapes=[pltpu.VMEM((2, images, S), F32), pltpu.VMEM((4 * PP, K + 256), BF16), pltpu.VMEM((4 * PP, K), F32),
                        pltpu.VMEM((4 * PP, 2 * width), F32), pltpu.VMEM((2, width, S), F32), pltpu.VMEM((2 * width, S), BF16),
                        pltpu.VMEM((2 * width, K + 256), BF16), pltpu.VMEM((4, PP, 2 * width), BF16)],
        compiler_params=pltpu.CompilerParams(vmem_limit_bytes=LIMIT),
        cost_estimate=cost(half),
        name="token_forward",
    )(ids, keep, *stats, tok, w_in, b_in, w_outT, b_out, g1, c1)


def upstream_kernel(keep, cot, og, b4, packed, *, P_):
    nb = cot.shape[0]
    rows = nb * P_
    half = pl.program_id(0)

    @pl.when(half == 0)
    def _():
        b4[...] = jnp.zeros_like(b4)
        packed[pl.ds(rows, packed.shape[0] - rows), :] = jnp.zeros((packed.shape[0] - rows, packed.shape[1]), F32)

    for b in range(nb):
        packed[pl.ds(b * P_, P_), :] = cot[b].astype(F32) * keep[half * nb + b]
    v = packed[...]
    og[0] = v.astype(BF16)
    b4[...] += jnp.sum(v, 0, keepdims=True)


def upstream_call(keep, cot, R):
    images, P_, W = cot.shape
    return pl.pallas_call(
        functools.partial(upstream_kernel, P_=P_),
        grid=(2,),
        in_specs=[SMEM, pl.BlockSpec((images // 2, P_, W), lambda i: (i, 0, 0))],
        out_specs=[pl.BlockSpec((1, R, W), lambda i: (i, 0, 0)), whole((1, W))],
        out_shape=[shape((2, R, W), BF16), shape((1, W))],
        scratch_shapes=[pltpu.VMEM((R, W), F32)],
        compiler_params=pltpu.CompilerParams(vmem_limit_bytes=LIMIT),
        cost_estimate=cost(0),
        name="upstream",
    )(keep, cot)


def chan_kernel(*refs, nb, P_, R, half, dp, blk):
    (ids, keep2, p0, p1, p2, p3, cot, og, w1, w2, b1, b2, g2, c2), refs = refs[:14], refs[14:]
    if half:
        (before4, before3, _, keep4, send4, keep3, send3), refs = refs[:7], refs[7:]
    else:
        (grad4, grad3), refs = refs[:2], refs[2:]
    (b3, out, s0, s1, s2, s3, gg, gc, x, nrm, r2s, acc_o, acc_i, bufi, bufo, ct, ct_sem), refs = refs[:17], refs[17:]
    step = pl.program_id(0)
    last = pl.num_programs(0) - 1
    W = x.shape[1]
    fb = w1.shape[1]
    q = W // 4
    PP = bufi.shape[2]
    load_ct = pltpu.make_async_copy(cot.at[pl.ds(half * nb, nb)], ct, ct_sem)
    if half:
        old4, old3, old_sem = refs
        here = pl.ds(step * fb, fb)
        load4 = pltpu.make_async_copy(before4.at[here], old4, old_sem.at[0])
        load3 = pltpu.make_async_copy(before3.at[here], old3, old_sem.at[1])
        load4.start()
        load3.start()

    @pl.when(step == 0)
    def _():
        load_ct.start()
        for k, p in enumerate((p0, p1, p2, p3)):
            bufi[ids[1] ^ k] = p[...]
        for b in range(nb):
            lo = (b % 2) * q
            v = jnp.concatenate([bufi[j, b // 2][:, lo:lo + q].astype(F32) for j in range(4)], axis=1)
            o = v - jnp.mean(v, 1, keepdims=True)
            rr = lax.rsqrt(jnp.mean(o * o, 1, keepdims=True) + EPS)
            n = o * rr
            nrm[b] = n
            r2s[b] = jnp.broadcast_to(rr, (PP, 128))
            acc_i[pl.ds(b * P_, PP), :] = n * g2[...] + c2[...]
        x[...] = acc_i[0:R, :].astype(BF16)
        acc_i[...] = jnp.zeros_like(acc_i)
        acc_o[...] = jnp.broadcast_to(b2[...], acc_o.shape)

    g, gp = gelu_pair(nn(x[...], w1[...]) + b1[...])
    a = g.astype(BF16)
    d = (nt(og[0], w2[...]) * gp).astype(BF16)
    b3[...] = jnp.sum(d.astype(F32), 0, keepdims=True)
    acc_o[...] += nn(a, w2[...])
    acc_i[0:R, :] += nt(d, w1[...])
    if half:
        load4.wait()
        load3.wait()
        core = ids[1] & 1
        per = fb // (4 * blk)
        for total, mine, other in ((tn(a, og[0]) + old4[...], keep4, send4), (tn(d, x[...]) + old3[...], keep3, send3)):
            for i in range(per):
                for y in range(2):
                    lo = total[(i * 4 + y * 2) * blk:(i * 4 + y * 2 + 1) * blk].astype(BF16)
                    hi = total[(i * 4 + y * 2 + 1) * blk:(i * 4 + y * 2 + 2) * blk].astype(BF16)
                    at_ = (i ^ (ids[0] & (per - 1)), y ^ (ids[1] >> 1))

                    @pl.when(core == 0)
                    def _(at_=at_, lo=lo, hi=hi, mine=mine, other=other):
                        mine[at_] = lo
                        other[at_] = hi

                    @pl.when(core == 1)
                    def _(at_=at_, lo=lo, hi=hi, mine=mine, other=other):
                        mine[at_] = hi
                        other[at_] = lo
    else:
        grad4[...] = tn(a, og[0])
        grad3[...] = tn(d, x[...])

    @pl.when(step == last)
    def _():
        load_ct.wait()
        gc[...] = jnp.sum(acc_i[0:R, :], 0, keepdims=True)
        total = jnp.zeros((1, W), F32)
        for p in range(nb // 2):
            pair = []
            for b in (2 * p, 2 * p + 1):
                rows = pl.ds(b * P_, P_)
                lo = (b % 2) * q
                v = jnp.concatenate([bufi[j, p][0:P_, lo:lo + q].astype(F32) for j in range(4)], axis=1)
                out[b] = (v + keep2[half * nb + b] * acc_o[rows, :]).astype(BF16)
                e = acc_i[rows, :]
                n = nrm[b, 0:P_, :]
                total = total + jnp.sum(e * n, 0, keepdims=True)
                e = e * g2[...]
                m1 = jnp.mean(e, 1, keepdims=True)
                m2 = jnp.mean(e * n, 1, keepdims=True)
                pair.append(ct[b].astype(F32) + r2s[b, 0:P_, 0:1] * (e - m1 - n * m2))
            for j in range(4):
                bufo[j, p, 0:P_, :] = jnp.concatenate([v[:, j * q:(j + 1) * q] for v in pair], axis=1).astype(BF16)
                bufo[j, p, P_:, :] = jnp.zeros((PP - P_, 2 * q), BF16)
        gg[...] = total
        for k, o in enumerate((s0, s1, s2, s3)):
            o[...] = bufo[ids[1] ^ k]


def chan_call(ids, keep2, pieces, cot, og, half, w1, w2, b1, b2, g2, c2, before, dp, fb=768):
    images, P_, W = cot.shape
    nb = images // 2
    R = og.shape[1]
    F = w1.shape[1]
    blk = F // (dp * 4)
    per = fb // (4 * blk)
    line = pl.BlockSpec((1, fb), lambda i, ids: (0, i))
    pin = lambda dims: pl.BlockSpec(dims, lambda i, ids: (0,) * len(dims))
    smem = pl.BlockSpec(memory_space=pltpu.SMEM)
    piece = pieces[0].shape
    placed = pl.BlockSpec((per, 2, blk, W), lambda i, ids: (dp_place(i * per ^ ids[0], dp) // per, 0, 0, 0))
    in_specs = [smem] + [pin(piece)] * 4 + [ANY, pl.BlockSpec((1, R, W), lambda i, ids: (half, 0, 0)),
                pl.BlockSpec((W, fb), lambda i, ids: (0, i)), pl.BlockSpec((fb, W), lambda i, ids: (i, 0)),
                line, pin((1, W)), pin((1, W)), pin((1, W))]
    args = [ids, keep2, *pieces, cot, og, w1, w2, b1, b2, g2, c2]
    if half:
        in_specs += [ANY, ANY, ANY]
        args += list(before)
        grads, grad_specs = [shape((dp, 2, blk, W), BF16)] * 4, [placed] * 4
        scratch = [pltpu.VMEM((fb, W), F32), pltpu.VMEM((fb, W), F32), pltpu.SemaphoreType.DMA((2,))]
    else:
        grads, grad_specs = [shape((F, W))] * 2, [pl.BlockSpec((fb, W), lambda i, ids: (i, 0))] * 2
        scratch = []
    n = len(grads)
    return pl.pallas_call(
        functools.partial(chan_kernel, nb=nb, P_=P_, R=R, half=half, dp=dp, blk=blk),
        grid_spec=pltpu.PrefetchScalarGridSpec(
            num_scalar_prefetch=1, grid=(F // fb,), in_specs=in_specs,
            out_specs=grad_specs + [line, pl.BlockSpec((nb, P_, W), lambda i, ids: (half, 0, 0))] + [pin(piece)] * 4
                      + [pin((1, W)), pin((1, W))],
            scratch_shapes=[pltpu.VMEM((R, W), BF16), pltpu.VMEM((nb, piece[1], W), F32), pltpu.VMEM((nb, piece[1], 128), F32),
                            pltpu.VMEM((R, W), F32), pltpu.VMEM((R + 8, W), F32), pltpu.VMEM((4,) + piece, BF16),
                            pltpu.VMEM((4,) + piece, BF16), pltpu.VMEM((nb, P_, W), BF16), pltpu.SemaphoreType.DMA] + scratch),
        out_shape=grads + [shape((1, F)), shape(cot.shape, BF16)] + [shape(piece, BF16)] * 4 + [shape((1, W)), shape((1, W))],
        input_output_aliases={16: n + 1} if half else {},
        compiler_params=pltpu.CompilerParams(vmem_limit_bytes=LIMIT),
        cost_estimate=cost(1),
        name="channel_mlp",
    )(*args)


def as_row(col, size):
    r = lax.broadcasted_iota(jnp.int32, (size, size), 0)
    c = lax.broadcasted_iota(jnp.int32, (size, size), 1)
    return jnp.sum(jnp.where(r == c, jnp.broadcast_to(col, (size, size)), 0.0), 0, keepdims=True)


VEC = 8


def split_rows(dst, at_, v):
    hi = v.astype(BF16).astype(F32)
    dst[pl.ds(at_, VEC), :] = hi
    dst[pl.ds(at_ + VEC, VEC), :] = v - hi


def back_kernel(ids, keep, t0, t1, t2, t3, p0, p1, p2, p3, act, gp, tok, w_in, w_outT, g1, c1, *rest, half, P_, PP):
    if half:
        before, vecs, _, rest = rest[:7], rest[7:14], rest[14], rest[15:]
        u, o0, o1, o2, o3, ps, gw1, gw2, vec, stage, quarters = rest[:11]
        rest = rest[11:]
    else:
        (u, ps, gw1, gw2, ob1, ob2, og, oc), rest = rest[:8], rest[8:]
    mr, right, wide, gcol, mix, buf, gb1, gb2, gg, gc = rest
    _, width, S = tok.shape
    K = w_in.shape[1]
    p = pl.program_id(0)
    first = half * 2 * pl.num_programs(0)

    @pl.when(p == 0)
    def _():
        join_stats((t0, t1, t2, t3), mr, width)
        gcol[0] = jnp.broadcast_to(column(g1[...], width), (width, S))
        gcol[1] = jnp.broadcast_to(column(c1[...], width), (width, S))
        wide[...] = jnp.zeros_like(wide)
        spread_rows(wide, w_outT, P_, PP)
        right[:, 0:K] = wide[...].astype(BF16)
        right[:, K:] = picker(4 * PP, right.shape[1] - K, P_, PP)
        for o in (gb1, gb2, gg, gc):
            o[...] = jnp.zeros_like(o)
        if half:
            gw1[...] = before[0][...]
            gw2[...] = before[1][...]
            ps[...] = before[6][...]
        else:
            for o in (gw1, gw2, ps):
                o[...] = jnp.zeros_like(o)

    for k, o in enumerate((p0, p1, p2, p3)):
        buf[ids[1] ^ k] = o[0]
    sg = buf[...].reshape(4 * PP, 2 * width)
    k0, k1 = keep[first + 2 * p], keep[first + 2 * p + 1]
    lanes = lax.broadcasted_iota(jnp.int32, (1, 2 * width), 1)
    gb2[...] += sg.astype(F32) * jnp.where(lanes < width, k0, k1)
    both = tn(sg, right[...])
    rows = lax.broadcasted_iota(jnp.int32, (2 * width, 1), 0)
    pre1 = ((both[:, 0:K] * gp[...].astype(F32)) * jnp.where(rows < width, k0, k1)).astype(BF16)
    gb1[...] += jnp.sum(pre1.astype(F32).reshape(2 * width // 8, 8, K), 0)
    gw2[...] += nn(sg, act[...])
    ng = nt(pre1, w_in[...])
    for i in range(2):
        b = first + 2 * p + i
        part = slice(i * width, (i + 1) * width)
        m = mr[0, pl.ds(b, 1), :]
        r = mr[1, pl.ds(b, 1), :]
        n = (tok[i].astype(F32) - m) * r
        mix[pl.ds(i * width, width), :] = (n * gcol[0] + gcol[1]).astype(BF16)
        v = ng[part, :]
        gg[...] += v * n
        gc[...] += v
        e = v * gcol[0]
        ps[0, pl.ds(b, 1), :] = jnp.sum(e, 0, keepdims=True)
        ps[1, pl.ds(b, 1), :] = jnp.sum(e * n, 0, keepdims=True)
        u[i] = both[part, K:K + S] + r * e
    gw1[...] += tn(mix[...], pre1)

    @pl.when(p == pl.num_programs(0) - 1)
    def _():
        sums = [jnp.sum(gb1[...], 0, keepdims=True),
                as_row(jnp.sum(gb2[...], 1, keepdims=True), 4 * PP),
                as_row(jnp.sum(gg[...], 1, keepdims=True), width),
                as_row(jnp.sum(gc[...], 1, keepdims=True), width)]
        if not half:
            for v, o in zip(sums, (ob1, ob2, og, oc)):
                o[...] = v
            return
        sums = [v + q[...] for v, q in zip(sums, before[2:6])]
        chan = ids[1]
        vec[...] = jnp.zeros_like(vec)
        row = 0
        for v in (vecs[0][...] + vecs[1][...], vecs[2][...] + vecs[3][...], vecs[4][...] + vecs[5][...], vecs[6][...]):
            for r in range(v.shape[1] // K):
                vec[row:row + 1, :] = v[:, r * K:(r + 1) * K]
                row += 1
        vec[row:row + 1, :] = sums[0]
        vec[row + 1:row + 2, 0:4 * PP] = sums[1]
        row += 2
        mine = jnp.logical_and(lanes >= (chan & 1) * width, lanes < (chan & 1) * width + width)
        for v in sums[2:]:
            twice = jnp.concatenate([v, v], axis=1)
            for r in range(2):
                vec[row:row + 1, :] = jnp.where(jnp.logical_and(mine, (chan >> 1) == r), twice, 0.0)
                row += 1
        stage[...] = jnp.zeros_like(stage)
        for j in range(4):
            stage[0:P_, :] = gw1[j * P_:(j + 1) * P_, :]
            stage[PP:2 * PP, :] = gw2[j * PP:(j + 1) * PP, :]
            split_rows(stage, 2 * PP, vec[j * VEC:(j + 1) * VEC, :])
            for i in range(2):
                stage[pl.ds(2 * PP + 2 * VEC + i * ps.shape[1], ps.shape[1]), 0:S] = ps[i]
            quarters[j] = stage[...].astype(BF16)
        for k, o in enumerate((o0, o1, o2, o3)):
            o[...] = quarters[chan ^ k]


def back_call(ids, keep, stats, pieces, act, gp, tok, w_in, w_outT, g1, c1, half, P_, PP, before, vecs, u_before):
    images, width, S = tok.shape
    nb = images // 2
    K = w_in.shape[1]
    sums = [(S, K), (4 * PP, K), (1, K), (1, 4 * PP), (1, width), (1, width)]
    quarter = (-(-(2 * PP + 2 * VEC + 2 * images) // 16) * 16, K)
    args = [ids, keep, *stats, *pieces, act, gp, tok, w_in, w_outT, g1, c1]
    rows = pl.BlockSpec((2 * width, K), lambda i: (i, 0))
    pairs = pl.BlockSpec((2, width, S), lambda i: (half * (nb // 2) + i, 0, 0))
    in_specs = ([SMEM, SMEM] + [whole(stats[0].shape)] * 4 + [pl.BlockSpec((1, PP, 2 * width), lambda i: (i, 0, 0))] * 4
                + [rows, rows, pairs, whole(w_in.shape), whole(w_outT.shape), whole(g1.shape), whole(c1.shape)])
    outs, out_specs, scratch = [shape((images, width, S))], [pairs], []
    if half:
        args += [*before, *vecs, u_before]
        in_specs += [whole(v.shape) for v in before] + [whole(v.shape) for v in vecs] + [ANY]
        outs += [shape(quarter, BF16)] * 4
        out_specs += [whole(quarter)] * 4
        scratch = [pltpu.VMEM((2, images, S), F32), pltpu.VMEM(sums[0], F32), pltpu.VMEM(sums[1], F32), pltpu.VMEM((4 * VEC, K), F32), pltpu.VMEM(quarter, F32),
                   pltpu.VMEM((4,) + quarter, BF16)]
    else:
        outs += [shape((2, images, S))] + [shape(v) for v in sums]
        out_specs += [whole((2, images, S))] + [whole(v) for v in sums]
    return pl.pallas_call(
        functools.partial(back_kernel, half=half, P_=P_, PP=PP),
        grid=(nb // 2,), in_specs=in_specs, out_specs=out_specs, out_shape=outs,
        scratch_shapes=scratch + [pltpu.VMEM((2, images, S), F32), pltpu.VMEM((4 * PP, K + 256), BF16), pltpu.VMEM((4 * PP, K), F32),
                        pltpu.VMEM((2, width, S), F32), pltpu.VMEM((2 * width, S), BF16), pltpu.VMEM((4, PP, 2 * width), BF16),
                        pltpu.VMEM((8, K), F32), pltpu.VMEM((4 * PP, 2 * width), F32), pltpu.VMEM((width, S), F32),
                        pltpu.VMEM((width, S), F32)],
        input_output_aliases={len(args) - 1: 0} if half else {},
        compiler_params=pltpu.CompilerParams(vmem_limit_bytes=LIMIT * 24 // 60),
        cost_estimate=cost(1),
        name="token_backward",
    )(*args)


def finish_kernel(t0, t1, t2, t3, s0, s1, s2, s3, u, tok, out, mr, sums, *, skip):
    nb, width, S = tok.shape
    first = pl.program_id(0) * nb

    @pl.when(pl.program_id(0) == 0)
    def _():
        join_stats((t0, t1, t2, t3), mr, width)
        total = ((s0[...].astype(F32) + s1[...].astype(F32)) + (s2[...].astype(F32) + s3[...].astype(F32))) * (1.0 / (4 * width))
        images = sums.shape[1]
        for i in range(2):
            sums[i] = total[skip + i * images:skip + (i + 1) * images, 0:S]

    for b in range(nb):
        at_ = pl.ds(first + b, 1)
        r = mr[1, at_, :]
        n = (tok[b].astype(F32) - mr[0, at_, :]) * r
        out[b] = u[b] - r * (sums[0, at_, :] + n * sums[1, at_, :])


def finish_call(stats, sums, u, tok, skip, steps=4):
    images, width, S = tok.shape
    part = pl.BlockSpec((images // steps, width, S), lambda i: (i, 0, 0))
    return pl.pallas_call(
        functools.partial(finish_kernel, skip=skip),
        grid=(steps,),
        in_specs=[whole(stats[0].shape)] * 4 + [whole(sums[0].shape)] * 4 + [part, part],
        out_specs=part,
        out_shape=shape((images, width, S)),
        scratch_shapes=[pltpu.VMEM((2, images, S), F32), pltpu.VMEM((2, images, S), F32)],
        compiler_params=pltpu.CompilerParams(vmem_limit_bytes=LIMIT * 24 // 60),
        cost_estimate=cost(0),
        name="norm_backward",
    )(*stats, *sums, u, tok)


def masks_of(dp):
    return [6, 2, 1] if dp == 8 else [1 << k for k in reversed(range(dp.bit_length() - 1))]


def dp_place(rel, dp):
    return rel ^ ((rel >> 1) & 2) if dp == 8 else rel


UNITS = 6
GROUPS = 3


def orders(dims):
    last, *most = dims
    if len(dims) == 4:
        a, x, y = most
        most = [x, y, a]
    return [(*most[g % len(most):], *most[:g % len(most)], last) for g in range(GROUPS)]


def first_kernel(k4, r4, k3, r3, *outs, plans):
    dp, _, blk, W = k4.shape
    n = 2 * dp
    bits = n.bit_length() - 1
    unit = 2 * W // UNITS
    per = UNITS // GROUPS
    for g, plan in enumerate(plans):
        for i in range(n):
            coord = [(i >> (bits - 1 - d)) & 1 for d in plan]
            j = 0
            for v in coord[1:]:
                j = 2 * j + v
            for m in range(per):
                k, r = (k4, r4) if g * per + m < UNITS // 2 else (k3, r3)
                c = pl.ds((g * per + m) % (UNITS // 2) * unit, unit)
                v = k[i // 2, i % 2, :, c].astype(F32) + r[i // 2, i % 2, :, c].astype(F32)
                outs[g + GROUPS * coord[0]][j, :, m * unit:(m + 1) * unit] = v.astype(BF16)


def next_kernel(*refs):
    ins, outs = refs[:2 * GROUPS], refs[2 * GROUPS:]
    for g in range(GROUPS):
        k, r = ins[2 * g], ins[2 * g + 1]
        n = k.shape[0] // 2
        outs[g][...] = (k[0:n].astype(F32) + r[0:n].astype(F32)).astype(BF16)
        v = (k[n:].astype(F32) + r[n:].astype(F32)).astype(BF16)
        if n > 1:
            outs[GROUPS + g][...] = v
        else:
            outs[GROUPS][g] = v[0]


def last_kernel(*refs):
    ins, got, outs = refs[:GROUPS], refs[GROUPS], refs[GROUPS + 1:]
    unit = 2 * outs[0].shape[1] // UNITS
    per = UNITS // GROUPS
    for g in range(GROUPS):
        v = ins[g][0].astype(F32) + got[g].astype(F32)
        for m in range(per):
            u = g * per + m
            outs[u // (UNITS // 2)][:, u % (UNITS // 2) * unit:(u % (UNITS // 2) + 1) * unit] = v[:, m * unit:(m + 1) * unit]


def plain_call(kernel, args, outs, name, weight=0):
    return pl.pallas_call(
        kernel, grid=(1,), in_specs=[whole(a.shape) for a in args], out_specs=[whole(o.shape) for o in outs], out_shape=outs,
        compiler_params=pltpu.CompilerParams(vmem_limit_bytes=LIMIT * 24 // 60), name=name, cost_estimate=cost(weight))(*args)


def swap(v, mask, world):
    return lax.ppermute(v, ("dp", "chan"), [(i, i ^ mask) for i in range(world)])


def after(values, done):
    *values, _ = lax.optimization_barrier((*values, done))
    return values


def start_sums(keep4, send4, keep3, send3):
    dp, _, blk, W = keep4.shape
    plans = orders(list(range(len(masks_of(dp)) + 1)))
    return plain_call(functools.partial(first_kernel, plans=plans), (keep4, swap(send4, 1, dp * 4), keep3, swap(send3, 1, dp * 4)),
                      [shape((dp, blk, 2 * W // GROUPS), BF16)] * (2 * GROUPS), "sum_first")


def send_step(parts, t, dp):
    masks = [4 * m for m in masks_of(dp)] + [2]
    plans = orders(list(range(len(masks))))
    return [*parts[:GROUPS], *(swap(v, masks[plans[g][t]], dp * 4) for g, v in enumerate(parts[GROUPS:]))]


def sum_step(got):
    n, blk, cols = got[0].shape
    if n == 1:
        return plain_call(last_kernel, got, [shape((blk, GROUPS * cols // 2))] * 2, "sum_last")
    sends = [shape((n // 2, blk, cols), BF16)] * GROUPS if n > 2 else [shape((GROUPS, blk, cols), BF16)]
    got = [v for g in range(GROUPS) for v in (got[g], got[GROUPS + g])]
    return plain_call(next_kernel, got, [shape((n // 2, blk, cols), BF16)] * GROUPS + sends, "sum_next")


def join_terms(s, PP):
    v = s[2 * PP:2 * PP + VEC] + s[2 * PP + VEC:2 * PP + 2 * VEC]
    hi = v.astype(BF16).astype(F32)
    return jnp.concatenate([s[0:2 * PP], hi, v - hi], axis=0).astype(BF16)


def quarter_sum_kernel(*refs, PP):
    *ins, out = refs
    v = [q[...].astype(F32) for q in ins]
    out[...] = join_terms((v[0] + v[1]) + (v[2] + v[3]) if len(v) == 4 else v[0] + v[1], PP)


def quarter_sum(ins, PP):
    dims = (2 * PP + 2 * VEC, ins[0].shape[1])
    return plain_call(functools.partial(quarter_sum_kernel, PP=PP), ins, [shape(dims, BF16)], "quarter_sum")[0]


def unpack_kernel(ids, q0, q1, q2, q3, w1, w2, b3, g2, c2, b4, b1, b2, g1, c1, quarters, vec, *, P_, PP):
    K = w1.shape[1]
    for k, q in enumerate((q0, q1, q2, q3)):
        quarters[ids[1] ^ k] = q[...]
    for j in range(4):
        s = quarters[j].astype(F32)
        w1[j * P_:(j + 1) * P_, :] = s[0:P_]
        w2[j * P_:(j + 1) * P_, :] = s[PP:PP + P_]
        vec[j * VEC:(j + 1) * VEC, :] = s[2 * PP:2 * PP + VEC] + s[2 * PP + VEC:2 * PP + 2 * VEC]
    row = 0
    for o in (b3, g2, c2, b4):
        for r in range(o.shape[0] // K):
            o[r * K:(r + 1) * K] = vec[row]
            row += 1
    b1[...] = vec[row]
    v = vec[row + 1:row + 2, :]
    b2[...] = jnp.concatenate([v[:, j * PP:j * PP + P_] for j in range(4)], axis=1)[0]
    row += 2
    for o in (g1, c1):
        for r in range(2):
            o[r * K:(r + 1) * K] = vec[row]
            row += 1


def unpack_call(ids, quarters, S, F, W, P_, PP):
    dims = quarters[0].shape
    K = dims[1]
    outs = [(S, K), (S, K), (F,), (W,), (W,), (W,), (K,), (S,), (W,), (W,)]
    return pl.pallas_call(
        functools.partial(unpack_kernel, P_=P_, PP=PP), grid=(1,),
        in_specs=[SMEM] + [whole(dims)] * 4, out_specs=[whole(o) for o in outs], out_shape=[shape(o) for o in outs],
        scratch_shapes=[pltpu.VMEM((4,) + dims, BF16), pltpu.VMEM((4 * VEC, K), F32)],
        compiler_params=pltpu.CompilerParams(vmem_limit_bytes=LIMIT * 8 // 60), name="unpack", cost_estimate=cost(0))(ids, *quarters)


def exchange(value):
    return [value] + [lax.ppermute(value, "chan", [(i, i ^ k) for i in range(4)]) for k in (1, 2, 3)]


def trade(pieces):
    return [pieces[0]] + [lax.ppermute(pieces[k], "chan", [(i, i ^ k) for i in range(4)]) for k in (1, 2, 3)]


def shards(tokens, ln1_gain, ln1_bias, mix_in, mix_in_bias, mix_out, mix_out_bias, ln2_gain, ln2_bias,
           chan_in, chan_in_bias, chan_out, chan_out_bias, skip_masks, cotangent):
    images, S, width = tokens.shape
    P_ = cotangent.shape[1]
    W = cotangent.shape[2]
    PP = -(-P_ // 8) * 8
    tok = jnp.swapaxes(tokens, 1, 2)
    w_outT = jnp.swapaxes(mix_out, 0, 1)
    row = lambda v: v.reshape(1, -1)
    chan = lax.axis_index("chan")
    keep1 = skip_masks[:, 0].astype(F32)
    keep2 = skip_masks[:, 1].astype(F32)
    g1, c1 = row(ln1_gain), row(ln1_bias)

    stats = exchange(stats_call(tok))
    halves = (0, 1)
    dp = lax.axis_size("dp")
    ids = jnp.stack([lax.axis_index("dp"), chan]).astype(jnp.int32)
    R = -(-(images // 2) * P_ // 16) * 16
    og, sum_b4 = upstream_call(keep2, cotangent, R)
    fwd = [token_call(ids, keep1, stats, tok, mix_in, row(mix_in_bias), w_outT, row(mix_out_bias), g1, c1, h, P_, PP) for h in halves]
    arrived = [trade(f[2:6]) for f in fwd]
    weights = (chan_in, chan_out, row(chan_in_bias), row(chan_out_bias), row(ln2_gain), row(ln2_bias))
    c0 = chan_call(ids, keep2, arrived[0], cotangent, og, 0, *weights, None, dp)
    part4, part3, b3_0, out = c0[:4]
    c1_ = chan_call(ids, keep2, arrived[1], cotangent, og, 1, *weights, (part4, part3, out), dp)
    keep4, send4, keep3, send3, b3_1, out = c1_[:6]
    tails = (c0[4:], c1_[6:])
    returned = [trade(t[:4]) for t in tails]
    vecs = [b3_0, b3_1, tails[0][4], tails[1][4], tails[0][5], tails[1][5], sum_b4]
    tokens_back = functools.partial(back_call, ids, keep1, stats)
    u, *sums = tokens_back(returned[0], *fwd[0][:2], tok, mix_in, w_outT, g1, c1, 0, P_, PP, None, None, None)
    keep4, keep3 = after((keep4, keep3), u)
    parts = after(start_sums(keep4, send4, keep3, send3), returned[1][3])
    pairs = send_step(parts, 0, dp)
    u, = after((u,), parts[0])
    u, *pieces = tokens_back(returned[1], *fwd[1][:2], tok, mix_in, w_outT, g1, c1, 1, P_, PP, [*sums[1:], sums[0]], vecs, u)
    pieces = trade(pieces)
    quarter = quarter_sum(pieces, PP)
    masks = [4 * m for m in reversed(masks_of(dp))]
    grad = None
    for t, mask in enumerate(masks):
        other = swap(quarter, mask, dp * 4)
        parts = sum_step(after(pairs, quarter))
        pairs = send_step(parts, t + 1, dp)
        done = parts[0]
        if grad is None:
            done = grad = finish_call(stats, after(pieces, done), u, tok, 2 * PP + 2 * VEC)
        quarter = quarter_sum(after((quarter, other), done), PP)
    share_w4, share_w3 = sum_step(after(pairs, quarter))
    s_w1, s_w2, s_b3, s_g2, s_c2, s_b4, s_b1, s_b2, s_g1, s_c1 = unpack_call(
        ids, exchange(quarter), S, chan_in.shape[1], W, P_, PP)
    return (out, jnp.swapaxes(grad, 1, 2), s_g1, s_c1, s_w1, s_b1, jnp.swapaxes(s_w2, 0, 1), s_b2, s_g2, s_c2,
            jnp.swapaxes(share_w3, 0, 1), s_b3, share_w4, s_b4)


def solution(mesh):
    rep = P()
    return jax.shard_map(
        shards, mesh=mesh,
        in_specs=(P("dp", None, "chan"), P("chan"), P("chan")) + (rep,) * 10 + (P("dp", None), P("dp", "chan", None)),
        out_specs=(P("dp", "chan", None), P("dp", None, "chan"), rep, rep, rep, rep, rep, rep, rep, rep,
                   P(None, ("dp", "chan")), rep, P(("dp", "chan"), None), rep),
        check_vma=False,
    )
```

time: 499 us -> 211 us (0.42)
  waiting for transfers between devices: 250 us -> 52 us
  blocking collectives: 40.6 us -> 0 us
  local copies, waits for them, and re-layouts: 35.8 us -> 8.7 us
  Pallas kernels: 135 us -> 119 us
  between operations: 14.2 us -> 1.29 us
  starting transfers between devices: 15.3 us -> 27.6 us
    psum x1 -> x0, waiting for transfers between devices: 133 us -> none  [shards(): lax.psum((place(gg1), place(gc1), gw1, gb1.reshape(-1), unpad(gw2), unpad...]
    reduce_scatter x2 -> x0, waiting for transfers between devices: 102 us -> none  [the longest x1 102 us: shards(): lax.psum_scatter(grad_w3, ('dp', 'chan'), scatter_dimension=0, tiled=True)]
    psum x1 -> x0, blocking collectives: 40.6 us -> none  [shards(): lax.psum((place(gg1), place(gc1), gw1, gb1.reshape(-1), unpad(gw2), unpad...]
    ppermute x0 -> x15, waiting for transfers between devices: none -> 29.8 us  [swap(): lax.ppermute(v, ('dp', 'chan'), [(i, i ^ mask) for i in range(world)])]
    unnamed x114 -> x80, local copies, waits for them, and re-layouts: 31.3 us -> 6.39 us
    pallas_call x9 -> x17, Pallas kernels: 122 us -> 103 us  [the longest x2 72.5 us: chan_call(): pl.pallas_call(functools.partial(chan_kernel, nb=nb, P_=P_, R=R, half=hal...]
    ppermute x0 -> x15, starting transfers between devices: none -> 11.8 us  [swap(): lax.ppermute(v, ('dp', 'chan'), [(i, i ^ mask) for i in range(world)])]
    ppermute x12 -> x15, waiting for transfers between devices: 12.1 us -> 17.6 us  [trade(): lax.ppermute(pieces[k], 'chan', [(i, i ^ k) for i in range(4)])]
  transfers between devices with their start and end apart: 24 -> 36, of which waited for: 7 -> 9; matrix products, arithmetic and copies ran while one was open for 2% -> 2% of each run, Pallas kernels for 16% -> 50%
where the time goes in v2:
time: 211 us; the launch traced here: 210 us
  Pallas kernels  119 us (56%)
  waiting for transfers between devices  52 us (25%)
  starting transfers between devices  27.6 us (13%)
  local copies, waits for them, and re-layouts  8.7 us (4%)
    pallas_call x2, Pallas kernels, chan_call(): pl.pallas_call(functools.partial(chan_kernel, nb=nb, P_=P_, R=R, half=hal...  72.5 us
    ppermute x15, waiting for transfers between devices, swap(): lax.ppermute(v, ('dp', 'chan'), [(i, i ^ mask) for i in range(world)])  29.8 us
    ppermute x15, waiting for transfers between devices, trade(): lax.ppermute(pieces[k], 'chan', [(i, i ^ k) for i in range(4)])  17.6 us
    pallas_call x2, Pallas kernels, token_call(): pl.pallas_call(functools.partial(token_kernel, first=half * nb, P_=P_, PP...  16.6 us
    pallas_call x2, Pallas kernels, back_call(): pl.pallas_call(functools.partial(back_kernel, half=half, P_=P_, PP=PP), g...  15.1 us
    ppermute x15, starting transfers between devices, swap(): lax.ppermute(v, ('dp', 'chan'), [(i, i ^ mask) for i in range(world)])  11.8 us
    ppermute x15, starting transfers between devices, trade(): lax.ppermute(pieces[k], 'chan', [(i, i ^ k) for i in range(4)])  10.8 us
    unnamed x80, local copies, waits for them, and re-layouts  6.39 us
  transfers between devices with their start and end apart: 36, of which 9 were waited for; matrix products, arithmetic and copies ran while one was open for 2% of the time, Pallas kernels for 50%

profile of v2, /device:TPU:17, one launch (start us, length us, event | category | flops | bytes accessed | tf_op | source)
XLA Modules:
  0.0 210.0 jit_solution(4073459947703439130)
XLA Ops:
  0.7 4.1 %stats.1.t0 = f32[2,28,196]{2,1,0:T(8,128)} custom-call(bf16[28,192,196]{2,1,0:T(8,128)(2,1)} %bitcast.15), custom_call_target="tpu_custom_call" | custom-call | flops 1 | bytes 1 | tf_op jit(solution)/shard_map/stats/pallas_call | solution.py:73
  4.8 1.8 collective-permute-start.2
  6.6 0.2 collective-permute-start.1
  7.0 0.6 convert_bitcast_fusion
  7.6 0.7 pad_add_fusion.me.refs_0_.ids
  8.3 3.2 %upstream.1 = (bf16[2,688,768]{2,1,0:T(8,128)(2,1)}, f32[1,768]{1,0:T(1,128)}) custom-call(f32[28]{0:T(128)} %get-tuple-element.263.keep.refs_1_, bf16[28,49,768]{2,1,0:T(8,128)(2,1)} %refs_6_.3), custom_call_target="tpu_custom_call" | custom-call | flops 1 | bytes 1 | tf_op jit(solution)/shard_map/upstream/pallas_call | solution.py:196
  11.5 0.6 reshape.56.b_in
  12.0 0.6 reshape.62.refs_12_
  12.6 0.6 reshape.63.refs_13_
  13.2 0.6 reshape.61.refs_11_
  13.8 0.6 copy-done.4
  14.5 8.3 %token_forward.3 = (bf16[2688,384]{1,0:T(8,128)(2,1)}, bf16[2688,384]{1,0:T(8,128)(2,1)}, bf16[7,56,384]{2,1,0:T(8,128)(2,1)}, bf16[7,56,384]{2,1,0:T(8,128)(2,1...) custom-call(s32[2]{0:T(128)} %pad_add_fusion.me.refs_0_.ids, f32[28]{0:T(128)} %get-tuple-element.262.keep, ...), custom_call_target="tpu_custom_call" | custom-call | flops 1 | bytes 1 | tf_op jit(solution)/shard_map/token_forward/pallas_call | solution.py:160
  22.7 0.4 collective-permute-start.6
  23.1 1.3 collective-permute-start.7
  24.4 0.6 collective-permute-start.8
  24.9 8.3 %token_forward.2 = (bf16[2688,384]{1,0:T(8,128)(2,1)}, bf16[2688,384]{1,0:T(8,128)(2,1)}, bf16[7,56,384]{2,1,0:T(8,128)(2,1)}, bf16[7,56,384]{2,1,0:T(8,128)(2,1...) custom-call(s32[2]{0:T(128)} %pad_add_fusion.me.refs_0_.ids, f32[28]{0:T(128)} %get-tuple-element.262.keep, ...), custom_call_target="tpu_custom_call" | custom-call | flops 99999997952 | bytes 1 | tf_op jit(solution)/shard_map/token_forward/pallas_call | solution.py:160
  33.3 1.3 collective-permute-start.4
  34.6 0.9 collective-permute-start.5
  35.4 3.8 %collective-permute-done.8.refs_5_ = bf16[7,56,384]{2,1,0:T(8,128)(2,1)S(1)} collective-permute-done((bf16[7,56,384]{2,1,0:T(8,128)(2,1)}, bf16[7,56,384]{2,1,0:T(8,128)(2,1)S(1)}, u32[]{:S(2)}, u32[]{:S(2)}) %collective-permute-start.8) | collective-permute-done | bytes 301088 | tf_op jit(solution)/shard_map/ppermute | solution.py:691
  39.3 0.7 copy-done.39
  40.0 35.5 %channel_mlp.2 = (f32[3072,768]{1,0:T(8,128)}, f32[3072,768]{1,0:T(8,128)}, f32[1,3072]{1,0:T(1,128)}, bf16[28,49,768]{2,1,0:T(8,128)(2,1)}, bf16[7,56,384]{2,1,...) custom-call(s32[2]{0:T(128)} %pad_add_fusion.me.refs_0_.ids, ...), custom_call_target="tpu_custom_call" | custom-call | flops 99999997952 | bytes 1 | tf_op jit(solution)/shard_map/channel_mlp/pallas_call | solution.py:332
  75.5 1.2 collective-permute-start.13
  76.7 0.9 collective-permute-start.14
  77.7 0.7 copy-done.35
  78.6 37.0 %channel_mlp.3 = (bf16[8,2,96,768]{3,2,1,0:T(8,128)(2,1)}, bf16[8,2,96,768]{3,2,1,0:T(8,128)(2,1)}, bf16[8,2,96,768]{3,2,1,0:T(8,128)(2,1)}, bf16[8,2,96,768]{3,...) custom-call(s32[2]{0:T(128)} %pad_add_fusion.me.refs_0_.ids, ...), custom_call_target="tpu_custom_call", output_to_operand_aliasing={{5}: (16, {})} | custom-call | flops 99999997952 | bytes 1 | tf_op jit(solution)/shard_map/channel_mlp/pallas_call | solution.py:332
  115.7 1.2 collective-permute-start.10
  116.9 0.9 collective-permute-start.11
  117.8 0.5 collective-permute-start.16
  118.4 1.6 copy-done.16
  120.0 1.6 copy-done.17
  121.6 1.0 copy-done.22
  122.6 7.8 %token_backward.2 = (f32[28,192,196]{2,1,0:T(8,128)S(1)}, f32[2,28,196]{2,1,0:T(8,128)S(1)}, f32[196,384]{1,0:T(8,128)S(1)}, f32[224,384]{1,0:T(8,128)S(1)}, f32...) custom-call(s32[2]{0:T(128)S(1)} %copy-done.12, f32[28]{0:T(128)S(1)} %copy-done.13, ...), custom_call_target="tpu_custom_call" | custom-call | flops 99999997952 | bytes 1 | tf_op jit(solution)/shard_map/token_backward/pallas_call | solution.py:485
  130.5 1.1 sum_first.1
  131.6 1.3 collective-permute-start.20
  132.9 1.1 collective-permute-start.21
  134.0 1.3 collective-permute-start.22
  135.4 7.2 %token_backward.3 = (f32[28,192,196]{2,1,0:T(8,128)S(1)}, bf16[192,384]{1,0:T(8,128)(2,1)S(1)}, bf16[192,384]{1,0:T(8,128)(2,1)S(1)}, bf16[192,384]{1,0:T(8,128)(2,1)S(1)}, bf16[192,384]{1,0:T(8,128)(2,1)S(1)}) custom-call(s32[2]{0:T(128)S(1)} %copy-done.12, f32[28]{0:T(128)S(1)} %copy-done.13, ...), custom_call_target="tpu_custom_call", output_to_operand_aliasing={{0}: (31, {})} | custom-call | flops 99999997952 | bytes 1 | tf_op jit(solution)/shard_map/token_backward/pallas_call | solution.py:485
  142.6 0.9 collective-permute-start.17
  143.6 0.4 collective-permute-start.18
  144.0 0.6 collective-permute-done.17.refs_1_.s1
  144.6 0.7 collective-permute-start.19
  145.3 9.5 %collective-permute-done.18.refs_2_.s2 = bf16[192,384]{1,0:T(8,128)(2,1)S(1)} collective-permute-done((bf16[192,384]{1,0:T(8,128)(2,1)S(1)}, bf16[192,384]{1,0:T(8,128)(2,1)S(1)}, u32[]{:S(2)}, u32[]{:S(2)}) %collective-permute-start.18) | collective-permute-done | bytes 147488 | tf_op jit(solution)/shard_map/ppermute | solution.py:691
  154.8 3.6 %collective-permute-done.19.refs_3_.s3 = bf16[192,384]{1,0:T(8,128)(2,1)S(1)} collective-permute-done((bf16[192,384]{1,0:T(8,128)(2,1)S(1)}, bf16[192,384]{1,0:T(8,128)(2,1)S(1)}, u32[]{:S(2)}, u32[]{:S(2)}) %collective-permute-start.19) | collective-permute-done | bytes 147488 | tf_op jit(solution)/shard_map/ppermute | solution.py:691
  158.6 0.5 sum_next.3
  159.1 1.2 collective-permute-start.25
  160.3 1.3 collective-permute-start.26
  161.6 0.2 collective-permute-start.27
  161.8 1.2 collective-permute-start.23
  163.0 3.3 %norm_backward.1 = f32[28,192,196]{2,1,0:T(8,128)} custom-call(f32[2,28,196]{2,1,0:T(8,128)S(1)} %copy-done.3, f32[2,28,196]{2,1,0:T(8,128)S(1)} %copy-done.9, f32[2,28,196]{2,1,0:T(8,128)S(1)} %copy-done.7, f32[2,28,196]{2,1,0:T(8,128)S(1)} %copy-done.5, bf16[192,384]{1,0:T(8,128)(2,1)S(1)} %get-tuple-element.208.refs_0_.s0, ...), custom_call_target="tpu_custom_call" | custom-call | flops 1 | bytes 1 | tf_op jit(solution)/shard_map/norm_backward/pallas_call | solution.py:521
  166.3 7.6 %collective-permute-done.23.refs_1_ = bf16[128,384]{1,0:T(8,128)(2,1)S(1)} collective-permute-done((bf16[128,384]{1,0:T(8,128)(2,1)S(1)}, bf16[128,384]{1,0:T(8,128)(2,1)S(1)}, u32[]{:S(2)}, u32[]{:S(2)}) %collective-permute-start.23) | collective-permute-done | bytes 98336 | tf_op jit(solution)/shard_map/ppermute | solution.py:604
  174.0 0.3 sum_next.4
  174.2 0.2 collective-permute-start.29
  174.5 0.3 collective-permute-start.30
  174.7 0.3 collective-permute-start.31
  175.1 1.3 collective-permute-start.24
  176.4 5.1 %collective-permute-done.24.refs_1_ = bf16[128,384]{1,0:T(8,128)(2,1)S(1)} collective-permute-done((bf16[128,384]{1,0:T(8,128)(2,1)S(1)}, bf16[128,384]{1,0:T(8,128)(2,1)S(1)}, u32[]{:S(2)}, u32[]{:S(2)}) %collective-permute-start.24) | collective-permute-done | bytes 98336 | tf_op jit(solution)/shard_map/ppermute | solution.py:604
  181.8 1.5 collective-permute-start.28
  183.2 17.1 %collective-permute-done.28.refs_1_ = bf16[128,384]{1,0:T(8,128)(2,1)S(1)} collective-permute-done((bf16[128,384]{1,0:T(8,128)(2,1)S(1)}, bf16[128,384]{1,0:T(8,128)(2,1)S(1)}, u32[]{:S(2)}, u32[]{:S(2)}) %collective-permute-start.28) | collective-permute-done | bytes 98336 | tf_op jit(solution)/shard_map/ppermute | solution.py:604
  200.4 1.7 collective-permute-start.34
  202.1 1.1 collective-permute-start.33
  203.2 2.1 collective-permute-done.34.q3
  205.3 2.4 %collective-permute-done.33.q2 = bf16[128,384]{1,0:T(8,128)(2,1)S(1)} collective-permute-done((bf16[128,384]{1,0:T(8,128)(2,1)S(1)}, bf16[128,384]{1,0:T(8,128)(2,1)S(1)}, u32[]{:S(2)}, u32[]{:S(2)}) %collective-permute-start.33) | collective-permute-done | bytes 98336 | tf_op jit(solution)/shard_map/ppermute | solution.py:687
  207.7 1.5 unpack.1
  209.2 0.8 sum_last.1
  (113 shorter events, 1.2 us)
Async XLA Ops:
  0.6 6.4 %copy-start.33 = (s32[28,2]{0,1:T(2,128)S(1)}, s32[28,2]{0,1:T(2,128)}, u32[]{:S(2)}) copy-start(s32[28,2]{0,1:T(2,128)} %param.28) | copy-start | bytes 676
  0.7 10.8 %copy-start.32 = (f32[384]{0:T(512)S(1)}, f32[384]{0:T(512)}, u32[]{:S(2)}) copy-start(f32[384]{0:T(512)} %param.19) | copy-start | bytes 4612
  0.7 11.4 %copy-start.29 = (f32[768]{0:T(1024)S(1)}, f32[768]{0:T(1024)}, u32[]{:S(2)}) copy-start(f32[768]{0:T(1024)} %param.22) | copy-start | bytes 9220
  0.7 11.9 %copy-start.30 = (f32[768]{0:T(1024)S(1)}, f32[768]{0:T(1024)}, u32[]{:S(2)}) copy-start(f32[768]{0:T(1024)} %param.23) | copy-start | bytes 9220
  0.7 12.5 %copy-start.31 = (f32[768]{0:T(1024)S(1)}, f32[768]{0:T(1024)}, u32[]{:S(2)}) copy-start(f32[768]{0:T(1024)} %param.27) | copy-start | bytes 9220
  4.8 9.0 %collective-permute-start.2 = (f32[2,28,196]{2,1,0:T(8,128)}, f32[2,28,196]{2,1,0:T(8,128)S(1)}, u32[]{:S(2)}, u32[]{:S(2)}) collective-permute-start(f32[2,28,196]{2,1,0:T(8,128)} %stats.1.t0), channel_id=1, source_target_pairs={{0,3},{1,2},{2,1},{3,0},{4,7},{5,6},{6,5},{7,4},{8,11},{9,10},{10,... | collective-permute-start | bytes 131720 | tf_op jit(solution)/shard_map/ppermute | solution.py:687
  6.6 7.2 %collective-permute-start.1 = (f32[2,28,196]{2,1,0:T(8,128)}, f32[2,28,196]{2,1,0:T(8,128)S(1)}, u32[]{:S(2)}, u32[]{:S(2)}) collective-permute-start(f32[2,28,196]{2,1,0:T(8,128)} %stats.1.t0), channel_id=1, source_target_pairs={{0,2},{1,3},{2,0},{3,1},{4,6},{5,7},{6,4},{7,5},{8,10},{9,11},{10,... | collective-permute-start | bytes 131720 | tf_op jit(solution)/shard_map/ppermute | solution.py:687
  6.8 7.0 %collective-permute-start = (f32[2,28,196]{2,1,0:T(8,128)}, f32[2,28,196]{2,1,0:T(8,128)S(1)}, u32[]{:S(2)}, u32[]{:S(2)}) collective-permute-start(f32[2,28,196]{2,1,0:T(8,128)} %stats.1.t0), channel_id=1, source_target_pairs={{0,1},{1,0},{2,3},{3,2},{4,5},{5,4},{6,7},{7,6},{8,9},{9,8},{10,11... | collective-permute-start | bytes 131720 | tf_op jit(solution)/shard_map/ppermute | solution.py:687
  22.7 11.8 %collective-permute-start.6 = (bf16[7,56,384]{2,1,0:T(8,128)(2,1)}, bf16[7,56,384]{2,1,0:T(8,128)(2,1)S(1)}, u32[]{:S(2)}, u32[]{:S(2)}) collective-permute-start(bf16[7,56,384]{2,1,0:T(8,128)(2,1)} %get-tuple-element.144), channel_id=1, source_target_pairs={{0,1},{1,0},{2,3},{3,2},{4,5},{5,4},{6,7},{7,6},{8,9},{9,8},{10,11... | collective-permute-start | bytes 903176 | tf_op jit(solution)/shard_map/ppermute | solution.py:691
  23.1 12.3 %collective-permute-start.7 = (bf16[7,56,384]{2,1,0:T(8,128)(2,1)}, bf16[7,56,384]{2,1,0:T(8,128)(2,1)S(1)}, u32[]{:S(2)}, u32[]{:S(2)}) collective-permute-start(bf16[7,56,384]{2,1,0:T(8,128)(2,1)} %get-tuple-element.145), channel_id=1, source_target_pairs={{0,2},{1,3},{2,0},{3,1},{4,6},{5,7},{6,4},{7,5},{8,10},{9,11},{10,... | collective-permute-start | bytes 903176 | tf_op jit(solution)/shard_map/ppermute | solution.py:691
  24.4 14.9 %collective-permute-start.8 = (bf16[7,56,384]{2,1,0:T(8,128)(2,1)}, bf16[7,56,384]{2,1,0:T(8,128)(2,1)S(1)}, u32[]{:S(2)}, u32[]{:S(2)}) collective-permute-start(bf16[7,56,384]{2,1,0:T(8,128)(2,1)} %get-tuple-element.146), channel_id=1, source_target_pairs={{0,3},{1,2},{2,1},{3,0},{4,7},{5,6},{6,5},{7,4},{8,11},{9,10},{10,... | collective-permute-start | bytes 903176 | tf_op jit(solution)/shard_map/ppermute | solution.py:691
  33.2 43.5 %collective-permute-start.3 = (bf16[7,56,384]{2,1,0:T(8,128)(2,1)}, bf16[7,56,384]{2,1,0:T(8,128)(2,1)S(1)}, u32[]{:S(2)}, u32[]{:S(2)}) collective-permute-start(bf16[7,56,384]{2,1,0:T(8,128)(2,1)} %get-tuple-element.139), channel_id=1, source_target_pairs={{0,1},{1,0},{2,3},{3,2},{4,5},{5,4},{6,7},{7,6},{8,9},{9,8},{10,11... | collective-permute-start | bytes 903176 | tf_op jit(solution)/shard_map/ppermute | solution.py:691
  33.3 44.4 %collective-permute-start.4 = (bf16[7,56,384]{2,1,0:T(8,128)(2,1)}, bf16[7,56,384]{2,1,0:T(8,128)(2,1)S(1)}, u32[]{:S(2)}, u32[]{:S(2)}) collective-permute-start(bf16[7,56,384]{2,1,0:T(8,128)(2,1)} %get-tuple-element.140), channel_id=1, source_target_pairs={{0,2},{1,3},{2,0},{3,1},{4,6},{5,7},{6,4},{7,5},{8,10},{9,11},{10,... | collective-permute-start | bytes 903176 | tf_op jit(solution)/shard_map/ppermute | solution.py:691
  34.6 43.1 %collective-permute-start.5 = (bf16[7,56,384]{2,1,0:T(8,128)(2,1)}, bf16[7,56,384]{2,1,0:T(8,128)(2,1)S(1)}, u32[]{:S(2)}, u32[]{:S(2)}) collective-permute-start(bf16[7,56,384]{2,1,0:T(8,128)(2,1)} %get-tuple-element.141), channel_id=1, source_target_pairs={{0,3},{1,2},{2,1},{3,0},{4,7},{5,6},{6,5},{7,4},{8,11},{9,10},{10,... | collective-permute-start | bytes 903176 | tf_op jit(solution)/shard_map/ppermute | solution.py:691
  75.5 41.4 %collective-permute-start.12 = (bf16[7,56,384]{2,1,0:T(8,128)(2,1)}, bf16[7,56,384]{2,1,0:T(8,128)(2,1)S(1)}, u32[]{:S(2)}, u32[]{:S(2)}) collective-permute-start(bf16[7,56,384]{2,1,0:T(8,128)(2,1)} %get-tuple-element.158), channel_id=1, source_target_pairs={{0,1},{1,0},{2,3},{3,2},{4,5},{5,4},{6,7},{7,6},{8,9},{9,8},{10,11... | collective-permute-start | bytes 903176 | tf_op jit(solution)/shard_map/ppermute | solution.py:691
  75.5 42.3 %collective-permute-start.13 = (bf16[7,56,384]{2,1,0:T(8,128)(2,1)}, bf16[7,56,384]{2,1,0:T(8,128)(2,1)S(1)}, u32[]{:S(2)}, u32[]{:S(2)}) collective-permute-start(bf16[7,56,384]{2,1,0:T(8,128)(2,1)} %get-tuple-element.159), channel_id=1, source_target_pairs={{0,2},{1,3},{2,0},{3,1},{4,6},{5,7},{6,4},{7,5},{8,10},{9,11},{10,... | collective-permute-start | bytes 903176 | tf_op jit(solution)/shard_map/ppermute | solution.py:691
  76.7 41.1 %collective-permute-start.14 = (bf16[7,56,384]{2,1,0:T(8,128)(2,1)}, bf16[7,56,384]{2,1,0:T(8,128)(2,1)}, u32[]{:S(2)}, u32[]{:S(2)}) collective-permute-start(bf16[7,56,384]{2,1,0:T(8,128)(2,1)} %get-tuple-element.160), channel_id=1, source_target_pairs={{0,3},{1,2},{2,1},{3,0},{4,7},{5,6},{6,5},{7,4},{8,11},{9,10},{10,... | collective-permute-start | bytes 903176 | tf_op jit(solution)/shard_map/ppermute | solution.py:691
  78.5 39.9 %copy-start = (bf16[28,196,192]{1,2,0:T(8,128)(2,1)S(1)}, bf16[28,196,192]{1,2,0:T(8,128)(2,1)}, u32[]{:S(2)}) copy-start(bf16[28,196,192]{1,2,0:T(8,128)(2,1)} %param.15) | copy-start | bytes 6322180
  78.5 39.9 %copy-start.3 = (f32[2,28,196]{2,1,0:T(8,128)S(1)}, f32[2,28,196]{2,1,0:T(8,128)}, u32[]{:S(2)}) copy-start(f32[2,28,196]{2,1,0:T(8,128)} %stats.1.t0) | copy-start | bytes 131716
  78.5 39.9 %copy-start.5 = (f32[2,28,196]{2,1,0:T(8,128)S(1)}, f32[2,28,196]{2,1,0:T(8,128)}, u32[]{:S(2)}) copy-start(f32[2,28,196]{2,1,0:T(8,128)} %copy-done.4) | copy-start | bytes 131716
  78.5 39.9 %copy-start.7 = (f32[2,28,196]{2,1,0:T(8,128)S(1)}, f32[2,28,196]{2,1,0:T(8,128)}, u32[]{:S(2)}) copy-start(f32[2,28,196]{2,1,0:T(8,128)} %copy-done.6) | copy-start | bytes 131716
  78.5 39.9 %copy-start.9 = (f32[2,28,196]{2,1,0:T(8,128)S(1)}, f32[2,28,196]{2,1,0:T(8,128)}, u32[]{:S(2)}) copy-start(f32[2,28,196]{2,1,0:T(8,128)} %copy-done.8) | copy-start | bytes 131716
  78.5 39.9 %copy-start.10 = (bf16[196,384]{1,0:T(8,128)(2,1)S(1)}, bf16[196,384]{1,0:T(8,128)(2,1)}, u32[]{:S(2)}) copy-start(bf16[196,384]{1,0:T(8,128)(2,1)} %w_in.7) | copy-start | bytes 451588
  78.5 39.9 %copy-start.11 = (bf16[384,196]{0,1:T(8,128)(2,1)S(1)}, bf16[384,196]{0,1:T(8,128)(2,1)}, u32[]{:S(2)}) copy-start(bf16[384,196]{0,1:T(8,128)(2,1)} %param.20) | copy-start | bytes 451588
  78.5 39.9 %copy-start.12 = (s32[2]{0:T(128)S(1)}, s32[2]{0:T(128)}, u32[]{:S(2)}) copy-start(s32[2]{0:T(128)} %pad_add_fusion.me.refs_0_.ids) | copy-start | bytes 28
  78.5 39.9 %copy-start.13 = (f32[28]{0:T(128)S(1)}, f32[28]{0:T(128)}, u32[]{:S(2)}) copy-start(f32[28]{0:T(128)} %get-tuple-element.262.keep) | copy-start | bytes 340
  78.5 39.9 %copy-start.14 = (f32[192]{0:T(256)S(1)}, f32[192]{0:T(256)}, u32[]{:S(2)}) copy-start(f32[192]{0:T(256)} %param.16) | copy-start | bytes 2308
  78.6 39.9 %copy-start.15 = (f32[192]{0:T(256)S(1)}, f32[192]{0:T(256)}, u32[]{:S(2)}) copy-start(f32[192]{0:T(256)} %param.17) | copy-start | bytes 2308
  115.6 19.7 %collective-permute-start.9 = (bf16[7,56,384]{2,1,0:T(8,128)(2,1)}, bf16[7,56,384]{2,1,0:T(8,128)(2,1)S(1)}, u32[]{:S(2)}, u32[]{:S(2)}) collective-permute-start(bf16[7,56,384]{2,1,0:T(8,128)(2,1)} %get-tuple-element.152), channel_id=1, source_target_pairs={{0,1},{1,0},{2,3},{3,2},{4,5},{5,4},{6,7},{7,6},{8,9},{9,8},{10,11... | collective-permute-start | bytes 903176 | tf_op jit(solution)/shard_map/ppermute | solution.py:691
  115.7 19.6 %collective-permute-start.10 = (bf16[7,56,384]{2,1,0:T(8,128)(2,1)}, bf16[7,56,384]{2,1,0:T(8,128)(2,1)S(1)}, u32[]{:S(2)}, u32[]{:S(2)}) collective-permute-start(bf16[7,56,384]{2,1,0:T(8,128)(2,1)} %get-tuple-element.153), channel_id=1, source_target_pairs={{0,2},{1,3},{2,0},{3,1},{4,6},{5,7},{6,4},{7,5},{8,10},{9,11},{10,... | collective-permute-start | bytes 903176 | tf_op jit(solution)/shard_map/ppermute | solution.py:691
  116.9 14.7 %collective-permute-start.11 = (bf16[7,56,384]{2,1,0:T(8,128)(2,1)}, bf16[7,56,384]{2,1,0:T(8,128)(2,1)S(1)}, u32[]{:S(2)}, u32[]{:S(2)}) collective-permute-start(bf16[7,56,384]{2,1,0:T(8,128)(2,1)} %get-tuple-element.154), channel_id=1, source_target_pairs={{0,3},{1,2},{2,1},{3,0},{4,7},{5,6},{6,5},{7,4},{8,11},{9,10},{10,... | collective-permute-start | bytes 903176 | tf_op jit(solution)/shard_map/ppermute | solution.py:691
  117.8 12.6 %collective-permute-start.15 = (bf16[8,2,96,768]{3,2,1,0:T(8,128)(2,1)}, bf16[8,2,96,768]{3,2,1,0:T(8,128)(2,1)S(1)}, u32[]{:S(2)}, u32[]{:S(2)}) collective-permute-start(bf16[8,2,96,768]{3,2,1,0:T(8,128)(2,1)} %get-tuple-element.181), channel_id=1, source_target_pairs={{0,1},{1,0},{2,3},{3,2},{4,5},{5,4},{6,7},{7,6},{8,9},{9,8},{10,11... | collective-permute-start | bytes 7077896 | tf_op jit(solution)/shard_map/ppermute | solution.py:604
  117.8 12.6 %collective-permute-start.16 = (bf16[8,2,96,768]{3,2,1,0:T(8,128)(2,1)}, bf16[8,2,96,768]{3,2,1,0:T(8,128)(2,1)S(1)}, u32[]{:S(2)}, u32[]{:S(2)}) collective-permute-start(bf16[8,2,96,768]{3,2,1,0:T(8,128)(2,1)} %get-tuple-element.183), channel_id=1, source_target_pairs={{0,1},{1,0},{2,3},{3,2},{4,5},{5,4},{6,7},{7,6},{8,9},{9,8},{10,11... | collective-permute-start | bytes 7077896 | tf_op jit(solution)/shard_map/ppermute | solution.py:604
  122.6 7.9 %copy-start.1 = (bf16[8,2,96,768]{3,2,1,0:T(8,128)(2,1)S(1)}, bf16[8,2,96,768]{3,2,1,0:T(8,128)(2,1)}, u32[]{:S(2)}) copy-start(bf16[8,2,96,768]{3,2,1,0:T(8,128)(2,1)} %get-tuple-element.180.k4) | copy-start | bytes 7077892
  122.6 8.0 %copy-start.2 = (bf16[8,2,96,768]{3,2,1,0:T(8,128)(2,1)S(1)}, bf16[8,2,96,768]{3,2,1,0:T(8,128)(2,1)}, u32[]{:S(2)}) copy-start(bf16[8,2,96,768]{3,2,1,0:T(8,128)(2,1)} %get-tuple-element.182.k3) | copy-start | bytes 7077892
  130.4 4.9 %copy-start.18 = (f32[1,768]{1,0:T(1,128)S(1)}, f32[1,768]{1,0:T(1,128)}, u32[]{:S(2)}) copy-start(f32[1,768]{1,0:T(1,128)} %get-tuple-element.176.rest_13_) | copy-start | bytes 9220
  130.4 4.9 %copy-start.19 = (bf16[2688,384]{1,0:T(8,128)(2,1)S(1)}, bf16[2688,384]{1,0:T(8,128)(2,1)}, u32[]{:S(2)}) copy-start(bf16[2688,384]{1,0:T(8,128)(2,1)} %get-tuple-element.155.act) | copy-start | bytes 6193156
  130.4 4.9 %copy-start.20 = (bf16[2688,384]{1,0:T(8,128)(2,1)S(1)}, bf16[2688,384]{1,0:T(8,128)(2,1)}, u32[]{:S(2)}) copy-start(bf16[2688,384]{1,0:T(8,128)(2,1)} %get-tuple-element.156.gp) | copy-start | bytes 6193156
  130.4 4.9 %copy-start.21 = (bf16[7,56,384]{2,1,0:T(8,128)(2,1)S(1)}, bf16[7,56,384]{2,1,0:T(8,128)(2,1)}, u32[]{:S(2)}) copy-start(bf16[7,56,384]{2,1,0:T(8,128)(2,1)} %get-tuple-element.151.p0) | copy-start | bytes 903172
  130.4 4.9 %copy-start.23 = (f32[1,3072]{1,0:T(1,128)S(1)}, f32[1,3072]{1,0:T(1,128)}, u32[]{:S(2)}) copy-start(f32[1,3072]{1,0:T(1,128)} %get-tuple-element.171.rest_8_) | copy-start | bytes 36868
  130.4 4.9 %copy-start.24 = (f32[1,3072]{1,0:T(1,128)S(1)}, f32[1,3072]{1,0:T(1,128)}, u32[]{:S(2)}) copy-start(f32[1,3072]{1,0:T(1,128)} %get-tuple-element.170.rest_7_) | copy-start | bytes 36868
  130.4 4.9 %copy-start.25 = (f32[1,768]{1,0:T(1,128)S(1)}, f32[1,768]{1,0:T(1,128)}, u32[]{:S(2)}) copy-start(f32[1,768]{1,0:T(1,128)} %get-tuple-element.173.rest_10_) | copy-start | bytes 9220
  130.4 4.9 %copy-start.26 = (f32[1,768]{1,0:T(1,128)S(1)}, f32[1,768]{1,0:T(1,128)}, u32[]{:S(2)}) copy-start(f32[1,768]{1,0:T(1,128)} %get-tuple-element.175.rest_12_) | copy-start | bytes 9220
  130.5 4.9 %copy-start.27 = (f32[1,768]{1,0:T(1,128)S(1)}, f32[1,768]{1,0:T(1,128)}, u32[]{:S(2)}) copy-start(f32[1,768]{1,0:T(1,128)} %get-tuple-element.172.rest_9_) | copy-start | bytes 9220
  130.5 4.9 %copy-start.28 = (f32[1,768]{1,0:T(1,128)S(1)}, f32[1,768]{1,0:T(1,128)}, u32[]{:S(2)}) copy-start(f32[1,768]{1,0:T(1,128)} %get-tuple-element.174.rest_11_) | copy-start | bytes 9220
  131.6 26.9 %collective-permute-start.20 = (bf16[8,96,512]{2,1,0:T(8,128)(2,1)S(1)}, bf16[8,96,512]{2,1,0:T(8,128)(2,1)S(1)}, u32[]{:S(2)}, u32[]{:S(2)}) collective-permute-start(bf16[8,96,512]{2,1,0:T(8,128)(2,1)S(1)} %get-tuple-element.198), channel_id=1, source_target_pairs={{0,4},{1,5},{2,6},{3,7},{4,0},{5,1},{6,2},{7,3},{8,12},{9,13},{10,... | collective-permute-start | bytes 2359304 | tf_op jit(solution)/shard_map/ppermute | solution.py:604
  132.9 25.7 %collective-permute-start.21 = (bf16[8,96,512]{2,1,0:T(8,128)(2,1)S(1)}, bf16[8,96,512]{2,1,0:T(8,128)(2,1)S(1)}, u32[]{:S(2)}, u32[]{:S(2)}) collective-permute-start(bf16[8,96,512]{2,1,0:T(8,128)(2,1)S(1)} %get-tuple-element.199), channel_id=1, source_target_pairs={{0,2},{1,3},{2,0},{3,1},{4,6},{5,7},{6,4},{7,5},{8,10},{9,11},{10,... | collective-permute-start | bytes 2359304 | tf_op jit(solution)/shard_map/ppermute | solution.py:604
  134.0 24.6 %collective-permute-start.22 = (bf16[8,96,512]{2,1,0:T(8,128)(2,1)S(1)}, bf16[8,96,512]{2,1,0:T(8,128)(2,1)S(1)}, u32[]{:S(2)}, u32[]{:S(2)}) collective-permute-start(bf16[8,96,512]{2,1,0:T(8,128)(2,1)S(1)} %get-tuple-element.200), channel_id=1, source_target_pairs={{0,8},{1,9},{2,10},{3,11},{4,12},{5,13},{6,14},{7,15},{8,0},{9,1},... | collective-permute-start | bytes 2359304 | tf_op jit(solution)/shard_map/ppermute | solution.py:604
  142.6 2.0 collective-permute-start.17
  143.6 11.3 %collective-permute-start.18 = (bf16[192,384]{1,0:T(8,128)(2,1)S(1)}, bf16[192,384]{1,0:T(8,128)(2,1)S(1)}, u32[]{:S(2)}, u32[]{:S(2)}) collective-permute-start(bf16[192,384]{1,0:T(8,128)(2,1)S(1)} %get-tuple-element.194), channel_id=1, source_target_pairs={{0,2},{1,3},{2,0},{3,1},{4,6},{5,7},{6,4},{7,5},{8,10},{9,11},{10,... | collective-permute-start | bytes 442376 | tf_op jit(solution)/shard_map/ppermute | solution.py:691
  144.6 13.9 %collective-permute-start.19 = (bf16[192,384]{1,0:T(8,128)(2,1)S(1)}, bf16[192,384]{1,0:T(8,128)(2,1)S(1)}, u32[]{:S(2)}, u32[]{:S(2)}) collective-permute-start(bf16[192,384]{1,0:T(8,128)(2,1)S(1)} %get-tuple-element.195), channel_id=1, source_target_pairs={{0,3},{1,2},{2,1},{3,0},{4,7},{5,6},{6,5},{7,4},{8,11},{9,10},{10,... | collective-permute-start | bytes 442376 | tf_op jit(solution)/shard_map/ppermute | solution.py:691
  159.1 14.8 %collective-permute-start.25 = (bf16[4,96,512]{2,1,0:T(8,128)(2,1)S(1)}, bf16[4,96,512]{2,1,0:T(8,128)(2,1)S(1)}, u32[]{:S(2)}, u32[]{:S(2)}) collective-permute-start(bf16[4,96,512]{2,1,0:T(8,128)(2,1)S(1)} %get-tuple-element.217), channel_id=1, source_target_pairs={{0,2},{1,3},{2,0},{3,1},{4,6},{5,7},{6,4},{7,5},{8,10},{9,11},{10,... | collective-permute-start | bytes 1179656 | tf_op jit(solution)/shard_map/ppermute | solution.py:604
  160.3 13.7 %collective-permute-start.26 = (bf16[4,96,512]{2,1,0:T(8,128)(2,1)S(1)}, bf16[4,96,512]{2,1,0:T(8,128)(2,1)S(1)}, u32[]{:S(2)}, u32[]{:S(2)}) collective-permute-start(bf16[4,96,512]{2,1,0:T(8,128)(2,1)S(1)} %get-tuple-element.218), channel_id=1, source_target_pairs={{0,8},{1,9},{2,10},{3,11},{4,12},{5,13},{6,14},{7,15},{8,0},{9,1},... | collective-permute-start | bytes 1179656 | tf_op jit(solution)/shard_map/ppermute | solution.py:604
  161.6 12.4 %collective-permute-start.27 = (bf16[4,96,512]{2,1,0:T(8,128)(2,1)S(1)}, bf16[4,96,512]{2,1,0:T(8,128)(2,1)S(1)}, u32[]{:S(2)}, u32[]{:S(2)}) collective-permute-start(bf16[4,96,512]{2,1,0:T(8,128)(2,1)S(1)} %get-tuple-element.219), channel_id=1, source_target_pairs={{0,4},{1,5},{2,6},{3,7},{4,0},{5,1},{6,2},{7,3},{8,12},{9,13},{10,... | collective-permute-start | bytes 1179656 | tf_op jit(solution)/shard_map/ppermute | solution.py:604
  161.8 12.1 %collective-permute-start.23 = (bf16[128,384]{1,0:T(8,128)(2,1)S(1)}, bf16[128,384]{1,0:T(8,128)(2,1)S(1)}, u32[]{:S(2)}, u32[]{:S(2)}) collective-permute-start(bf16[128,384]{1,0:T(8,128)(2,1)S(1)} %quarter_sum.4.refs_0_), channel_id=1, source_target_pairs={{0,4},{1,5},{2,6},{3,7},{4,0},{5,1},{6,2},{7,3},{8,12},{9,13},{10,... | collective-permute-start | bytes 294920 | tf_op jit(solution)/shard_map/ppermute | solution.py:604
  174.2 7.3 %collective-permute-start.29 = (bf16[2,96,512]{2,1,0:T(8,128)(2,1)S(1)}, bf16[2,96,512]{2,1,0:T(8,128)(2,1)S(1)}, u32[]{:S(2)}, u32[]{:S(2)}) collective-permute-start(bf16[2,96,512]{2,1,0:T(8,128)(2,1)S(1)} %get-tuple-element.231), channel_id=1, source_target_pairs={{0,8},{1,9},{2,10},{3,11},{4,12},{5,13},{6,14},{7,15},{8,0},{9,1},... | collective-permute-start | bytes 589832 | tf_op jit(solution)/shard_map/ppermute | solution.py:604
  174.5 7.1 %collective-permute-start.30 = (bf16[2,96,512]{2,1,0:T(8,128)(2,1)S(1)}, bf16[2,96,512]{2,1,0:T(8,128)(2,1)S(1)}, u32[]{:S(2)}, u32[]{:S(2)}) collective-permute-start(bf16[2,96,512]{2,1,0:T(8,128)(2,1)S(1)} %get-tuple-element.232), channel_id=1, source_target_pairs={{0,4},{1,5},{2,6},{3,7},{4,0},{5,1},{6,2},{7,3},{8,12},{9,13},{10,... | collective-permute-start | bytes 589832 | tf_op jit(solution)/shard_map/ppermute | solution.py:604
  174.7 6.8 %collective-permute-start.31 = (bf16[2,96,512]{2,1,0:T(8,128)(2,1)S(1)}, bf16[2,96,512]{2,1,0:T(8,128)(2,1)S(1)}, u32[]{:S(2)}, u32[]{:S(2)}) collective-permute-start(bf16[2,96,512]{2,1,0:T(8,128)(2,1)S(1)} %get-tuple-element.233), channel_id=1, source_target_pairs={{0,2},{1,3},{2,0},{3,1},{4,6},{5,7},{6,4},{7,5},{8,10},{9,11},{10,... | collective-permute-start | bytes 589832 | tf_op jit(solution)/shard_map/ppermute | solution.py:604
  175.1 6.4 %collective-permute-start.24 = (bf16[128,384]{1,0:T(8,128)(2,1)S(1)}, bf16[128,384]{1,0:T(8,128)(2,1)S(1)}, u32[]{:S(2)}, u32[]{:S(2)}) collective-permute-start(bf16[128,384]{1,0:T(8,128)(2,1)S(1)} %quarter_sum.5.refs_0_), channel_id=1, source_target_pairs={{0,8},{1,9},{2,10},{3,11},{4,12},{5,13},{6,14},{7,15},{8,0},{9,1},... | collective-permute-start | bytes 294920 | tf_op jit(solution)/shard_map/ppermute | solution.py:604
  181.7 27.5 %collective-permute-start.35 = (bf16[3,96,512]{2,1,0:T(8,128)(2,1)S(1)}, bf16[3,96,512]{2,1,0:T(8,128)(2,1)S(1)}, u32[]{:S(2)}, u32[]{:S(2)}) collective-permute-start(bf16[3,96,512]{2,1,0:T(8,128)(2,1)S(1)} %get-tuple-element.253), channel_id=1, source_target_pairs={{0,24},{1,25},{2,26},{3,27},{4,28},{5,29},{6,30},{7,31},{8,16},{9,... | collective-permute-start | bytes 884744 | tf_op jit(solution)/shard_map/ppermute | solution.py:604
  181.8 18.6 %collective-permute-start.28 = (bf16[128,384]{1,0:T(8,128)(2,1)S(1)}, bf16[128,384]{1,0:T(8,128)(2,1)S(1)}, u32[]{:S(2)}, u32[]{:S(2)}) collective-permute-start(bf16[128,384]{1,0:T(8,128)(2,1)S(1)} %quarter_sum.6.refs_0_), channel_id=1, source_target_pairs={{0,24},{1,25},{2,26},{3,27},{4,28},{5,29},{6,30},{7,31},{8,16},{9,... | collective-permute-start | bytes 294920 | tf_op jit(solution)/shard_map/ppermute | solution.py:604
  200.4 4.8 %collective-permute-start.34 = (bf16[128,384]{1,0:T(8,128)(2,1)S(1)}, bf16[128,384]{1,0:T(8,128)(2,1)S(1)}, u32[]{:S(2)}, u32[]{:S(2)}) collective-permute-start(bf16[128,384]{1,0:T(8,128)(2,1)S(1)} %quarter_sum.7.q0), channel_id=1, source_target_pairs={{0,3},{1,2},{2,1},{3,0},{4,7},{5,6},{6,5},{7,4},{8,11},{9,10},{10,... | collective-permute-start | bytes 294920 | tf_op jit(solution)/shard_map/ppermute | solution.py:687
  202.1 5.6 %collective-permute-start.33 = (bf16[128,384]{1,0:T(8,128)(2,1)S(1)}, bf16[128,384]{1,0:T(8,128)(2,1)S(1)}, u32[]{:S(2)}, u32[]{:S(2)}) collective-permute-start(bf16[128,384]{1,0:T(8,128)(2,1)S(1)} %quarter_sum.7.q0), channel_id=1, source_target_pairs={{0,2},{1,3},{2,0},{3,1},{4,6},{5,7},{6,4},{7,5},{8,10},{9,11},{10,... | collective-permute-start | bytes 294920 | tf_op jit(solution)/shard_map/ppermute | solution.py:687
  203.2 4.5 %collective-permute-start.32 = (bf16[128,384]{1,0:T(8,128)(2,1)S(1)}, bf16[128,384]{1,0:T(8,128)(2,1)S(1)}, u32[]{:S(2)}, u32[]{:S(2)}) collective-permute-start(bf16[128,384]{1,0:T(8,128)(2,1)S(1)} %quarter_sum.7.q0), channel_id=1, source_target_pairs={{0,1},{1,0},{2,3},{3,2},{4,5},{5,4},{6,7},{7,6},{8,9},{9,8},{10,11... | collective-permute-start | bytes 294920 | tf_op jit(solution)/shard_map/ppermute | solution.py:687
  (12 other events, 17.7 us)

commit v3 on v2

--- a/solution.py
+++ b/solution.py
@@ -76,7 +76,7 @@
         in_specs=[pl.BlockSpec((images // steps, width, patches), lambda i: (i, 0, 0))],
         out_specs=whole((2, images, patches)),
         out_shape=shape((2, images, patches)),
-        compiler_params=pltpu.CompilerParams(vmem_limit_bytes=LIMIT),
+        compiler_params=pltpu.CompilerParams(vmem_limit_bytes=LIMIT * 16 // 60),
         cost_estimate=cost(0),
         name="stats",
     )(tok)
@@ -108,7 +108,7 @@
 
 
 def token_kernel(me, keep, t0, t1, t2, t3, tok, w_in, b_in, w_outT, b_out, g1, c1,
-                 act, gp, s0, s1, s2, s3, mr, left, wide, biasb, gcol, mix, rhs, buf, *, first, P_, PP):
+                 s0, s1, s2, s3, mr, left, wide, biasb, gcol, mix, rhs, buf, *, first, P_, PP):
     _, width, S = tok.shape
     K = w_in.shape[1]
     p = pl.program_id(0)
@@ -135,13 +135,10 @@
         r = mr[1, pl.ds(b, 1), :]
         mix[pl.ds(i * width, width), :] = (((raw.astype(F32) - m) * r) * gcol[0] + gcol[1]).astype(BF16)
         rhs[pl.ds(i * width, width), K:K + S] = raw
-    g, d = gelu_pair(nn(mix[...], w_in[...]) + b_in[...])
+    g, _ = gelu_pair(nn(mix[...], w_in[...]) + b_in[...])
     k0, k1 = keep[first + 2 * p], keep[first + 2 * p + 1]
     rows = lax.broadcasted_iota(jnp.int32, (2 * width, 1), 0)
-    a = (g * jnp.where(rows < width, k0, k1)).astype(BF16)
-    rhs[:, 0:K] = a
-    act[...] = a
-    gp[...] = d.astype(BF16)
+    rhs[:, 0:K] = (g * jnp.where(rows < width, k0, k1)).astype(BF16)
     lanes = lax.broadcasted_iota(jnp.int32, (1, 2 * width), 1)
     out = nt(left[...], rhs[...]) + biasb[...] * jnp.where(lanes < width, k0, k1)
     for j in range(4):
@@ -155,7 +152,6 @@
     nb = images // 2
     K = w_in.shape[1]
     piece = shape((nb // 2, PP, 2 * width), BF16)
-    rows = pl.BlockSpec((2 * width, K), lambda i: (i, 0))
     send = pl.BlockSpec((1, PP, 2 * width), lambda i: (i, 0, 0))
     return pl.pallas_call(
         functools.partial(token_kernel, first=half * nb, P_=P_, PP=PP),
@@ -163,12 +159,12 @@
         in_specs=[SMEM, SMEM] + [whole(stats[0].shape)] * 4
                  + [pl.BlockSpec((2, width, S), lambda i: (half * (nb // 2) + i, 0, 0)), whole(w_in.shape), whole(b_in.shape),
                     whole(w_outT.shape), whole(b_out.shape), whole(g1.shape), whole(c1.shape)],
-        out_specs=[rows, rows, send, send, send, send],
-        out_shape=[shape((nb * width, K), BF16), shape((nb * width, K), BF16), piece, piece, piece, piece],
+        out_specs=[send] * 4,
+        out_shape=[piece] * 4,
         scratch_shapes=[pltpu.VMEM((2, images, S), F32), pltpu.VMEM((4 * PP, K + 256), BF16), pltpu.VMEM((4 * PP, K), F32),
                         pltpu.VMEM((4 * PP, 2 * width), F32), pltpu.VMEM((2, width, S), F32), pltpu.VMEM((2 * width, S), BF16),
                         pltpu.VMEM((2 * width, K + 256), BF16), pltpu.VMEM((4, PP, 2 * width), BF16)],
-        compiler_params=pltpu.CompilerParams(vmem_limit_bytes=LIMIT),
+        compiler_params=pltpu.CompilerParams(vmem_limit_bytes=LIMIT * 16 // 60),
         cost_estimate=cost(half),
         name="token_forward",
     )(ids, keep, *stats, tok, w_in, b_in, w_outT, b_out, g1, c1)
@@ -200,7 +196,7 @@
         out_specs=[pl.BlockSpec((1, R, W), lambda i: (i, 0, 0)), whole((1, W))],
         out_shape=[shape((2, R, W), BF16), shape((1, W))],
         scratch_shapes=[pltpu.VMEM((R, W), F32)],
-        compiler_params=pltpu.CompilerParams(vmem_limit_bytes=LIMIT),
+        compiler_params=pltpu.CompilerParams(vmem_limit_bytes=LIMIT * 24 // 60),
         cost_estimate=cost(0),
         name="upstream",
     )(keep, cot)
@@ -212,7 +208,7 @@
         (before4, before3, _, keep4, send4, keep3, send3), refs = refs[:7], refs[7:]
     else:
         (grad4, grad3), refs = refs[:2], refs[2:]
-    (b3, out, s0, s1, s2, s3, gg, gc, x, nrm, r2s, acc_o, acc_i, bufi, bufo, ct, ct_sem), refs = refs[:17], refs[17:]
+    (b3, out, s0, s1, s2, s3, gg, gc, x, nrm, r2s, acc_o, acc_i, bufi, bufo, ct, ct_sem, ag, act, dact), refs = refs[:20], refs[20:]
     step = pl.program_id(0)
     last = pl.num_programs(0) - 1
     W = x.shape[1]
@@ -243,43 +239,53 @@
             r2s[b] = jnp.broadcast_to(rr, (PP, 128))
             acc_i[pl.ds(b * P_, PP), :] = n * g2[...] + c2[...]
         x[...] = acc_i[0:R, :].astype(BF16)
+        ag[...] = nt(og[0], w2[...])
         acc_i[...] = jnp.zeros_like(acc_i)
         acc_o[...] = jnp.broadcast_to(b2[...], acc_o.shape)
 
+    @pl.when(step > 0)
+    def _():
+        ag[...] = nt(og[0], w2[...])
+
     g, gp = gelu_pair(nn(x[...], w1[...]) + b1[...])
     a = g.astype(BF16)
-    d = (nt(og[0], w2[...]) * gp).astype(BF16)
+    d = (ag[...] * gp).astype(BF16)
     b3[...] = jnp.sum(d.astype(F32), 0, keepdims=True)
     acc_o[...] += nn(a, w2[...])
     acc_i[0:R, :] += nt(d, w1[...])
+    act[...] = a
+    dact[...] = d
+
+    def weight_grads():
+        g4 = tn(act[...], og[0])
+        g3 = tn(dact[...], x[...])
+        if not half:
+            grad4[...] = g4
+            grad3[...] = g3
+            return
+        mine_first = (ids[1] & 1) == 0
+        per = fb // (4 * blk)
+        for total, mine, other in ((g4 + old4[...], keep4, send4), (g3 + old3[...], keep3, send3)):
+            for i in range(per):
+                for y in range(2):
+                    lo = total[(i * 4 + y * 2) * blk:(i * 4 + y * 2 + 1) * blk]
+                    hi = total[(i * 4 + y * 2 + 1) * blk:(i * 4 + y * 2 + 2) * blk]
+                    at_ = (i ^ (ids[0] & (per - 1)), y ^ (ids[1] >> 1))
+                    mine[at_] = jnp.where(mine_first, lo, hi).astype(BF16)
+                    other[at_] = jnp.where(mine_first, hi, lo).astype(BF16)
+
     if half:
         load4.wait()
         load3.wait()
-        core = ids[1] & 1
-        per = fb // (4 * blk)
-        for total, mine, other in ((tn(a, og[0]) + old4[...], keep4, send4), (tn(d, x[...]) + old3[...], keep3, send3)):
-            for i in range(per):
-                for y in range(2):
-                    lo = total[(i * 4 + y * 2) * blk:(i * 4 + y * 2 + 1) * blk].astype(BF16)
-                    hi = total[(i * 4 + y * 2 + 1) * blk:(i * 4 + y * 2 + 2) * blk].astype(BF16)
-                    at_ = (i ^ (ids[0] & (per - 1)), y ^ (ids[1] >> 1))
-
-                    @pl.when(core == 0)
-                    def _(at_=at_, lo=lo, hi=hi, mine=mine, other=other):
-                        mine[at_] = lo
-                        other[at_] = hi
-
-                    @pl.when(core == 1)
-                    def _(at_=at_, lo=lo, hi=hi, mine=mine, other=other):
-                        mine[at_] = hi
-                        other[at_] = lo
-    else:
-        grad4[...] = tn(a, og[0])
-        grad3[...] = tn(d, x[...])
+
+    @pl.when(step < last)
+    def _():
+        weight_grads()
 
     @pl.when(step == last)
     def _():
         load_ct.wait()
+        weight_grads()
         gc[...] = jnp.sum(acc_i[0:R, :], 0, keepdims=True)
         total = jnp.zeros((1, W), F32)
         for p in range(nb // 2):
@@ -337,10 +343,11 @@
                       + [pin((1, W)), pin((1, W))],
             scratch_shapes=[pltpu.VMEM((R, W), BF16), pltpu.VMEM((nb, piece[1], W), F32), pltpu.VMEM((nb, piece[1], 128), F32),
                             pltpu.VMEM((R, W), F32), pltpu.VMEM((R + 8, W), F32), pltpu.VMEM((4,) + piece, BF16),
-                            pltpu.VMEM((4,) + piece, BF16), pltpu.VMEM((nb, P_, W), BF16), pltpu.SemaphoreType.DMA] + scratch),
+                            pltpu.VMEM((4,) + piece, BF16), pltpu.VMEM((nb, P_, W), BF16), pltpu.SemaphoreType.DMA, pltpu.VMEM((R, fb), F32),
+                            pltpu.VMEM((R, fb), BF16), pltpu.VMEM((R, fb), BF16)] + scratch),
         out_shape=grads + [shape((1, F)), shape(cot.shape, BF16)] + [shape(piece, BF16)] * 4 + [shape((1, W)), shape((1, W))],
         input_output_aliases={16: n + 1} if half else {},
-        compiler_params=pltpu.CompilerParams(vmem_limit_bytes=LIMIT),
+        compiler_params=pltpu.CompilerParams(vmem_limit_bytes=LIMIT * 50 // 60),
         cost_estimate=cost(1),
         name="channel_mlp",
     )(*args)
@@ -361,7 +368,7 @@
     dst[pl.ds(at_ + VEC, VEC), :] = v - hi
 
 
-def back_kernel(ids, keep, t0, t1, t2, t3, p0, p1, p2, p3, act, gp, tok, w_in, w_outT, g1, c1, *rest, half, P_, PP):
+def back_kernel(ids, keep, t0, t1, t2, t3, p0, p1, p2, p3, tok, w_in, b_in, w_outT, g1, c1, *rest, half, P_, PP):
     if half:
         before, vecs, _, rest = rest[:7], rest[7:14], rest[14], rest[15:]
         u, o0, o1, o2, o3, ps, gw1, gw2, vec, stage, quarters = rest[:11]
@@ -400,25 +407,29 @@
     lanes = lax.broadcasted_iota(jnp.int32, (1, 2 * width), 1)
     gb2[...] += sg.astype(F32) * jnp.where(lanes < width, k0, k1)
     both = tn(sg, right[...])
+    normed = []
+    for i in range(2):
+        at_ = pl.ds(first + 2 * p + i, 1)
+        n = (tok[i].astype(F32) - mr[0, at_, :]) * mr[1, at_, :]
+        mix[pl.ds(i * width, width), :] = (n * gcol[0] + gcol[1]).astype(BF16)
+        normed.append(n)
+    act, slope = gelu_pair(nn(mix[...], w_in[...]) + b_in[...])
     rows = lax.broadcasted_iota(jnp.int32, (2 * width, 1), 0)
-    pre1 = ((both[:, 0:K] * gp[...].astype(F32)) * jnp.where(rows < width, k0, k1)).astype(BF16)
+    kept = jnp.where(rows < width, k0, k1)
+    pre1 = ((both[:, 0:K] * slope) * kept).astype(BF16)
     gb1[...] += jnp.sum(pre1.astype(F32).reshape(2 * width // 8, 8, K), 0)
-    gw2[...] += nn(sg, act[...])
+    gw2[...] += nn(sg, (act * kept).astype(BF16))
     ng = nt(pre1, w_in[...])
     for i in range(2):
-        b = first + 2 * p + i
+        at_ = pl.ds(first + 2 * p + i, 1)
         part = slice(i * width, (i + 1) * width)
-        m = mr[0, pl.ds(b, 1), :]
-        r = mr[1, pl.ds(b, 1), :]
-        n = (tok[i].astype(F32) - m) * r
-        mix[pl.ds(i * width, width), :] = (n * gcol[0] + gcol[1]).astype(BF16)
-        v = ng[part, :]
+        n, v = normed[i], ng[part, :]
         gg[...] += v * n
         gc[...] += v
         e = v * gcol[0]
-        ps[0, pl.ds(b, 1), :] = jnp.sum(e, 0, keepdims=True)
-        ps[1, pl.ds(b, 1), :] = jnp.sum(e * n, 0, keepdims=True)
-        u[i] = both[part, K:K + S] + r * e
+        ps[0, at_, :] = jnp.sum(e, 0, keepdims=True)
+        ps[1, at_, :] = jnp.sum(e * n, 0, keepdims=True)
+        u[i] = both[part, K:K + S] + mr[1, at_, :] * e
     gw1[...] += tn(mix[...], pre1)
 
     @pl.when(p == pl.num_programs(0) - 1)
@@ -460,17 +471,16 @@
             o[...] = quarters[chan ^ k]
 
 
-def back_call(ids, keep, stats, pieces, act, gp, tok, w_in, w_outT, g1, c1, half, P_, PP, before, vecs, u_before):
+def back_call(ids, keep, stats, pieces, tok, w_in, b_in, w_outT, g1, c1, half, P_, PP, before, vecs, u_before):
     images, width, S = tok.shape
     nb = images // 2
     K = w_in.shape[1]
     sums = [(S, K), (4 * PP, K), (1, K), (1, 4 * PP), (1, width), (1, width)]
     quarter = (-(-(2 * PP + 2 * VEC + 2 * images) // 16) * 16, K)
-    args = [ids, keep, *stats, *pieces, act, gp, tok, w_in, w_outT, g1, c1]
-    rows = pl.BlockSpec((2 * width, K), lambda i: (i, 0))
+    args = [ids, keep, *stats, *pieces, tok, w_in, b_in, w_outT, g1, c1]
     pairs = pl.BlockSpec((2, width, S), lambda i: (half * (nb // 2) + i, 0, 0))
     in_specs = ([SMEM, SMEM] + [whole(stats[0].shape)] * 4 + [pl.BlockSpec((1, PP, 2 * width), lambda i: (i, 0, 0))] * 4
-                + [rows, rows, pairs, whole(w_in.shape), whole(w_outT.shape), whole(g1.shape), whole(c1.shape)])
+                + [pairs, whole(w_in.shape), whole(b_in.shape), whole(w_outT.shape), whole(g1.shape), whole(c1.shape)])
     outs, out_specs, scratch = [shape((images, width, S))], [pairs], []
     if half:
         args += [*before, *vecs, u_before]
@@ -712,7 +722,7 @@
     R = -(-(images // 2) * P_ // 16) * 16
     og, sum_b4 = upstream_call(keep2, cotangent, R)
     fwd = [token_call(ids, keep1, stats, tok, mix_in, row(mix_in_bias), w_outT, row(mix_out_bias), g1, c1, h, P_, PP) for h in halves]
-    arrived = [trade(f[2:6]) for f in fwd]
+    arrived = [trade(f) for f in fwd]
     weights = (chan_in, chan_out, row(chan_in_bias), row(chan_out_bias), row(ln2_gain), row(ln2_bias))
     c0 = chan_call(ids, keep2, arrived[0], cotangent, og, 0, *weights, None, dp)
     part4, part3, b3_0, out = c0[:4]
@@ -722,12 +732,13 @@
     returned = [trade(t[:4]) for t in tails]
     vecs = [b3_0, b3_1, tails[0][4], tails[1][4], tails[0][5], tails[1][5], sum_b4]
     tokens_back = functools.partial(back_call, ids, keep1, stats)
-    u, *sums = tokens_back(returned[0], *fwd[0][:2], tok, mix_in, w_outT, g1, c1, 0, P_, PP, None, None, None)
+    u, *sums = tokens_back(returned[0], tok, mix_in, row(mix_in_bias), w_outT, g1, c1, 0, P_, PP, None, None, None)
     keep4, keep3 = after((keep4, keep3), u)
-    parts = after(start_sums(keep4, send4, keep3, send3), returned[1][3])
+    parts = list(start_sums(keep4, send4, keep3, send3))
+    parts[GROUPS + 1], = after((parts[GROUPS + 1],), returned[1][3])
     pairs = send_step(parts, 0, dp)
     u, = after((u,), parts[0])
-    u, *pieces = tokens_back(returned[1], *fwd[1][:2], tok, mix_in, w_outT, g1, c1, 1, P_, PP, [*sums[1:], sums[0]], vecs, u)
+    u, *pieces = tokens_back(returned[1], tok, mix_in, row(mix_in_bias), w_outT, g1, c1, 1, P_, PP, [*sums[1:], sums[0]], vecs, u)
     pieces = trade(pieces)
     quarter = quarter_sum(pieces, PP)
     masks = [4 * m for m in reversed(masks_of(dp))]

time: 211 us -> 195 us (0.924)
  Pallas kernels: 119 us -> 107 us
  local copies, waits for them, and re-layouts: 8.7 us -> 3.55 us
    pallas_call x2, Pallas kernels: 16.6 us -> 11.1 us  [token_call(): pl.pallas_call(functools.partial(token_kernel, first=half * nb, P_=P_, PP...]
    pallas_call x2, Pallas kernels: 72.5 us -> 67.9 us  [chan_call(): pl.pallas_call(functools.partial(chan_kernel, nb=nb, P_=P_, R=R, half=hal...]
    ppermute x15, waiting for transfers between devices: 17.6 us -> 20.9 us  [trade(): lax.ppermute(pieces[k], 'chan', [(i, i ^ k) for i in range(4)])]
    unnamed x80 -> x42, local copies, waits for them, and re-layouts: 6.39 us -> 3.54 us
    ppermute x15, waiting for transfers between devices: 29.8 us -> 27.1 us  [swap(): lax.ppermute(v, ('dp', 'chan'), [(i, i ^ mask) for i in range(world)])]
    pallas_call x1, Pallas kernels: 4.09 us -> 1.61 us  [stats_call(): pl.pallas_call(stats_kernel, grid=(steps,), in_specs=[pl.BlockSpec((image...]
    reshape x4, local copies, waits for them, and re-layouts: 2.31 us -> 0.02 us  [shards(): row = lambda v: v.reshape(1, -1)]
  transfers between devices with their start and end apart: 36 -> 36, of which waited for: 9 -> 11; matrix products, arithmetic and copies ran while one was open for 2% -> 0% of each run, Pallas kernels for 50% -> 50%
where the time goes in v3:
time: 195 us
  Pallas kernels  107 us (55%)
  waiting for transfers between devices  53.3 us (27%)
  starting transfers between devices  29.4 us (15%)
  local copies, waits for them, and re-layouts  3.55 us (2%)
    pallas_call x2, Pallas kernels, chan_call(): pl.pallas_call(functools.partial(chan_kernel, nb=nb, P_=P_, R=R, half=hal...  67.9 us
    ppermute x15, waiting for transfers between devices, swap(): lax.ppermute(v, ('dp', 'chan'), [(i, i ^ mask) for i in range(world)])  27.1 us
    ppermute x15, waiting for transfers between devices, trade(): lax.ppermute(pieces[k], 'chan', [(i, i ^ k) for i in range(4)])  20.9 us
    pallas_call x2, Pallas kernels, back_call(): pl.pallas_call(functools.partial(back_kernel, half=half, P_=P_, PP=PP), g...  17.2 us
    ppermute x15, starting transfers between devices, swap(): lax.ppermute(v, ('dp', 'chan'), [(i, i ^ mask) for i in range(world)])  12.9 us
    pallas_call x2, Pallas kernels, token_call(): pl.pallas_call(functools.partial(token_kernel, first=half * nb, P_=P_, PP...  11.1 us
    ppermute x15, starting transfers between devices, trade(): lax.ppermute(pieces[k], 'chan', [(i, i ^ k) for i in range(4)])  10.6 us
    ppermute x6, starting transfers between devices, exchange(): lax.ppermute(value, 'chan', [(i, i ^ k) for i in range(4)])  5.92 us
  transfers between devices with their start and end apart: 36, of which 11 were waited for; matrix products, arithmetic and copies ran while one was open for 0% of the time, Pallas kernels for 50%

profile of v3, /device:TPU:17, one launch (start us, length us, event | category | flops | bytes accessed | tf_op | source)
XLA Modules:
  0.0 194.6 jit_solution(13173773740415998315)
XLA Ops:
  0.7 1.8 copy-done
  2.5 1.6 stats.1.t0
  4.1 1.9 collective-permute-start.2
  6.0 0.2 collective-permute-start.1
  6.2 0.2 collective-permute-start
  6.5 0.1 pad_add_fusion.me.refs_0_.ids
  6.5 1.7 copy-done.2
  8.2 1.6 upstream.1
  9.9 0.2 collective-permute-done.1.t2
  10.1 5.6 %token_forward.3 = (bf16[7,56,384]{2,1,0:T(8,128)(2,1)S(1)}, bf16[7,56,384]{2,1,0:T(8,128)(2,1)S(1)}, bf16[7,56,384]{2,1,0:T(8,128)(2,1)S(1)}, bf16[7,56,384]{2,1,0:T(8,128)(2,1)S(1)}) custom-call(s32[2]{0:T(128)S(1)} %pad_add_fusion.me.refs_0_.ids, f32[28]{0:T(128)S(1)} %get-tuple-element.244.keep, f32[2,28,196]{2,1,0:T(8,128)S(1)} %stats.1.t0, ...), custom_call_target="tpu_custom_call" | custom-call | flops 1 | bytes 1 | tf_op jit(solution)/shard_map/token_forward/pallas_call | solution.py:156
  15.7 0.7 collective-permute-start.6
  16.3 1.2 collective-permute-start.7
  17.6 0.5 collective-permute-start.8
  18.1 5.5 %token_forward.2 = (bf16[7,56,384]{2,1,0:T(8,128)(2,1)S(1)}, bf16[7,56,384]{2,1,0:T(8,128)(2,1)S(1)}, bf16[7,56,384]{2,1,0:T(8,128)(2,1)S(1)}, bf16[7,56,384]{2,1,0:T(8,128)(2,1)S(1)}) custom-call(s32[2]{0:T(128)S(1)} %pad_add_fusion.me.refs_0_.ids, f32[28]{0:T(128)S(1)} %get-tuple-element.244.keep, f32[2,28,196]{2,1,0:T(8,128)S(1)} %stats.1.t0, ...), custom_call_target="tpu_custom_call" | custom-call | flops 99999997952 | bytes 1 | tf_op jit(solution)/shard_map/token_forward/pallas_call | solution.py:156
  23.6 0.2 collective-permute-start.3
  23.9 1.2 collective-permute-start.4
  25.1 0.8 collective-permute-start.5
  25.8 6.3 %collective-permute-done.8.refs_5_ = bf16[7,56,384]{2,1,0:T(8,128)(2,1)S(1)} collective-permute-done((bf16[7,56,384]{2,1,0:T(8,128)(2,1)S(1)}, bf16[7,56,384]{2,1,0:T(8,128)(2,1)S(1)}, u32[]{:S(2)}, u32[]{:S(2)}) %collective-permute-start.8) | collective-permute-done | bytes 301088 | tf_op jit(solution)/shard_map/ppermute | solution.py:701
  32.1 33.8 %channel_mlp.2 = (f32[3072,768]{1,0:T(8,128)}, f32[3072,768]{1,0:T(8,128)}, f32[1,3072]{1,0:T(1,128)S(1)}, bf16[28,49,768]{2,1,0:T(8,128)(2,1)}, bf16[7,56,384]{...) custom-call(s32[2]{0:T(128)S(1)} %pad_add_fusion.me.refs_0_.ids, ...), custom_call_target="tpu_custom_call" | custom-call | flops 99999997952 | bytes 1 | tf_op jit(solution)/shard_map/channel_mlp/pallas_call | solution.py:338
  66.0 0.1 collective-permute-start.12
  66.1 1.3 collective-permute-start.13
  67.4 0.8 collective-permute-start.14
  68.2 34.1 %channel_mlp.3 = (bf16[8,2,96,768]{3,2,1,0:T(8,128)(2,1)}, bf16[8,2,96,768]{3,2,1,0:T(8,128)(2,1)}, bf16[8,2,96,768]{3,2,1,0:T(8,128)(2,1)}, bf16[8,2,96,768]{3,...) custom-call(s32[2]{0:T(128)S(1)} %pad_add_fusion.me.refs_0_.ids, ...), custom_call_target="tpu_custom_call", output_to_operand_aliasing={{5}: (16, {})} | custom-call | flops 99999997952 | bytes 1 | tf_op jit(solution)/shard_map/channel_mlp/pallas_call | solution.py:338
  102.3 0.1 collective-permute-start.9
  102.4 1.3 collective-permute-start.10
  103.7 0.8 collective-permute-start.11
  104.6 0.5 collective-permute-start.16
  105.1 8.6 %token_backward.2 = (f32[28,192,196]{2,1,0:T(8,128)S(1)}, f32[2,28,196]{2,1,0:T(8,128)S(1)}, f32[196,384]{1,0:T(8,128)S(1)}, f32[224,384]{1,0:T(8,128)S(1)}, f32...) custom-call(s32[2]{0:T(128)S(1)} %pad_add_fusion.me.refs_0_.ids, ...), custom_call_target="tpu_custom_call" | custom-call | flops 99999997952 | bytes 1 | tf_op jit(solution)/shard_map/token_backward/pallas_call | solution.py:495
  113.8 1.1 sum_first.1
  114.8 2.9 %collective-permute-done.11.p3 = bf16[7,56,384]{2,1,0:T(8,128)(2,1)S(1)} collective-permute-done((bf16[7,56,384]{2,1,0:T(8,128)(2,1)S(1)}, bf16[7,56,384]{2,1,0:T(8,128)(2,1)S(1)}, u32[]{:S(2)}, u32[]{:S(2)}) %collective-permute-start.11) | collective-permute-done | bytes 301088 | tf_op jit(solution)/shard_map/ppermute | solution.py:701
  117.8 1.3 collective-permute-start.21
  119.0 1.2 collective-permute-start.20
  120.3 1.3 collective-permute-start.22
  121.6 8.5 %token_backward.3 = (f32[28,192,196]{2,1,0:T(8,128)S(1)}, bf16[192,384]{1,0:T(8,128)(2,1)S(1)}, bf16[192,384]{1,0:T(8,128)(2,1)S(1)}, bf16[192,384]{1,0:T(8,128)(2,1)S(1)}, bf16[192,384]{1,0:T(8,128)(2,1)S(1)}) custom-call(s32[2]{0:T(128)S(1)} %pad_add_fusion.me.refs_0_.ids, f32[28]{0:T(128)S(1)} %get-tuple-element.244.keep, ...), custom_call_target="tpu_custom_call", output_to_operand_aliasing={{0}: (30, {})} | custom-call | flops 99999997952 | bytes 1 | tf_op jit(solution)/shard_map/token_backward/pallas_call | solution.py:495
  130.1 0.7 collective-permute-start.17
  130.8 0.2 collective-permute-start.18
  131.0 0.8 collective-permute-done.17.refs_1_.s1
  131.8 0.7 collective-permute-start.19
  132.5 7.7 %collective-permute-done.18.refs_2_.s2 = bf16[192,384]{1,0:T(8,128)(2,1)S(1)} collective-permute-done((bf16[192,384]{1,0:T(8,128)(2,1)S(1)}, bf16[192,384]{1,0:T(8,128)(2,1)S(1)}, u32[]{:S(2)}, u32[]{:S(2)}) %collective-permute-start.18) | collective-permute-done | bytes 147488 | tf_op jit(solution)/shard_map/ppermute | solution.py:701
  140.2 3.2 %collective-permute-done.19.refs_3_.s3 = bf16[192,384]{1,0:T(8,128)(2,1)S(1)} collective-permute-done((bf16[192,384]{1,0:T(8,128)(2,1)S(1)}, bf16[192,384]{1,0:T(8,128)(2,1)S(1)}, u32[]{:S(2)}, u32[]{:S(2)}) %collective-permute-start.19) | collective-permute-done | bytes 147488 | tf_op jit(solution)/shard_map/ppermute | solution.py:701
  143.4 0.1 quarter_sum.4.refs_0_
  143.5 0.5 sum_next.3
  144.0 1.3 collective-permute-start.25
  145.4 1.3 collective-permute-start.26
  146.7 1.2 collective-permute-start.27
  147.9 0.3 collective-permute-start.23
  148.2 3.3 %norm_backward.1 = f32[28,192,196]{2,1,0:T(8,128)} custom-call(f32[2,28,196]{2,1,0:T(8,128)S(1)} %stats.1.t0, f32[2,28,196]{2,1,0:T(8,128)S(1)} %collective-permute-done.t1, f32[2,28,196]{2,1,0:T(8,128)S(1)} %collective-permute-done.1.t2, f32[2,28,196]{2,1,0:T(8,128)S(1)} %collective-permute-done.2.t3, bf16[192,384]{1,0:T(8,128)(2,1)S(1)} %get-tuple-element.190.refs_0_.s0, ...), custom_call_target="tpu_custom_call" | custom-call | flops 1 | bytes 1 | tf_op jit(solution)/shard_map/norm_backward/pallas_call | solution.py:531
  151.5 7.0 %collective-permute-done.23.refs_1_ = bf16[128,384]{1,0:T(8,128)(2,1)S(1)} collective-permute-done((bf16[128,384]{1,0:T(8,128)(2,1)S(1)}, bf16[128,384]{1,0:T(8,128)(2,1)S(1)}, u32[]{:S(2)}, u32[]{:S(2)}) %collective-permute-start.23) | collective-permute-done | bytes 98336 | tf_op jit(solution)/shard_map/ppermute | solution.py:614
  158.5 0.3 sum_next.4
  158.8 0.2 collective-permute-start.29
  159.0 1.2 collective-permute-start.30
  160.2 0.2 collective-permute-start.31
  160.4 1.3 collective-permute-start.24
  161.8 3.7 %collective-permute-done.24.refs_1_ = bf16[128,384]{1,0:T(8,128)(2,1)S(1)} collective-permute-done((bf16[128,384]{1,0:T(8,128)(2,1)S(1)}, bf16[128,384]{1,0:T(8,128)(2,1)S(1)}, u32[]{:S(2)}, u32[]{:S(2)}) %collective-permute-start.24) | collective-permute-done | bytes 98336 | tf_op jit(solution)/shard_map/ppermute | solution.py:614
  165.6 0.1 sum_next.5
  165.7 0.1 collective-permute-start.35
  165.8 1.5 collective-permute-start.28
  167.2 16.3 %collective-permute-done.28.refs_1_ = bf16[128,384]{1,0:T(8,128)(2,1)S(1)} collective-permute-done((bf16[128,384]{1,0:T(8,128)(2,1)S(1)}, bf16[128,384]{1,0:T(8,128)(2,1)S(1)}, u32[]{:S(2)}, u32[]{:S(2)}) %collective-permute-start.28) | collective-permute-done | bytes 98336 | tf_op jit(solution)/shard_map/ppermute | solution.py:614
  183.6 3.1 %collective-permute-start.34 = (bf16[128,384]{1,0:T(8,128)(2,1)S(1)}, bf16[128,384]{1,0:T(8,128)(2,1)S(1)}, u32[]{:S(2)}, u32[]{:S(2)}) collective-permute-start(bf16[128,384]{1,0:T(8,128)(2,1)S(1)} %quarter_sum.7.q0), channel_id=1, source_target_pairs={{0,3},{1,2},{2,1},{3,0},{4,7},{5,6},{6,5},{7,4},{8,11},{9,10},{10,... | collective-permute-start | bytes 294920 | tf_op jit(solution)/shard_map/ppermute | solution.py:697
  186.7 0.5 collective-permute-start.33
  187.2 3.0 %collective-permute-done.34.q3 = bf16[128,384]{1,0:T(8,128)(2,1)S(1)} collective-permute-done((bf16[128,384]{1,0:T(8,128)(2,1)S(1)}, bf16[128,384]{1,0:T(8,128)(2,1)S(1)}, u32[]{:S(2)}, u32[]{:S(2)}) %collective-permute-start.34) | collective-permute-done | bytes 98336 | tf_op jit(solution)/shard_map/ppermute | solution.py:697
  190.2 2.1 %collective-permute-done.33.q2 = bf16[128,384]{1,0:T(8,128)(2,1)S(1)} collective-permute-done((bf16[128,384]{1,0:T(8,128)(2,1)S(1)}, bf16[128,384]{1,0:T(8,128)(2,1)S(1)}, u32[]{:S(2)}, u32[]{:S(2)}) %collective-permute-start.33) | collective-permute-done | bytes 98336 | tf_op jit(solution)/shard_map/ppermute | solution.py:697
  192.3 1.5 unpack.1
  193.8 0.8 sum_last.1
  (75 shorter events, 0.3 us)
Async XLA Ops:
  0.6 5.8 %copy-start.20 = (s32[28,2]{0,1:T(2,128)S(1)}, s32[28,2]{0,1:T(2,128)}, u32[]{:S(2)}) copy-start(s32[28,2]{0,1:T(2,128)} %param.28) | copy-start | bytes 676
  0.7 1.8 copy-start
  2.4 7.3 %copy-start.19 = (f32[384]{0:T(512)S(1)}, f32[384]{0:T(512)}, u32[]{:S(2)}) copy-start(f32[384]{0:T(512)} %param.19) | copy-start | bytes 4612
  2.4 7.4 %copy-start.16 = (f32[768]{0:T(1024)S(1)}, f32[768]{0:T(1024)}, u32[]{:S(2)}) copy-start(f32[768]{0:T(1024)} %param.22) | copy-start | bytes 9220
  2.4 7.4 %copy-start.17 = (f32[768]{0:T(1024)S(1)}, f32[768]{0:T(1024)}, u32[]{:S(2)}) copy-start(f32[768]{0:T(1024)} %param.23) | copy-start | bytes 9220
  2.4 7.4 %copy-start.18 = (f32[768]{0:T(1024)S(1)}, f32[768]{0:T(1024)}, u32[]{:S(2)}) copy-start(f32[768]{0:T(1024)} %param.27) | copy-start | bytes 9220
  2.5 7.6 %copy-start.1 = (bf16[28,196,192]{1,2,0:T(8,128)(2,1)S(1)}, bf16[28,196,192]{1,2,0:T(8,128)(2,1)}, u32[]{:S(2)}) copy-start(bf16[28,196,192]{1,2,0:T(8,128)(2,1)} %param.15) | copy-start | bytes 6322180
  2.5 7.6 %copy-start.11 = (f32[196]{0:T(256)S(1)}, f32[196]{0:T(256)}, u32[]{:S(2)}) copy-start(f32[196]{0:T(256)} %param.21) | copy-start | bytes 2356
  2.5 7.6 %copy-start.12 = (f32[192]{0:T(256)S(1)}, f32[192]{0:T(256)}, u32[]{:S(2)}) copy-start(f32[192]{0:T(256)} %param.16) | copy-start | bytes 2308
  2.5 7.6 %copy-start.13 = (f32[192]{0:T(256)S(1)}, f32[192]{0:T(256)}, u32[]{:S(2)}) copy-start(f32[192]{0:T(256)} %param.17) | copy-start | bytes 2308
  4.1 5.8 %collective-permute-start.2 = (f32[2,28,196]{2,1,0:T(8,128)S(1)}, f32[2,28,196]{2,1,0:T(8,128)S(1)}, u32[]{:S(2)}, u32[]{:S(2)}) collective-permute-start(f32[2,28,196]{2,1,0:T(8,128)S(1)} %stats.1.t0), channel_id=1, source_target_pairs={{0,3},{1,2},{2,1},{3,0},{4,7},{5,6},{6,5},{7,4},{8,11},{9,10},{10,... | collective-permute-start | bytes 131720 | tf_op jit(solution)/shard_map/ppermute | solution.py:697
  6.0 4.1 %collective-permute-start.1 = (f32[2,28,196]{2,1,0:T(8,128)S(1)}, f32[2,28,196]{2,1,0:T(8,128)S(1)}, u32[]{:S(2)}, u32[]{:S(2)}) collective-permute-start(f32[2,28,196]{2,1,0:T(8,128)S(1)} %stats.1.t0), channel_id=1, source_target_pairs={{0,2},{1,3},{2,0},{3,1},{4,6},{5,7},{6,4},{7,5},{8,10},{9,11},{10,... | collective-permute-start | bytes 131720 | tf_op jit(solution)/shard_map/ppermute | solution.py:697
  6.2 3.9 %collective-permute-start = (f32[2,28,196]{2,1,0:T(8,128)S(1)}, f32[2,28,196]{2,1,0:T(8,128)S(1)}, u32[]{:S(2)}, u32[]{:S(2)}) collective-permute-start(f32[2,28,196]{2,1,0:T(8,128)S(1)} %stats.1.t0), channel_id=1, source_target_pairs={{0,1},{1,0},{2,3},{3,2},{4,5},{5,4},{6,7},{7,6},{8,9},{9,8},{10,11... | collective-permute-start | bytes 131720 | tf_op jit(solution)/shard_map/ppermute | solution.py:697
  6.5 1.7 copy-start.2
  8.2 1.9 copy-start.5
  8.2 1.9 copy-start.7
  9.8 13.8 %copy-start.14 = (bf16[2,688,768]{2,1,0:T(8,128)(2,1)}, bf16[2,688,768]{2,1,0:T(8,128)(2,1)S(1)}, u32[]{:S(2)}) copy-start(bf16[2,688,768]{2,1,0:T(8,128)(2,1)S(1)} %get-tuple-element.133.refs_7_) | copy-start | bytes 6340612
  9.8 13.8 %copy-start.9 = (f32[1,384]{1,0:T(1,128)}, f32[1,384]{1,0:T(1,128)S(1)}, u32[]{:S(2)}) copy-start(f32[1,384]{1,0:T(1,128)S(1)} %reshape.58.b_in) | copy-start | bytes 4612
  15.7 9.4 %collective-permute-start.6 = (bf16[7,56,384]{2,1,0:T(8,128)(2,1)S(1)}, bf16[7,56,384]{2,1,0:T(8,128)(2,1)S(1)}, u32[]{:S(2)}, u32[]{:S(2)}) collective-permute-start(bf16[7,56,384]{2,1,0:T(8,128)(2,1)S(1)} %get-tuple-element.135), channel_id=1, source_target_pairs={{0,1},{1,0},{2,3},{3,2},{4,5},{5,4},{6,7},{7,6},{8,9},{9,8},{10,11... | collective-permute-start | bytes 903176 | tf_op jit(solution)/shard_map/ppermute | solution.py:701
  16.3 9.5 %collective-permute-start.7 = (bf16[7,56,384]{2,1,0:T(8,128)(2,1)S(1)}, bf16[7,56,384]{2,1,0:T(8,128)(2,1)S(1)}, u32[]{:S(2)}, u32[]{:S(2)}) collective-permute-start(bf16[7,56,384]{2,1,0:T(8,128)(2,1)S(1)} %get-tuple-element.136), channel_id=1, source_target_pairs={{0,2},{1,3},{2,0},{3,1},{4,6},{5,7},{6,4},{7,5},{8,10},{9,11},{10,... | collective-permute-start | bytes 903176 | tf_op jit(solution)/shard_map/ppermute | solution.py:701
  17.6 14.5 %copy-start.15 = (f32[3072]{0:T(1024)S(1)}, f32[3072]{0:T(1024)}, u32[]{:S(2)}) copy-start(f32[3072]{0:T(1024)} %param.25) | copy-start | bytes 36868
  17.6 14.5 %collective-permute-start.8 = (bf16[7,56,384]{2,1,0:T(8,128)(2,1)S(1)}, bf16[7,56,384]{2,1,0:T(8,128)(2,1)S(1)}, u32[]{:S(2)}, u32[]{:S(2)}) collective-permute-start(bf16[7,56,384]{2,1,0:T(8,128)(2,1)S(1)} %get-tuple-element.137), channel_id=1, source_target_pairs={{0,3},{1,2},{2,1},{3,0},{4,7},{5,6},{6,5},{7,4},{8,11},{9,10},{10,... | collective-permute-start | bytes 903176 | tf_op jit(solution)/shard_map/ppermute | solution.py:701
  23.6 43.8 %collective-permute-start.3 = (bf16[7,56,384]{2,1,0:T(8,128)(2,1)S(1)}, bf16[7,56,384]{2,1,0:T(8,128)(2,1)S(1)}, u32[]{:S(2)}, u32[]{:S(2)}) collective-permute-start(bf16[7,56,384]{2,1,0:T(8,128)(2,1)S(1)} %get-tuple-element.130), channel_id=1, source_target_pairs={{0,1},{1,0},{2,3},{3,2},{4,5},{5,4},{6,7},{7,6},{8,9},{9,8},{10,11... | collective-permute-start | bytes 903176 | tf_op jit(solution)/shard_map/ppermute | solution.py:701
  23.9 44.3 %collective-permute-start.4 = (bf16[7,56,384]{2,1,0:T(8,128)(2,1)S(1)}, bf16[7,56,384]{2,1,0:T(8,128)(2,1)S(1)}, u32[]{:S(2)}, u32[]{:S(2)}) collective-permute-start(bf16[7,56,384]{2,1,0:T(8,128)(2,1)S(1)} %get-tuple-element.131), channel_id=1, source_target_pairs={{0,2},{1,3},{2,0},{3,1},{4,6},{5,7},{6,4},{7,5},{8,10},{9,11},{10,... | collective-permute-start | bytes 903176 | tf_op jit(solution)/shard_map/ppermute | solution.py:701
  25.1 43.1 %collective-permute-start.5 = (bf16[7,56,384]{2,1,0:T(8,128)(2,1)S(1)}, bf16[7,56,384]{2,1,0:T(8,128)(2,1)S(1)}, u32[]{:S(2)}, u32[]{:S(2)}) collective-permute-start(bf16[7,56,384]{2,1,0:T(8,128)(2,1)S(1)} %get-tuple-element.132), channel_id=1, source_target_pairs={{0,3},{1,2},{2,1},{3,0},{4,7},{5,6},{6,5},{7,4},{8,11},{9,10},{10,... | collective-permute-start | bytes 903176 | tf_op jit(solution)/shard_map/ppermute | solution.py:701
  66.0 37.7 %collective-permute-start.12 = (bf16[7,56,384]{2,1,0:T(8,128)(2,1)S(1)}, bf16[7,56,384]{2,1,0:T(8,128)(2,1)S(1)}, u32[]{:S(2)}, u32[]{:S(2)}) collective-permute-start(bf16[7,56,384]{2,1,0:T(8,128)(2,1)S(1)} %get-tuple-element.147), channel_id=1, source_target_pairs={{0,1},{1,0},{2,3},{3,2},{4,5},{5,4},{6,7},{7,6},{8,9},{9,8},{10,11... | collective-permute-start | bytes 903176 | tf_op jit(solution)/shard_map/ppermute | solution.py:701
  66.1 38.5 %collective-permute-start.13 = (bf16[7,56,384]{2,1,0:T(8,128)(2,1)S(1)}, bf16[7,56,384]{2,1,0:T(8,128)(2,1)S(1)}, u32[]{:S(2)}, u32[]{:S(2)}) collective-permute-start(bf16[7,56,384]{2,1,0:T(8,128)(2,1)S(1)} %get-tuple-element.148), channel_id=1, source_target_pairs={{0,2},{1,3},{2,0},{3,1},{4,6},{5,7},{6,4},{7,5},{8,10},{9,11},{10,... | collective-permute-start | bytes 903176 | tf_op jit(solution)/shard_map/ppermute | solution.py:701
  67.4 37.2 %collective-permute-start.14 = (bf16[7,56,384]{2,1,0:T(8,128)(2,1)S(1)}, bf16[7,56,384]{2,1,0:T(8,128)(2,1)S(1)}, u32[]{:S(2)}, u32[]{:S(2)}) collective-permute-start(bf16[7,56,384]{2,1,0:T(8,128)(2,1)S(1)} %get-tuple-element.149), channel_id=1, source_target_pairs={{0,3},{1,2},{2,1},{3,0},{4,7},{5,6},{6,5},{7,4},{8,11},{9,10},{10,... | collective-permute-start | bytes 903176 | tf_op jit(solution)/shard_map/ppermute | solution.py:701
  68.2 36.9 %copy-start.6 = (bf16[196,384]{1,0:T(8,128)(2,1)S(1)}, bf16[196,384]{1,0:T(8,128)(2,1)}, u32[]{:S(2)}) copy-start(bf16[196,384]{1,0:T(8,128)(2,1)} %w_in.7) | copy-start | bytes 451588
  68.2 36.9 %copy-start.8 = (bf16[384,196]{0,1:T(8,128)(2,1)S(1)}, bf16[384,196]{0,1:T(8,128)(2,1)}, u32[]{:S(2)}) copy-start(bf16[384,196]{0,1:T(8,128)(2,1)} %param.20) | copy-start | bytes 451588
  68.2 36.8 %copy-start.10 = (f32[1,384]{1,0:T(1,128)S(1)}, f32[1,384]{1,0:T(1,128)}, u32[]{:S(2)}) copy-start(f32[1,384]{1,0:T(1,128)} %copy-done.9) | copy-start | bytes 4612
  102.3 19.3 %collective-permute-start.9 = (bf16[7,56,384]{2,1,0:T(8,128)(2,1)S(1)}, bf16[7,56,384]{2,1,0:T(8,128)(2,1)S(1)}, u32[]{:S(2)}, u32[]{:S(2)}) collective-permute-start(bf16[7,56,384]{2,1,0:T(8,128)(2,1)S(1)} %get-tuple-element.143), channel_id=1, source_target_pairs={{0,1},{1,0},{2,3},{3,2},{4,5},{5,4},{6,7},{7,6},{8,9},{9,8},{10,11... | collective-permute-start | bytes 903176 | tf_op jit(solution)/shard_map/ppermute | solution.py:701
  102.4 19.2 %collective-permute-start.10 = (bf16[7,56,384]{2,1,0:T(8,128)(2,1)S(1)}, bf16[7,56,384]{2,1,0:T(8,128)(2,1)S(1)}, u32[]{:S(2)}, u32[]{:S(2)}) collective-permute-start(bf16[7,56,384]{2,1,0:T(8,128)(2,1)S(1)} %get-tuple-element.144), channel_id=1, source_target_pairs={{0,2},{1,3},{2,0},{3,1},{4,6},{5,7},{6,4},{7,5},{8,10},{9,11},{10,... | collective-permute-start | bytes 903176 | tf_op jit(solution)/shard_map/ppermute | solution.py:701
  103.7 14.1 %collective-permute-start.11 = (bf16[7,56,384]{2,1,0:T(8,128)(2,1)S(1)}, bf16[7,56,384]{2,1,0:T(8,128)(2,1)S(1)}, u32[]{:S(2)}, u32[]{:S(2)}) collective-permute-start(bf16[7,56,384]{2,1,0:T(8,128)(2,1)S(1)} %get-tuple-element.145), channel_id=1, source_target_pairs={{0,3},{1,2},{2,1},{3,0},{4,7},{5,6},{6,5},{7,4},{8,11},{9,10},{10,... | collective-permute-start | bytes 903176 | tf_op jit(solution)/shard_map/ppermute | solution.py:701
  104.5 9.2 %collective-permute-start.15 = (bf16[8,2,96,768]{3,2,1,0:T(8,128)(2,1)}, bf16[8,2,96,768]{3,2,1,0:T(8,128)(2,1)S(1)}, u32[]{:S(2)}, u32[]{:S(2)}) collective-permute-start(bf16[8,2,96,768]{3,2,1,0:T(8,128)(2,1)} %get-tuple-element.168), channel_id=1, source_target_pairs={{0,1},{1,0},{2,3},{3,2},{4,5},{5,4},{6,7},{7,6},{8,9},{9,8},{10,11... | collective-permute-start | bytes 7077896 | tf_op jit(solution)/shard_map/ppermute | solution.py:614
  104.6 9.2 %collective-permute-start.16 = (bf16[8,2,96,768]{3,2,1,0:T(8,128)(2,1)}, bf16[8,2,96,768]{3,2,1,0:T(8,128)(2,1)S(1)}, u32[]{:S(2)}, u32[]{:S(2)}) collective-permute-start(bf16[8,2,96,768]{3,2,1,0:T(8,128)(2,1)} %get-tuple-element.170), channel_id=1, source_target_pairs={{0,1},{1,0},{2,3},{3,2},{4,5},{5,4},{6,7},{7,6},{8,9},{9,8},{10,11... | collective-permute-start | bytes 7077896 | tf_op jit(solution)/shard_map/ppermute | solution.py:614
  105.1 8.7 %copy-start.3 = (bf16[8,2,96,768]{3,2,1,0:T(8,128)(2,1)S(1)}, bf16[8,2,96,768]{3,2,1,0:T(8,128)(2,1)}, u32[]{:S(2)}) copy-start(bf16[8,2,96,768]{3,2,1,0:T(8,128)(2,1)} %get-tuple-element.167.k4) | copy-start | bytes 7077892
  105.1 8.7 %copy-start.4 = (bf16[8,2,96,768]{3,2,1,0:T(8,128)(2,1)S(1)}, bf16[8,2,96,768]{3,2,1,0:T(8,128)(2,1)}, u32[]{:S(2)}) copy-start(bf16[8,2,96,768]{3,2,1,0:T(8,128)(2,1)} %get-tuple-element.169.k3) | copy-start | bytes 7077892
  117.8 25.7 %collective-permute-start.21 = (bf16[8,96,512]{2,1,0:T(8,128)(2,1)S(1)}, bf16[8,96,512]{2,1,0:T(8,128)(2,1)S(1)}, u32[]{:S(2)}, u32[]{:S(2)}) collective-permute-start(bf16[8,96,512]{2,1,0:T(8,128)(2,1)S(1)} %get-tuple-element.181), channel_id=1, source_target_pairs={{0,2},{1,3},{2,0},{3,1},{4,6},{5,7},{6,4},{7,5},{8,10},{9,11},{10,... | collective-permute-start | bytes 2359304 | tf_op jit(solution)/shard_map/ppermute | solution.py:614
  119.0 24.4 %collective-permute-start.20 = (bf16[8,96,512]{2,1,0:T(8,128)(2,1)S(1)}, bf16[8,96,512]{2,1,0:T(8,128)(2,1)S(1)}, u32[]{:S(2)}, u32[]{:S(2)}) collective-permute-start(bf16[8,96,512]{2,1,0:T(8,128)(2,1)S(1)} %get-tuple-element.179), channel_id=1, source_target_pairs={{0,4},{1,5},{2,6},{3,7},{4,0},{5,1},{6,2},{7,3},{8,12},{9,13},{10,... | collective-permute-start | bytes 2359304 | tf_op jit(solution)/shard_map/ppermute | solution.py:614
  120.3 23.2 %collective-permute-start.22 = (bf16[8,96,512]{2,1,0:T(8,128)(2,1)S(1)}, bf16[8,96,512]{2,1,0:T(8,128)(2,1)S(1)}, u32[]{:S(2)}, u32[]{:S(2)}) collective-permute-start(bf16[8,96,512]{2,1,0:T(8,128)(2,1)S(1)} %get-tuple-element.182), channel_id=1, source_target_pairs={{0,8},{1,9},{2,10},{3,11},{4,12},{5,13},{6,14},{7,15},{8,0},{9,1},... | collective-permute-start | bytes 2359304 | tf_op jit(solution)/shard_map/ppermute | solution.py:614
  130.1 1.7 collective-permute-start.17
  130.8 9.4 %collective-permute-start.18 = (bf16[192,384]{1,0:T(8,128)(2,1)S(1)}, bf16[192,384]{1,0:T(8,128)(2,1)S(1)}, u32[]{:S(2)}, u32[]{:S(2)}) collective-permute-start(bf16[192,384]{1,0:T(8,128)(2,1)S(1)} %get-tuple-element.175), channel_id=1, source_target_pairs={{0,2},{1,3},{2,0},{3,1},{4,6},{5,7},{6,4},{7,5},{8,10},{9,11},{10,... | collective-permute-start | bytes 442376 | tf_op jit(solution)/shard_map/ppermute | solution.py:701
  131.8 11.6 %collective-permute-start.19 = (bf16[192,384]{1,0:T(8,128)(2,1)S(1)}, bf16[192,384]{1,0:T(8,128)(2,1)S(1)}, u32[]{:S(2)}, u32[]{:S(2)}) collective-permute-start(bf16[192,384]{1,0:T(8,128)(2,1)S(1)} %get-tuple-element.176), channel_id=1, source_target_pairs={{0,3},{1,2},{2,1},{3,0},{4,7},{5,6},{6,5},{7,4},{8,11},{9,10},{10,... | collective-permute-start | bytes 442376 | tf_op jit(solution)/shard_map/ppermute | solution.py:701
  144.0 14.5 %collective-permute-start.25 = (bf16[4,96,512]{2,1,0:T(8,128)(2,1)S(1)}, bf16[4,96,512]{2,1,0:T(8,128)(2,1)S(1)}, u32[]{:S(2)}, u32[]{:S(2)}) collective-permute-start(bf16[4,96,512]{2,1,0:T(8,128)(2,1)S(1)} %get-tuple-element.199), channel_id=1, source_target_pairs={{0,2},{1,3},{2,0},{3,1},{4,6},{5,7},{6,4},{7,5},{8,10},{9,11},{10,... | collective-permute-start | bytes 1179656 | tf_op jit(solution)/shard_map/ppermute | solution.py:614
  145.4 13.1 %collective-permute-start.26 = (bf16[4,96,512]{2,1,0:T(8,128)(2,1)S(1)}, bf16[4,96,512]{2,1,0:T(8,128)(2,1)S(1)}, u32[]{:S(2)}, u32[]{:S(2)}) collective-permute-start(bf16[4,96,512]{2,1,0:T(8,128)(2,1)S(1)} %get-tuple-element.200), channel_id=1, source_target_pairs={{0,8},{1,9},{2,10},{3,11},{4,12},{5,13},{6,14},{7,15},{8,0},{9,1},... | collective-permute-start | bytes 1179656 | tf_op jit(solution)/shard_map/ppermute | solution.py:614
  146.7 11.8 %collective-permute-start.27 = (bf16[4,96,512]{2,1,0:T(8,128)(2,1)S(1)}, bf16[4,96,512]{2,1,0:T(8,128)(2,1)S(1)}, u32[]{:S(2)}, u32[]{:S(2)}) collective-permute-start(bf16[4,96,512]{2,1,0:T(8,128)(2,1)S(1)} %get-tuple-element.201), channel_id=1, source_target_pairs={{0,4},{1,5},{2,6},{3,7},{4,0},{5,1},{6,2},{7,3},{8,12},{9,13},{10,... | collective-permute-start | bytes 1179656 | tf_op jit(solution)/shard_map/ppermute | solution.py:614
  147.9 10.6 %collective-permute-start.23 = (bf16[128,384]{1,0:T(8,128)(2,1)S(1)}, bf16[128,384]{1,0:T(8,128)(2,1)S(1)}, u32[]{:S(2)}, u32[]{:S(2)}) collective-permute-start(bf16[128,384]{1,0:T(8,128)(2,1)S(1)} %quarter_sum.4.refs_0_), channel_id=1, source_target_pairs={{0,4},{1,5},{2,6},{3,7},{4,0},{5,1},{6,2},{7,3},{8,12},{9,13},{10,... | collective-permute-start | bytes 294920 | tf_op jit(solution)/shard_map/ppermute | solution.py:614
  158.8 6.7 %collective-permute-start.29 = (bf16[2,96,512]{2,1,0:T(8,128)(2,1)S(1)}, bf16[2,96,512]{2,1,0:T(8,128)(2,1)S(1)}, u32[]{:S(2)}, u32[]{:S(2)}) collective-permute-start(bf16[2,96,512]{2,1,0:T(8,128)(2,1)S(1)} %get-tuple-element.213), channel_id=1, source_target_pairs={{0,8},{1,9},{2,10},{3,11},{4,12},{5,13},{6,14},{7,15},{8,0},{9,1},... | collective-permute-start | bytes 589832 | tf_op jit(solution)/shard_map/ppermute | solution.py:614
  159.0 6.5 %collective-permute-start.30 = (bf16[2,96,512]{2,1,0:T(8,128)(2,1)S(1)}, bf16[2,96,512]{2,1,0:T(8,128)(2,1)S(1)}, u32[]{:S(2)}, u32[]{:S(2)}) collective-permute-start(bf16[2,96,512]{2,1,0:T(8,128)(2,1)S(1)} %get-tuple-element.214), channel_id=1, source_target_pairs={{0,4},{1,5},{2,6},{3,7},{4,0},{5,1},{6,2},{7,3},{8,12},{9,13},{10,... | collective-permute-start | bytes 589832 | tf_op jit(solution)/shard_map/ppermute | solution.py:614
  160.2 5.3 %collective-permute-start.31 = (bf16[2,96,512]{2,1,0:T(8,128)(2,1)S(1)}, bf16[2,96,512]{2,1,0:T(8,128)(2,1)S(1)}, u32[]{:S(2)}, u32[]{:S(2)}) collective-permute-start(bf16[2,96,512]{2,1,0:T(8,128)(2,1)S(1)} %get-tuple-element.215), channel_id=1, source_target_pairs={{0,2},{1,3},{2,0},{3,1},{4,6},{5,7},{6,4},{7,5},{8,10},{9,11},{10,... | collective-permute-start | bytes 589832 | tf_op jit(solution)/shard_map/ppermute | solution.py:614
  160.4 5.1 %collective-permute-start.24 = (bf16[128,384]{1,0:T(8,128)(2,1)S(1)}, bf16[128,384]{1,0:T(8,128)(2,1)S(1)}, u32[]{:S(2)}, u32[]{:S(2)}) collective-permute-start(bf16[128,384]{1,0:T(8,128)(2,1)S(1)} %quarter_sum.5.refs_0_), channel_id=1, source_target_pairs={{0,8},{1,9},{2,10},{3,11},{4,12},{5,13},{6,14},{7,15},{8,0},{9,1},... | collective-permute-start | bytes 294920 | tf_op jit(solution)/shard_map/ppermute | solution.py:614
  165.7 28.1 %collective-permute-start.35 = (bf16[3,96,512]{2,1,0:T(8,128)(2,1)S(1)}, bf16[3,96,512]{2,1,0:T(8,128)(2,1)S(1)}, u32[]{:S(2)}, u32[]{:S(2)}) collective-permute-start(bf16[3,96,512]{2,1,0:T(8,128)(2,1)S(1)} %get-tuple-element.235), channel_id=1, source_target_pairs={{0,24},{1,25},{2,26},{3,27},{4,28},{5,29},{6,30},{7,31},{8,16},{9,... | collective-permute-start | bytes 884744 | tf_op jit(solution)/shard_map/ppermute | solution.py:614
  165.8 17.8 %collective-permute-start.28 = (bf16[128,384]{1,0:T(8,128)(2,1)S(1)}, bf16[128,384]{1,0:T(8,128)(2,1)S(1)}, u32[]{:S(2)}, u32[]{:S(2)}) collective-permute-start(bf16[128,384]{1,0:T(8,128)(2,1)S(1)} %quarter_sum.6.refs_0_), channel_id=1, source_target_pairs={{0,24},{1,25},{2,26},{3,27},{4,28},{5,29},{6,30},{7,31},{8,16},{9,... | collective-permute-start | bytes 294920 | tf_op jit(solution)/shard_map/ppermute | solution.py:614
  183.6 6.6 %collective-permute-start.34 = (bf16[128,384]{1,0:T(8,128)(2,1)S(1)}, bf16[128,384]{1,0:T(8,128)(2,1)S(1)}, u32[]{:S(2)}, u32[]{:S(2)}) collective-permute-start(bf16[128,384]{1,0:T(8,128)(2,1)S(1)} %quarter_sum.7.q0), channel_id=1, source_target_pairs={{0,3},{1,2},{2,1},{3,0},{4,7},{5,6},{6,5},{7,4},{8,11},{9,10},{10,... | collective-permute-start | bytes 294920 | tf_op jit(solution)/shard_map/ppermute | solution.py:697
  186.7 5.6 %collective-permute-start.33 = (bf16[128,384]{1,0:T(8,128)(2,1)S(1)}, bf16[128,384]{1,0:T(8,128)(2,1)S(1)}, u32[]{:S(2)}, u32[]{:S(2)}) collective-permute-start(bf16[128,384]{1,0:T(8,128)(2,1)S(1)} %quarter_sum.7.q0), channel_id=1, source_target_pairs={{0,2},{1,3},{2,0},{3,1},{4,6},{5,7},{6,4},{7,5},{8,10},{9,11},{10,... | collective-permute-start | bytes 294920 | tf_op jit(solution)/shard_map/ppermute | solution.py:697
  187.2 5.1 %collective-permute-start.32 = (bf16[128,384]{1,0:T(8,128)(2,1)S(1)}, bf16[128,384]{1,0:T(8,128)(2,1)S(1)}, u32[]{:S(2)}, u32[]{:S(2)}) collective-permute-start(bf16[128,384]{1,0:T(8,128)(2,1)S(1)} %quarter_sum.7.q0), channel_id=1, source_target_pairs={{0,1},{1,0},{2,3},{3,2},{4,5},{5,4},{6,7},{7,6},{8,9},{9,8},{10,11... | collective-permute-start | bytes 294920 | tf_op jit(solution)/shard_map/ppermute | solution.py:697

commit v4 on v3

--- a/solution.py
+++ b/solution.py
@@ -735,7 +735,6 @@
     u, *sums = tokens_back(returned[0], tok, mix_in, row(mix_in_bias), w_outT, g1, c1, 0, P_, PP, None, None, None)
     keep4, keep3 = after((keep4, keep3), u)
     parts = list(start_sums(keep4, send4, keep3, send3))
-    parts[GROUPS + 1], = after((parts[GROUPS + 1],), returned[1][3])
     pairs = send_step(parts, 0, dp)
     u, = after((u,), parts[0])
     u, *pieces = tokens_back(returned[1], tok, mix_in, row(mix_in_bias), w_outT, g1, c1, 1, P_, PP, [*sums[1:], sums[0]], vecs, u)

time: 195 us -> 194 us (level)
    ppermute x15, waiting for transfers between devices: 27.1 us -> 29.9 us  [swap(): lax.ppermute(v, ('dp', 'chan'), [(i, i ^ mask) for i in range(world)])]
    ppermute x15, waiting for transfers between devices: 20.9 us -> 18.9 us  [trade(): lax.ppermute(pieces[k], 'chan', [(i, i ^ k) for i in range(4)])]
  transfers between devices with their start and end apart: 36 -> 36, of which waited for: 11 -> 10; matrix products, arithmetic and copies ran while one was open for 0% -> 0% of each run, Pallas kernels for 50% -> 51%
where the time goes in v4:
time: 194 us; the launch traced here: 193 us
  Pallas kernels  107 us (55%)
  waiting for transfers between devices  53.4 us (28%)
  starting transfers between devices  28 us (14%)
  local copies, waits for them, and re-layouts  3.55 us (2%)
    pallas_call x2, Pallas kernels, chan_call(): pl.pallas_call(functools.partial(chan_kernel, nb=nb, P_=P_, R=R, half=hal...  67.9 us
    ppermute x15, waiting for transfers between devices, swap(): lax.ppermute(v, ('dp', 'chan'), [(i, i ^ mask) for i in range(world)])  29.9 us
    ppermute x15, waiting for transfers between devices, trade(): lax.ppermute(pieces[k], 'chan', [(i, i ^ k) for i in range(4)])  18.9 us
    pallas_call x2, Pallas kernels, back_call(): pl.pallas_call(functools.partial(back_kernel, half=half, P_=P_, PP=PP), g...  17.2 us
    ppermute x15, starting transfers between devices, swap(): lax.ppermute(v, ('dp', 'chan'), [(i, i ^ mask) for i in range(world)])  11.9 us
    pallas_call x2, Pallas kernels, token_call(): pl.pallas_call(functools.partial(token_kernel, first=half * nb, P_=P_, PP...  11.1 us
    ppermute x15, starting transfers between devices, trade(): lax.ppermute(pieces[k], 'chan', [(i, i ^ k) for i in range(4)])  10.9 us
    ppermute x6, starting transfers between devices, exchange(): lax.ppermute(value, 'chan', [(i, i ^ k) for i in range(4)])  5.14 us
  transfers between devices with their start and end apart: 36, of which 10 were waited for; matrix products, arithmetic and copies ran while one was open for 0% of the time, Pallas kernels for 51%

profile of v4, /device:TPU:17, one launch (start us, length us, event | category | flops | bytes accessed | tf_op | source)
XLA Modules:
  0.0 193.3 jit_solution(14989650764208220854)
XLA Ops:
  0.7 1.8 copy-done
  2.5 1.6 stats.1.t0
  4.1 1.9 collective-permute-start.2
  6.0 0.2 collective-permute-start.1
  6.2 0.2 collective-permute-start
  6.5 0.1 pad_add_fusion.me.refs_0_.ids
  6.5 1.7 copy-done.2
  8.2 1.6 upstream.1
  9.9 0.2 collective-permute-done.1.t2
  10.1 5.6 %token_forward.3 = (bf16[7,56,384]{2,1,0:T(8,128)(2,1)S(1)}, bf16[7,56,384]{2,1,0:T(8,128)(2,1)S(1)}, bf16[7,56,384]{2,1,0:T(8,128)(2,1)S(1)}, bf16[7,56,384]{2,1,0:T(8,128)(2,1)S(1)}) custom-call(s32[2]{0:T(128)S(1)} %pad_add_fusion.me.refs_0_.ids, f32[28]{0:T(128)S(1)} %get-tuple-element.242.keep, f32[2,28,196]{2,1,0:T(8,128)S(1)} %stats.1.t0, ...), custom_call_target="tpu_custom_call" | custom-call | flops 1 | bytes 1 | tf_op jit(solution)/shard_map/token_forward/pallas_call | solution.py:156
  15.7 0.7 collective-permute-start.6
  16.3 1.2 collective-permute-start.7
  17.6 0.5 collective-permute-start.8
  18.1 5.5 %token_forward.2 = (bf16[7,56,384]{2,1,0:T(8,128)(2,1)S(1)}, bf16[7,56,384]{2,1,0:T(8,128)(2,1)S(1)}, bf16[7,56,384]{2,1,0:T(8,128)(2,1)S(1)}, bf16[7,56,384]{2,1,0:T(8,128)(2,1)S(1)}) custom-call(s32[2]{0:T(128)S(1)} %pad_add_fusion.me.refs_0_.ids, f32[28]{0:T(128)S(1)} %get-tuple-element.242.keep, f32[2,28,196]{2,1,0:T(8,128)S(1)} %stats.1.t0, ...), custom_call_target="tpu_custom_call" | custom-call | flops 99999997952 | bytes 1 | tf_op jit(solution)/shard_map/token_forward/pallas_call | solution.py:156
  23.6 0.2 collective-permute-start.3
  23.9 1.2 collective-permute-start.4
  25.1 0.8 collective-permute-start.5
  25.8 6.3 %collective-permute-done.8.refs_5_ = bf16[7,56,384]{2,1,0:T(8,128)(2,1)S(1)} collective-permute-done((bf16[7,56,384]{2,1,0:T(8,128)(2,1)S(1)}, bf16[7,56,384]{2,1,0:T(8,128)(2,1)S(1)}, u32[]{:S(2)}, u32[]{:S(2)}) %collective-permute-start.8) | collective-permute-done | bytes 301088 | tf_op jit(solution)/shard_map/ppermute | solution.py:701
  32.1 33.8 %channel_mlp.2 = (f32[3072,768]{1,0:T(8,128)}, f32[3072,768]{1,0:T(8,128)}, f32[1,3072]{1,0:T(1,128)S(1)}, bf16[28,49,768]{2,1,0:T(8,128)(2,1)}, bf16[7,56,384]{...) custom-call(s32[2]{0:T(128)S(1)} %pad_add_fusion.me.refs_0_.ids, ...), custom_call_target="tpu_custom_call" | custom-call | flops 99999997952 | bytes 1 | tf_op jit(solution)/shard_map/channel_mlp/pallas_call | solution.py:338
  66.0 0.1 collective-permute-start.12
  66.1 1.3 collective-permute-start.13
  67.4 0.8 collective-permute-start.14
  68.2 0.0 copy-start.10
  68.2 34.1 %channel_mlp.3 = (bf16[8,2,96,768]{3,2,1,0:T(8,128)(2,1)}, bf16[8,2,96,768]{3,2,1,0:T(8,128)(2,1)}, bf16[8,2,96,768]{3,2,1,0:T(8,128)(2,1)}, bf16[8,2,96,768]{3,...) custom-call(s32[2]{0:T(128)S(1)} %pad_add_fusion.me.refs_0_.ids, ...), custom_call_target="tpu_custom_call", output_to_operand_aliasing={{5}: (16, {})} | custom-call | flops 99999997952 | bytes 1 | tf_op jit(solution)/shard_map/channel_mlp/pallas_call | solution.py:338
  102.3 0.1 collective-permute-start.9
  102.4 1.3 collective-permute-start.10
  103.7 0.8 collective-permute-start.11
  104.6 0.5 collective-permute-start.16
  105.1 8.6 %token_backward.2 = (f32[28,192,196]{2,1,0:T(8,128)S(1)}, f32[2,28,196]{2,1,0:T(8,128)S(1)}, f32[196,384]{1,0:T(8,128)S(1)}, f32[224,384]{1,0:T(8,128)S(1)}, f32...) custom-call(s32[2]{0:T(128)S(1)} %pad_add_fusion.me.refs_0_.ids, ...), custom_call_target="tpu_custom_call" | custom-call | flops 99999997952 | bytes 1 | tf_op jit(solution)/shard_map/token_backward/pallas_call | solution.py:495
  113.8 1.1 sum_first.1
  114.8 1.3 collective-permute-start.20
  116.1 1.2 collective-permute-start.21
  117.4 1.3 collective-permute-start.22
  118.7 8.5 %token_backward.3 = (f32[28,192,196]{2,1,0:T(8,128)S(1)}, bf16[192,384]{1,0:T(8,128)(2,1)S(1)}, bf16[192,384]{1,0:T(8,128)(2,1)S(1)}, bf16[192,384]{1,0:T(8,128)(2,1)S(1)}, bf16[192,384]{1,0:T(8,128)(2,1)S(1)}) custom-call(s32[2]{0:T(128)S(1)} %pad_add_fusion.me.refs_0_.ids, f32[28]{0:T(128)S(1)} %get-tuple-element.242.keep, ...), custom_call_target="tpu_custom_call", output_to_operand_aliasing={{0}: (30, {})} | custom-call | flops 99999997952 | bytes 1 | tf_op jit(solution)/shard_map/token_backward/pallas_call | solution.py:495
  127.2 0.9 collective-permute-start.17
  128.2 0.3 collective-permute-start.18
  128.4 0.8 collective-permute-done.17.refs_1_.s1
  129.2 0.7 collective-permute-start.19
  129.9 8.2 %collective-permute-done.18.refs_2_.s2 = bf16[192,384]{1,0:T(8,128)(2,1)S(1)} collective-permute-done((bf16[192,384]{1,0:T(8,128)(2,1)S(1)}, bf16[192,384]{1,0:T(8,128)(2,1)S(1)}, u32[]{:S(2)}, u32[]{:S(2)}) %collective-permute-start.18) | collective-permute-done | bytes 147488 | tf_op jit(solution)/shard_map/ppermute | solution.py:701
  138.1 3.6 %collective-permute-done.19.refs_3_.s3 = bf16[192,384]{1,0:T(8,128)(2,1)S(1)} collective-permute-done((bf16[192,384]{1,0:T(8,128)(2,1)S(1)}, bf16[192,384]{1,0:T(8,128)(2,1)S(1)}, u32[]{:S(2)}, u32[]{:S(2)}) %collective-permute-start.19) | collective-permute-done | bytes 147488 | tf_op jit(solution)/shard_map/ppermute | solution.py:701
  141.7 0.1 quarter_sum.4.refs_0_
  141.8 0.5 sum_next.3
  142.3 1.3 collective-permute-start.25
  143.6 1.3 collective-permute-start.26
  145.0 0.5 collective-permute-start.27
  145.5 1.0 collective-permute-start.23
  146.4 3.3 %norm_backward.1 = f32[28,192,196]{2,1,0:T(8,128)} custom-call(f32[2,28,196]{2,1,0:T(8,128)S(1)} %stats.1.t0, f32[2,28,196]{2,1,0:T(8,128)S(1)} %collective-permute-done.t1, f32[2,28,196]{2,1,0:T(8,128)S(1)} %collective-permute-done.1.t2, f32[2,28,196]{2,1,0:T(8,128)S(1)} %collective-permute-done.2.t3, bf16[192,384]{1,0:T(8,128)(2,1)S(1)} %get-tuple-element.188.refs_0_.s0, ...), custom_call_target="tpu_custom_call" | custom-call | flops 1 | bytes 1 | tf_op jit(solution)/shard_map/norm_backward/pallas_call | solution.py:531
  149.7 7.5 %collective-permute-done.23.refs_1_ = bf16[128,384]{1,0:T(8,128)(2,1)S(1)} collective-permute-done((bf16[128,384]{1,0:T(8,128)(2,1)S(1)}, bf16[128,384]{1,0:T(8,128)(2,1)S(1)}, u32[]{:S(2)}, u32[]{:S(2)}) %collective-permute-start.23) | collective-permute-done | bytes 98336 | tf_op jit(solution)/shard_map/ppermute | solution.py:614
  157.3 0.3 sum_next.4
  157.6 0.2 collective-permute-start.29
  157.9 0.2 collective-permute-start.30
  158.1 0.2 collective-permute-start.31
  158.3 1.3 collective-permute-start.24
  159.6 5.2 %collective-permute-done.24.refs_1_ = bf16[128,384]{1,0:T(8,128)(2,1)S(1)} collective-permute-done((bf16[128,384]{1,0:T(8,128)(2,1)S(1)}, bf16[128,384]{1,0:T(8,128)(2,1)S(1)}, u32[]{:S(2)}, u32[]{:S(2)}) %collective-permute-start.24) | collective-permute-done | bytes 98336 | tf_op jit(solution)/shard_map/ppermute | solution.py:614
  164.9 0.1 sum_next.5
  165.1 0.1 collective-permute-start.35
  165.1 1.5 collective-permute-start.28
  166.6 17.1 %collective-permute-done.28.refs_1_ = bf16[128,384]{1,0:T(8,128)(2,1)S(1)} collective-permute-done((bf16[128,384]{1,0:T(8,128)(2,1)S(1)}, bf16[128,384]{1,0:T(8,128)(2,1)S(1)}, u32[]{:S(2)}, u32[]{:S(2)}) %collective-permute-start.28) | collective-permute-done | bytes 98336 | tf_op jit(solution)/shard_map/ppermute | solution.py:614
  183.7 1.6 collective-permute-start.34
  185.4 1.2 collective-permute-start.33
  186.5 2.0 %collective-permute-done.34.q3 = bf16[128,384]{1,0:T(8,128)(2,1)S(1)} collective-permute-done((bf16[128,384]{1,0:T(8,128)(2,1)S(1)}, bf16[128,384]{1,0:T(8,128)(2,1)S(1)}, u32[]{:S(2)}, u32[]{:S(2)}) %collective-permute-start.34) | collective-permute-done | bytes 98336 | tf_op jit(solution)/shard_map/ppermute | solution.py:697
  188.5 2.5 %collective-permute-done.33.q2 = bf16[128,384]{1,0:T(8,128)(2,1)S(1)} collective-permute-done((bf16[128,384]{1,0:T(8,128)(2,1)S(1)}, bf16[128,384]{1,0:T(8,128)(2,1)S(1)}, u32[]{:S(2)}, u32[]{:S(2)}) %collective-permute-start.33) | collective-permute-done | bytes 98336 | tf_op jit(solution)/shard_map/ppermute | solution.py:697
  191.0 1.5 unpack.1
  192.5 0.8 sum_last.1
  (75 shorter events, 0.3 us)
Async XLA Ops:
  0.6 5.8 %copy-start.20 = (s32[28,2]{0,1:T(2,128)S(1)}, s32[28,2]{0,1:T(2,128)}, u32[]{:S(2)}) copy-start(s32[28,2]{0,1:T(2,128)} %param.28) | copy-start | bytes 676
  0.7 1.8 copy-start
  2.4 7.3 %copy-start.19 = (f32[384]{0:T(512)S(1)}, f32[384]{0:T(512)}, u32[]{:S(2)}) copy-start(f32[384]{0:T(512)} %param.19) | copy-start | bytes 4612
  2.4 7.4 %copy-start.16 = (f32[768]{0:T(1024)S(1)}, f32[768]{0:T(1024)}, u32[]{:S(2)}) copy-start(f32[768]{0:T(1024)} %param.22) | copy-start | bytes 9220
  2.4 7.4 %copy-start.17 = (f32[768]{0:T(1024)S(1)}, f32[768]{0:T(1024)}, u32[]{:S(2)}) copy-start(f32[768]{0:T(1024)} %param.23) | copy-start | bytes 9220
  2.4 7.4 %copy-start.18 = (f32[768]{0:T(1024)S(1)}, f32[768]{0:T(1024)}, u32[]{:S(2)}) copy-start(f32[768]{0:T(1024)} %param.27) | copy-start | bytes 9220
  2.5 7.6 %copy-start.1 = (bf16[28,196,192]{1,2,0:T(8,128)(2,1)S(1)}, bf16[28,196,192]{1,2,0:T(8,128)(2,1)}, u32[]{:S(2)}) copy-start(bf16[28,196,192]{1,2,0:T(8,128)(2,1)} %param.15) | copy-start | bytes 6322180
  2.5 7.6 %copy-start.11 = (f32[196]{0:T(256)S(1)}, f32[196]{0:T(256)}, u32[]{:S(2)}) copy-start(f32[196]{0:T(256)} %param.21) | copy-start | bytes 2356
  2.5 7.6 %copy-start.12 = (f32[192]{0:T(256)S(1)}, f32[192]{0:T(256)}, u32[]{:S(2)}) copy-start(f32[192]{0:T(256)} %param.16) | copy-start | bytes 2308
  2.5 7.6 %copy-start.13 = (f32[192]{0:T(256)S(1)}, f32[192]{0:T(256)}, u32[]{:S(2)}) copy-start(f32[192]{0:T(256)} %param.17) | copy-start | bytes 2308
  4.1 5.8 %collective-permute-start.2 = (f32[2,28,196]{2,1,0:T(8,128)S(1)}, f32[2,28,196]{2,1,0:T(8,128)S(1)}, u32[]{:S(2)}, u32[]{:S(2)}) collective-permute-start(f32[2,28,196]{2,1,0:T(8,128)S(1)} %stats.1.t0), channel_id=1, source_target_pairs={{0,3},{1,2},{2,1},{3,0},{4,7},{5,6},{6,5},{7,4},{8,11},{9,10},{10,... | collective-permute-start | bytes 131720 | tf_op jit(solution)/shard_map/ppermute | solution.py:697
  6.0 4.1 %collective-permute-start.1 = (f32[2,28,196]{2,1,0:T(8,128)S(1)}, f32[2,28,196]{2,1,0:T(8,128)S(1)}, u32[]{:S(2)}, u32[]{:S(2)}) collective-permute-start(f32[2,28,196]{2,1,0:T(8,128)S(1)} %stats.1.t0), channel_id=1, source_target_pairs={{0,2},{1,3},{2,0},{3,1},{4,6},{5,7},{6,4},{7,5},{8,10},{9,11},{10,... | collective-permute-start | bytes 131720 | tf_op jit(solution)/shard_map/ppermute | solution.py:697
  6.2 3.9 %collective-permute-start = (f32[2,28,196]{2,1,0:T(8,128)S(1)}, f32[2,28,196]{2,1,0:T(8,128)S(1)}, u32[]{:S(2)}, u32[]{:S(2)}) collective-permute-start(f32[2,28,196]{2,1,0:T(8,128)S(1)} %stats.1.t0), channel_id=1, source_target_pairs={{0,1},{1,0},{2,3},{3,2},{4,5},{5,4},{6,7},{7,6},{8,9},{9,8},{10,11... | collective-permute-start | bytes 131720 | tf_op jit(solution)/shard_map/ppermute | solution.py:697
  6.5 1.7 copy-start.2
  8.2 1.9 copy-start.5
  8.2 1.9 copy-start.7
  9.8 13.8 %copy-start.14 = (bf16[2,688,768]{2,1,0:T(8,128)(2,1)}, bf16[2,688,768]{2,1,0:T(8,128)(2,1)S(1)}, u32[]{:S(2)}) copy-start(bf16[2,688,768]{2,1,0:T(8,128)(2,1)S(1)} %get-tuple-element.132.refs_7_) | copy-start | bytes 6340612
  9.8 13.8 %copy-start.9 = (f32[1,384]{1,0:T(1,128)}, f32[1,384]{1,0:T(1,128)S(1)}, u32[]{:S(2)}) copy-start(f32[1,384]{1,0:T(1,128)S(1)} %reshape.58.b_in) | copy-start | bytes 4612
  15.7 9.4 %collective-permute-start.6 = (bf16[7,56,384]{2,1,0:T(8,128)(2,1)S(1)}, bf16[7,56,384]{2,1,0:T(8,128)(2,1)S(1)}, u32[]{:S(2)}, u32[]{:S(2)}) collective-permute-start(bf16[7,56,384]{2,1,0:T(8,128)(2,1)S(1)} %get-tuple-element.134), channel_id=1, source_target_pairs={{0,1},{1,0},{2,3},{3,2},{4,5},{5,4},{6,7},{7,6},{8,9},{9,8},{10,11... | collective-permute-start | bytes 903176 | tf_op jit(solution)/shard_map/ppermute | solution.py:701
  16.3 9.5 %collective-permute-start.7 = (bf16[7,56,384]{2,1,0:T(8,128)(2,1)S(1)}, bf16[7,56,384]{2,1,0:T(8,128)(2,1)S(1)}, u32[]{:S(2)}, u32[]{:S(2)}) collective-permute-start(bf16[7,56,384]{2,1,0:T(8,128)(2,1)S(1)} %get-tuple-element.135), channel_id=1, source_target_pairs={{0,2},{1,3},{2,0},{3,1},{4,6},{5,7},{6,4},{7,5},{8,10},{9,11},{10,... | collective-permute-start | bytes 903176 | tf_op jit(solution)/shard_map/ppermute | solution.py:701
  17.6 14.5 %copy-start.15 = (f32[3072]{0:T(1024)S(1)}, f32[3072]{0:T(1024)}, u32[]{:S(2)}) copy-start(f32[3072]{0:T(1024)} %param.25) | copy-start | bytes 36868
  17.6 14.5 %collective-permute-start.8 = (bf16[7,56,384]{2,1,0:T(8,128)(2,1)S(1)}, bf16[7,56,384]{2,1,0:T(8,128)(2,1)S(1)}, u32[]{:S(2)}, u32[]{:S(2)}) collective-permute-start(bf16[7,56,384]{2,1,0:T(8,128)(2,1)S(1)} %get-tuple-element.136), channel_id=1, source_target_pairs={{0,3},{1,2},{2,1},{3,0},{4,7},{5,6},{6,5},{7,4},{8,11},{9,10},{10,... | collective-permute-start | bytes 903176 | tf_op jit(solution)/shard_map/ppermute | solution.py:701
  23.6 43.8 %collective-permute-start.3 = (bf16[7,56,384]{2,1,0:T(8,128)(2,1)S(1)}, bf16[7,56,384]{2,1,0:T(8,128)(2,1)S(1)}, u32[]{:S(2)}, u32[]{:S(2)}) collective-permute-start(bf16[7,56,384]{2,1,0:T(8,128)(2,1)S(1)} %get-tuple-element.129), channel_id=1, source_target_pairs={{0,1},{1,0},{2,3},{3,2},{4,5},{5,4},{6,7},{7,6},{8,9},{9,8},{10,11... | collective-permute-start | bytes 903176 | tf_op jit(solution)/shard_map/ppermute | solution.py:701
  23.9 44.3 %collective-permute-start.4 = (bf16[7,56,384]{2,1,0:T(8,128)(2,1)S(1)}, bf16[7,56,384]{2,1,0:T(8,128)(2,1)S(1)}, u32[]{:S(2)}, u32[]{:S(2)}) collective-permute-start(bf16[7,56,384]{2,1,0:T(8,128)(2,1)S(1)} %get-tuple-element.130), channel_id=1, source_target_pairs={{0,2},{1,3},{2,0},{3,1},{4,6},{5,7},{6,4},{7,5},{8,10},{9,11},{10,... | collective-permute-start | bytes 903176 | tf_op jit(solution)/shard_map/ppermute | solution.py:701
  25.1 43.1 %collective-permute-start.5 = (bf16[7,56,384]{2,1,0:T(8,128)(2,1)S(1)}, bf16[7,56,384]{2,1,0:T(8,128)(2,1)S(1)}, u32[]{:S(2)}, u32[]{:S(2)}) collective-permute-start(bf16[7,56,384]{2,1,0:T(8,128)(2,1)S(1)} %get-tuple-element.131), channel_id=1, source_target_pairs={{0,3},{1,2},{2,1},{3,0},{4,7},{5,6},{6,5},{7,4},{8,11},{9,10},{10,... | collective-permute-start | bytes 903176 | tf_op jit(solution)/shard_map/ppermute | solution.py:701
  66.0 37.7 %collective-permute-start.12 = (bf16[7,56,384]{2,1,0:T(8,128)(2,1)S(1)}, bf16[7,56,384]{2,1,0:T(8,128)(2,1)S(1)}, u32[]{:S(2)}, u32[]{:S(2)}) collective-permute-start(bf16[7,56,384]{2,1,0:T(8,128)(2,1)S(1)} %get-tuple-element.146), channel_id=1, source_target_pairs={{0,1},{1,0},{2,3},{3,2},{4,5},{5,4},{6,7},{7,6},{8,9},{9,8},{10,11... | collective-permute-start | bytes 903176 | tf_op jit(solution)/shard_map/ppermute | solution.py:701
  66.1 38.5 %collective-permute-start.13 = (bf16[7,56,384]{2,1,0:T(8,128)(2,1)S(1)}, bf16[7,56,384]{2,1,0:T(8,128)(2,1)S(1)}, u32[]{:S(2)}, u32[]{:S(2)}) collective-permute-start(bf16[7,56,384]{2,1,0:T(8,128)(2,1)S(1)} %get-tuple-element.147), channel_id=1, source_target_pairs={{0,2},{1,3},{2,0},{3,1},{4,6},{5,7},{6,4},{7,5},{8,10},{9,11},{10,... | collective-permute-start | bytes 903176 | tf_op jit(solution)/shard_map/ppermute | solution.py:701
  67.4 37.2 %collective-permute-start.14 = (bf16[7,56,384]{2,1,0:T(8,128)(2,1)S(1)}, bf16[7,56,384]{2,1,0:T(8,128)(2,1)S(1)}, u32[]{:S(2)}, u32[]{:S(2)}) collective-permute-start(bf16[7,56,384]{2,1,0:T(8,128)(2,1)S(1)} %get-tuple-element.148), channel_id=1, source_target_pairs={{0,3},{1,2},{2,1},{3,0},{4,7},{5,6},{6,5},{7,4},{8,11},{9,10},{10,... | collective-permute-start | bytes 903176 | tf_op jit(solution)/shard_map/ppermute | solution.py:701
  68.2 36.9 %copy-start.6 = (bf16[196,384]{1,0:T(8,128)(2,1)S(1)}, bf16[196,384]{1,0:T(8,128)(2,1)}, u32[]{:S(2)}) copy-start(bf16[196,384]{1,0:T(8,128)(2,1)} %w_in.7) | copy-start | bytes 451588
  68.2 36.9 %copy-start.8 = (bf16[384,196]{0,1:T(8,128)(2,1)S(1)}, bf16[384,196]{0,1:T(8,128)(2,1)}, u32[]{:S(2)}) copy-start(bf16[384,196]{0,1:T(8,128)(2,1)} %param.20) | copy-start | bytes 451588
  68.2 36.8 %copy-start.10 = (f32[1,384]{1,0:T(1,128)S(1)}, f32[1,384]{1,0:T(1,128)}, u32[]{:S(2)}) copy-start(f32[1,384]{1,0:T(1,128)} %copy-done.9) | copy-start | bytes 4612
  102.3 15.0 %collective-permute-start.9 = (bf16[7,56,384]{2,1,0:T(8,128)(2,1)S(1)}, bf16[7,56,384]{2,1,0:T(8,128)(2,1)S(1)}, u32[]{:S(2)}, u32[]{:S(2)}) collective-permute-start(bf16[7,56,384]{2,1,0:T(8,128)(2,1)S(1)} %get-tuple-element.142), channel_id=1, source_target_pairs={{0,1},{1,0},{2,3},{3,2},{4,5},{5,4},{6,7},{7,6},{8,9},{9,8},{10,11... | collective-permute-start | bytes 903176 | tf_op jit(solution)/shard_map/ppermute | solution.py:701
  102.4 16.3 %collective-permute-start.10 = (bf16[7,56,384]{2,1,0:T(8,128)(2,1)S(1)}, bf16[7,56,384]{2,1,0:T(8,128)(2,1)S(1)}, u32[]{:S(2)}, u32[]{:S(2)}) collective-permute-start(bf16[7,56,384]{2,1,0:T(8,128)(2,1)S(1)} %get-tuple-element.143), channel_id=1, source_target_pairs={{0,2},{1,3},{2,0},{3,1},{4,6},{5,7},{6,4},{7,5},{8,10},{9,11},{10,... | collective-permute-start | bytes 903176 | tf_op jit(solution)/shard_map/ppermute | solution.py:701
  103.7 15.0 %collective-permute-start.11 = (bf16[7,56,384]{2,1,0:T(8,128)(2,1)S(1)}, bf16[7,56,384]{2,1,0:T(8,128)(2,1)S(1)}, u32[]{:S(2)}, u32[]{:S(2)}) collective-permute-start(bf16[7,56,384]{2,1,0:T(8,128)(2,1)S(1)} %get-tuple-element.144), channel_id=1, source_target_pairs={{0,3},{1,2},{2,1},{3,0},{4,7},{5,6},{6,5},{7,4},{8,11},{9,10},{10,... | collective-permute-start | bytes 903176 | tf_op jit(solution)/shard_map/ppermute | solution.py:701
  104.5 9.2 %collective-permute-start.15 = (bf16[8,2,96,768]{3,2,1,0:T(8,128)(2,1)}, bf16[8,2,96,768]{3,2,1,0:T(8,128)(2,1)S(1)}, u32[]{:S(2)}, u32[]{:S(2)}) collective-permute-start(bf16[8,2,96,768]{3,2,1,0:T(8,128)(2,1)} %get-tuple-element.167), channel_id=1, source_target_pairs={{0,1},{1,0},{2,3},{3,2},{4,5},{5,4},{6,7},{7,6},{8,9},{9,8},{10,11... | collective-permute-start | bytes 7077896 | tf_op jit(solution)/shard_map/ppermute | solution.py:614
  104.6 9.2 %collective-permute-start.16 = (bf16[8,2,96,768]{3,2,1,0:T(8,128)(2,1)}, bf16[8,2,96,768]{3,2,1,0:T(8,128)(2,1)S(1)}, u32[]{:S(2)}, u32[]{:S(2)}) collective-permute-start(bf16[8,2,96,768]{3,2,1,0:T(8,128)(2,1)} %get-tuple-element.169), channel_id=1, source_target_pairs={{0,1},{1,0},{2,3},{3,2},{4,5},{5,4},{6,7},{7,6},{8,9},{9,8},{10,11... | collective-permute-start | bytes 7077896 | tf_op jit(solution)/shard_map/ppermute | solution.py:614
  105.1 8.7 %copy-start.3 = (bf16[8,2,96,768]{3,2,1,0:T(8,128)(2,1)S(1)}, bf16[8,2,96,768]{3,2,1,0:T(8,128)(2,1)}, u32[]{:S(2)}) copy-start(bf16[8,2,96,768]{3,2,1,0:T(8,128)(2,1)} %get-tuple-element.166.k4) | copy-start | bytes 7077892
  105.1 8.7 %copy-start.4 = (bf16[8,2,96,768]{3,2,1,0:T(8,128)(2,1)S(1)}, bf16[8,2,96,768]{3,2,1,0:T(8,128)(2,1)}, u32[]{:S(2)}) copy-start(bf16[8,2,96,768]{3,2,1,0:T(8,128)(2,1)} %get-tuple-element.168.k3) | copy-start | bytes 7077892
  114.8 26.9 %collective-permute-start.20 = (bf16[8,96,512]{2,1,0:T(8,128)(2,1)S(1)}, bf16[8,96,512]{2,1,0:T(8,128)(2,1)S(1)}, u32[]{:S(2)}, u32[]{:S(2)}) collective-permute-start(bf16[8,96,512]{2,1,0:T(8,128)(2,1)S(1)} %get-tuple-element.178), channel_id=1, source_target_pairs={{0,4},{1,5},{2,6},{3,7},{4,0},{5,1},{6,2},{7,3},{8,12},{9,13},{10,... | collective-permute-start | bytes 2359304 | tf_op jit(solution)/shard_map/ppermute | solution.py:614
  116.1 25.7 %collective-permute-start.21 = (bf16[8,96,512]{2,1,0:T(8,128)(2,1)S(1)}, bf16[8,96,512]{2,1,0:T(8,128)(2,1)S(1)}, u32[]{:S(2)}, u32[]{:S(2)}) collective-permute-start(bf16[8,96,512]{2,1,0:T(8,128)(2,1)S(1)} %get-tuple-element.179), channel_id=1, source_target_pairs={{0,2},{1,3},{2,0},{3,1},{4,6},{5,7},{6,4},{7,5},{8,10},{9,11},{10,... | collective-permute-start | bytes 2359304 | tf_op jit(solution)/shard_map/ppermute | solution.py:614
  117.4 24.4 %collective-permute-start.22 = (bf16[8,96,512]{2,1,0:T(8,128)(2,1)S(1)}, bf16[8,96,512]{2,1,0:T(8,128)(2,1)S(1)}, u32[]{:S(2)}, u32[]{:S(2)}) collective-permute-start(bf16[8,96,512]{2,1,0:T(8,128)(2,1)S(1)} %get-tuple-element.180), channel_id=1, source_target_pairs={{0,8},{1,9},{2,10},{3,11},{4,12},{5,13},{6,14},{7,15},{8,0},{9,1},... | collective-permute-start | bytes 2359304 | tf_op jit(solution)/shard_map/ppermute | solution.py:614
  127.2 2.0 %collective-permute-start.17 = (bf16[192,384]{1,0:T(8,128)(2,1)S(1)}, bf16[192,384]{1,0:T(8,128)(2,1)S(1)}, u32[]{:S(2)}, u32[]{:S(2)}) collective-permute-start(bf16[192,384]{1,0:T(8,128)(2,1)S(1)} %get-tuple-element.173), channel_id=1, source_target_pairs={{0,1},{1,0},{2,3},{3,2},{4,5},{5,4},{6,7},{7,6},{8,9},{9,8},{10,11... | collective-permute-start | bytes 442376 | tf_op jit(solution)/shard_map/ppermute | solution.py:701
  128.2 9.9 %collective-permute-start.18 = (bf16[192,384]{1,0:T(8,128)(2,1)S(1)}, bf16[192,384]{1,0:T(8,128)(2,1)S(1)}, u32[]{:S(2)}, u32[]{:S(2)}) collective-permute-start(bf16[192,384]{1,0:T(8,128)(2,1)S(1)} %get-tuple-element.174), channel_id=1, source_target_pairs={{0,2},{1,3},{2,0},{3,1},{4,6},{5,7},{6,4},{7,5},{8,10},{9,11},{10,... | collective-permute-start | bytes 442376 | tf_op jit(solution)/shard_map/ppermute | solution.py:701
  129.2 12.5 %collective-permute-start.19 = (bf16[192,384]{1,0:T(8,128)(2,1)S(1)}, bf16[192,384]{1,0:T(8,128)(2,1)S(1)}, u32[]{:S(2)}, u32[]{:S(2)}) collective-permute-start(bf16[192,384]{1,0:T(8,128)(2,1)S(1)} %get-tuple-element.175), channel_id=1, source_target_pairs={{0,3},{1,2},{2,1},{3,0},{4,7},{5,6},{6,5},{7,4},{8,11},{9,10},{10,... | collective-permute-start | bytes 442376 | tf_op jit(solution)/shard_map/ppermute | solution.py:701
  142.3 15.0 %collective-permute-start.25 = (bf16[4,96,512]{2,1,0:T(8,128)(2,1)S(1)}, bf16[4,96,512]{2,1,0:T(8,128)(2,1)S(1)}, u32[]{:S(2)}, u32[]{:S(2)}) collective-permute-start(bf16[4,96,512]{2,1,0:T(8,128)(2,1)S(1)} %get-tuple-element.197), channel_id=1, source_target_pairs={{0,2},{1,3},{2,0},{3,1},{4,6},{5,7},{6,4},{7,5},{8,10},{9,11},{10,... | collective-permute-start | bytes 1179656 | tf_op jit(solution)/shard_map/ppermute | solution.py:614
  143.6 13.7 %collective-permute-start.26 = (bf16[4,96,512]{2,1,0:T(8,128)(2,1)S(1)}, bf16[4,96,512]{2,1,0:T(8,128)(2,1)S(1)}, u32[]{:S(2)}, u32[]{:S(2)}) collective-permute-start(bf16[4,96,512]{2,1,0:T(8,128)(2,1)S(1)} %get-tuple-element.198), channel_id=1, source_target_pairs={{0,8},{1,9},{2,10},{3,11},{4,12},{5,13},{6,14},{7,15},{8,0},{9,1},... | collective-permute-start | bytes 1179656 | tf_op jit(solution)/shard_map/ppermute | solution.py:614
  145.0 12.4 %collective-permute-start.27 = (bf16[4,96,512]{2,1,0:T(8,128)(2,1)S(1)}, bf16[4,96,512]{2,1,0:T(8,128)(2,1)S(1)}, u32[]{:S(2)}, u32[]{:S(2)}) collective-permute-start(bf16[4,96,512]{2,1,0:T(8,128)(2,1)S(1)} %get-tuple-element.199), channel_id=1, source_target_pairs={{0,4},{1,5},{2,6},{3,7},{4,0},{5,1},{6,2},{7,3},{8,12},{9,13},{10,... | collective-permute-start | bytes 1179656 | tf_op jit(solution)/shard_map/ppermute | solution.py:614
  145.5 11.8 %collective-permute-start.23 = (bf16[128,384]{1,0:T(8,128)(2,1)S(1)}, bf16[128,384]{1,0:T(8,128)(2,1)S(1)}, u32[]{:S(2)}, u32[]{:S(2)}) collective-permute-start(bf16[128,384]{1,0:T(8,128)(2,1)S(1)} %quarter_sum.4.refs_0_), channel_id=1, source_target_pairs={{0,4},{1,5},{2,6},{3,7},{4,0},{5,1},{6,2},{7,3},{8,12},{9,13},{10,... | collective-permute-start | bytes 294920 | tf_op jit(solution)/shard_map/ppermute | solution.py:614
  157.6 7.3 %collective-permute-start.29 = (bf16[2,96,512]{2,1,0:T(8,128)(2,1)S(1)}, bf16[2,96,512]{2,1,0:T(8,128)(2,1)S(1)}, u32[]{:S(2)}, u32[]{:S(2)}) collective-permute-start(bf16[2,96,512]{2,1,0:T(8,128)(2,1)S(1)} %get-tuple-element.211), channel_id=1, source_target_pairs={{0,8},{1,9},{2,10},{3,11},{4,12},{5,13},{6,14},{7,15},{8,0},{9,1},... | collective-permute-start | bytes 589832 | tf_op jit(solution)/shard_map/ppermute | solution.py:614
  157.9 7.0 %collective-permute-start.30 = (bf16[2,96,512]{2,1,0:T(8,128)(2,1)S(1)}, bf16[2,96,512]{2,1,0:T(8,128)(2,1)S(1)}, u32[]{:S(2)}, u32[]{:S(2)}) collective-permute-start(bf16[2,96,512]{2,1,0:T(8,128)(2,1)S(1)} %get-tuple-element.212), channel_id=1, source_target_pairs={{0,4},{1,5},{2,6},{3,7},{4,0},{5,1},{6,2},{7,3},{8,12},{9,13},{10,... | collective-permute-start | bytes 589832 | tf_op jit(solution)/shard_map/ppermute | solution.py:614
  158.1 6.8 %collective-permute-start.31 = (bf16[2,96,512]{2,1,0:T(8,128)(2,1)S(1)}, bf16[2,96,512]{2,1,0:T(8,128)(2,1)S(1)}, u32[]{:S(2)}, u32[]{:S(2)}) collective-permute-start(bf16[2,96,512]{2,1,0:T(8,128)(2,1)S(1)} %get-tuple-element.213), channel_id=1, source_target_pairs={{0,2},{1,3},{2,0},{3,1},{4,6},{5,7},{6,4},{7,5},{8,10},{9,11},{10,... | collective-permute-start | bytes 589832 | tf_op jit(solution)/shard_map/ppermute | solution.py:614
  158.3 6.6 %collective-permute-start.24 = (bf16[128,384]{1,0:T(8,128)(2,1)S(1)}, bf16[128,384]{1,0:T(8,128)(2,1)S(1)}, u32[]{:S(2)}, u32[]{:S(2)}) collective-permute-start(bf16[128,384]{1,0:T(8,128)(2,1)S(1)} %quarter_sum.5.refs_0_), channel_id=1, source_target_pairs={{0,8},{1,9},{2,10},{3,11},{4,12},{5,13},{6,14},{7,15},{8,0},{9,1},... | collective-permute-start | bytes 294920 | tf_op jit(solution)/shard_map/ppermute | solution.py:614
  165.1 27.4 %collective-permute-start.35 = (bf16[3,96,512]{2,1,0:T(8,128)(2,1)S(1)}, bf16[3,96,512]{2,1,0:T(8,128)(2,1)S(1)}, u32[]{:S(2)}, u32[]{:S(2)}) collective-permute-start(bf16[3,96,512]{2,1,0:T(8,128)(2,1)S(1)} %get-tuple-element.233), channel_id=1, source_target_pairs={{0,24},{1,25},{2,26},{3,27},{4,28},{5,29},{6,30},{7,31},{8,16},{9,... | collective-permute-start | bytes 884744 | tf_op jit(solution)/shard_map/ppermute | solution.py:614
  165.1 18.6 %collective-permute-start.28 = (bf16[128,384]{1,0:T(8,128)(2,1)S(1)}, bf16[128,384]{1,0:T(8,128)(2,1)S(1)}, u32[]{:S(2)}, u32[]{:S(2)}) collective-permute-start(bf16[128,384]{1,0:T(8,128)(2,1)S(1)} %quarter_sum.6.refs_0_), channel_id=1, source_target_pairs={{0,24},{1,25},{2,26},{3,27},{4,28},{5,29},{6,30},{7,31},{8,16},{9,... | collective-permute-start | bytes 294920 | tf_op jit(solution)/shard_map/ppermute | solution.py:614
  183.7 4.8 %collective-permute-start.34 = (bf16[128,384]{1,0:T(8,128)(2,1)S(1)}, bf16[128,384]{1,0:T(8,128)(2,1)S(1)}, u32[]{:S(2)}, u32[]{:S(2)}) collective-permute-start(bf16[128,384]{1,0:T(8,128)(2,1)S(1)} %quarter_sum.7.q0), channel_id=1, source_target_pairs={{0,3},{1,2},{2,1},{3,0},{4,7},{5,6},{6,5},{7,4},{8,11},{9,10},{10,... | collective-permute-start | bytes 294920 | tf_op jit(solution)/shard_map/ppermute | solution.py:697
  185.4 5.6 %collective-permute-start.33 = (bf16[128,384]{1,0:T(8,128)(2,1)S(1)}, bf16[128,384]{1,0:T(8,128)(2,1)S(1)}, u32[]{:S(2)}, u32[]{:S(2)}) collective-permute-start(bf16[128,384]{1,0:T(8,128)(2,1)S(1)} %quarter_sum.7.q0), channel_id=1, source_target_pairs={{0,2},{1,3},{2,0},{3,1},{4,6},{5,7},{6,4},{7,5},{8,10},{9,11},{10,... | collective-permute-start | bytes 294920 | tf_op jit(solution)/shard_map/ppermute | solution.py:697
  186.5 4.5 %collective-permute-start.32 = (bf16[128,384]{1,0:T(8,128)(2,1)S(1)}, bf16[128,384]{1,0:T(8,128)(2,1)S(1)}, u32[]{:S(2)}, u32[]{:S(2)}) collective-permute-start(bf16[128,384]{1,0:T(8,128)(2,1)S(1)} %quarter_sum.7.q0), channel_id=1, source_target_pairs={{0,1},{1,0},{2,3},{3,2},{4,5},{5,4},{6,7},{7,6},{8,9},{9,8},{10,11... | collective-permute-start | bytes 294920 | tf_op jit(solution)/shard_map/ppermute | solution.py:697
